TPU v7x, 32 devices: a whole 2x2x4 slice. The times are simulated.
32 devices in a mesh: section: 4 (over y, x), dp: 8 (over z, core).
Axes of the slice: x: 2, y: 2, z: 4, core: 2. Of those that a mesh axis runs over, the one named last changes fastest.
Arguments:
- stream_input: bfloat16 [16384, 512], P('dp', 'section'), may hold values from -6 to 6
- accum_input: bfloat16 [16384, 512], P('dp', 'section'), may hold values from -6 to 6
- section_weights: bfloat16 [4, 512, 3072], P('section')
- section_norms: bfloat16 [4, 2, 512], P('section')
- final_norm: bfloat16 [2, 512], P(None, 'section')
- seq_lengths: int32 [16, 16], P('dp'), may hold values from 0 to 1024, as said below
- out_cotangent: bfloat16 [16384, 512], P('dp', 'section'), may hold values from -6 to 6
Outputs:
- final_output: bfloat16 [16384, 512], P('dp', 'section')
- stream_input_grad: float32 [16384, 512], P('dp', 'section')
- accum_input_grad: float32 [16384, 512], P('dp', 'section')
- section_weights_grad: float32 [4, 512, 3072], P('section', None, 'dp')
- section_norms_grad: float32 [4, 2, 512], P('section', None, 'dp')
- final_norm_grad: float32 [2, 512], P(None, 'section')
Inputs may be any that keep to these rules, and one draw needn't show every extreme that they name: `seq_lengths`: A row is either one sequence of 512 to 1024 tokens followed by zeros, or 16 sequences of 1 to 64 tokens each; a row sums to at most 1024, and some row holds one sequence of 1024 tokens.
All inputs are finite; a program needn't handle non-finite values.
Results may differ from a plain program's by a relative error of at most 0.02.
Values may be sent and summed in bfloat16 or wider, within the bound.
No kernel may reach another device: no remote copies, remote signals or barrier semaphores. Data moves between devices by JAX's collectives and lax.ppermute only.
A program may use at most 256 MiB of HBM per device.

v0:
```python
import jax
import jax.numpy as jnp
from jax import lax
from jax.sharding import PartitionSpec as P

D = 512
HEADS = 8
HEAD = 64
PACK = 1024


NEG_FILL = -1e30
block_limit = 512


def passed_along(block, axis, distance):
    devices = range(lax.axis_size(axis))
    route = [(i - distance, i) for i in devices if i - distance in devices]
    return lax.ppermute(block, axis, route)


def norm_rows(summed, row_gain, row_shift):
    average = jnp.mean(summed, axis=-1, keepdims=True)
    centered = summed - average
    spread = jnp.mean(centered * centered, axis=-1, keepdims=True)
    return centered * lax.rsqrt(spread + 1e-05) * row_gain + row_shift


def segments_of(lengths):
    ending = jnp.cumsum(lengths, dtype=jnp.int32)
    places = jnp.arange(PACK, dtype=jnp.int32)
    segment = jnp.sum(
        (places[:, None] >= ending[None, :]).astype(jnp.int32), axis=1, dtype=jnp.int32
    )
    living = (places < ending[-1]).astype(jnp.float32)
    return (segment, living)


def split_heads(projected):
    queries = projected[:, :D].reshape(PACK, HEADS, HEAD)
    key_rows = projected[:, D : 2 * D].reshape(PACK, HEADS, HEAD)
    value_rows = projected[:, 2 * D :].reshape(PACK, HEADS, HEAD)
    return (queries, key_rows, value_rows)


def block_scores(query_block, key_rows, seg_block, segment):
    scores = jnp.einsum(
        "qhd,khd->hqk", query_block, key_rows, preferred_element_type=jnp.float32
    ) * HEAD ** (-0.5)
    same_seq = seg_block[:, None] == segment[None, :]
    return jnp.where(same_seq[None], scores, NEG_FILL)


def attend_forward(stream, weights, segment):
    projected = jnp.dot(stream, weights[:, : 3 * D], preferred_element_type=jnp.float32).astype(
        jnp.bfloat16
    )
    queries, key_rows, value_rows = split_heads(projected)
    block_rows = min(block_limit, PACK)
    block_count = PACK // block_rows

    def attend_one_block(block_items):
        query_block, seg_block = block_items
        scores = block_scores(query_block, key_rows, seg_block, segment)
        row_peak = jnp.max(scores, axis=-1, keepdims=True)
        exponent = jnp.exp(scores - row_peak)
        row_total = jnp.sum(exponent, axis=-1, keepdims=True)
        probability = (exponent / row_total).astype(jnp.bfloat16)
        context = jnp.einsum(
            "hqk,khd->qhd", probability, value_rows, preferred_element_type=jnp.float32
        )
        return (context.astype(jnp.bfloat16), (row_peak + jnp.log(row_total))[..., 0])

    context, log_total = lax.map(
        attend_one_block,
        (
            queries.reshape(block_count, block_rows, HEADS, HEAD),
            segment.reshape(block_count, block_rows),
        ),
    )
    context = context.reshape(PACK, D)
    branch = jnp.dot(context, weights[:, 3 * D : 4 * D], preferred_element_type=jnp.float32)
    return (branch, projected, context, log_total)


def feed_forward(stream, inward, outward_t):
    preact = jnp.dot(stream, inward, preferred_element_type=jnp.float32)
    hidden = jax.nn.gelu(preact).astype(jnp.bfloat16)
    branch = lax.dot_general(
        hidden, outward_t, (((1,), (1,)), ((), ())), preferred_element_type=jnp.float32
    )
    return (branch, preact, hidden)


def norm_back(stream, branch, row_gain, row_shift, grad_next, grad_accum):
    summed = stream.astype(jnp.float32) + branch
    _, pullback = jax.vjp(norm_rows, summed, row_gain, row_shift)
    grad_sum, gain_grad, shift_grad = pullback(grad_next)
    grad_branch = (grad_sum + grad_accum).astype(jnp.bfloat16)
    return (grad_sum, grad_branch, gain_grad, shift_grad)


def skip_step(stream, weights, half_piece, segment):
    return jnp.zeros((PACK, D), jnp.float32)


def attention_step(stream, weights, half_piece, segment):
    return attend_forward(stream, weights, segment)[0]


def feed_step(stream, weights, half_piece, segment):
    inward = jnp.concatenate([half_piece, weights[:, : 2 * D]], axis=1)
    return feed_forward(stream, inward, weights[:, 2 * D :])[0]


def skip_back(stream, weights, half_piece, segment, grad_next, grad_accum, row_gain, row_shift):
    return (
        jnp.zeros((PACK, D), jnp.float32),
        jnp.zeros((D, 6 * D), jnp.float32),
        jnp.zeros((D, 2 * D), jnp.float32),
        jnp.zeros((D,), jnp.float32),
        jnp.zeros((D,), jnp.float32),
    )


def attention_back(
    stream, weights, half_piece, segment, grad_next, grad_accum, row_gain, row_shift
):
    branch, projected, context, log_total = attend_forward(stream, weights, segment)
    grad_direct, grad_branch, gain_grad, shift_grad = norm_back(
        stream, branch, row_gain, row_shift, grad_next, grad_accum
    )
    weight_out = weights[:, 3 * D : 4 * D]
    out_proj_grad = lax.dot_general(
        context, grad_branch, (((0,), (0,)), ((), ())), preferred_element_type=jnp.float32
    )
    context_grad = lax.dot_general(
        grad_branch, weight_out, (((1,), (1,)), ((), ())), preferred_element_type=jnp.float32
    ).astype(jnp.bfloat16)
    queries, key_rows, value_rows = split_heads(projected)
    block_rows = min(block_limit, PACK)
    block_count = PACK // block_rows
    scale = HEAD ** (-0.5)

    def attention_one_block(running, block_items):
        key_grad, value_grad = running
        query_block, seg_block, lse_block, ctx_grad_block = block_items
        scores = block_scores(query_block, key_rows, seg_block, segment)
        probability = jnp.exp(scores - lse_block[..., None])
        prob_grad = jnp.einsum(
            "qhd,khd->hqk", ctx_grad_block, value_rows, preferred_element_type=jnp.float32
        )
        inner_sum = jnp.sum(probability * prob_grad, axis=-1, keepdims=True)
        score_grad = (probability * (prob_grad - inner_sum)).astype(jnp.bfloat16)
        query_grad = (
            jnp.einsum("hqk,khd->qhd", score_grad, key_rows, preferred_element_type=jnp.float32)
            * scale
        )
        key_grad = (
            key_grad
            + jnp.einsum(
                "hqk,qhd->khd", score_grad, query_block, preferred_element_type=jnp.float32
            )
            * scale
        )
        value_grad = value_grad + jnp.einsum(
            "hqk,qhd->khd",
            probability.astype(jnp.bfloat16),
            ctx_grad_block,
            preferred_element_type=jnp.float32,
        )
        return ((key_grad, value_grad), query_grad)

    zero_heads = jnp.zeros((PACK, HEADS, HEAD), jnp.float32)
    (key_grad, value_grad), query_grad = lax.scan(
        attention_one_block,
        (zero_heads, zero_heads),
        (
            queries.reshape(block_count, block_rows, HEADS, HEAD),
            segment.reshape(block_count, block_rows),
            log_total,
            context_grad.reshape(block_count, block_rows, HEADS, HEAD),
        ),
    )
    proj_grad = jnp.concatenate(
        [query_grad.reshape(PACK, D), key_grad.reshape(PACK, D), value_grad.reshape(PACK, D)],
        axis=1,
    ).astype(jnp.bfloat16)
    qkv_grad = lax.dot_general(
        stream, proj_grad, (((0,), (0,)), ((), ())), preferred_element_type=jnp.float32
    )
    stream_grad = lax.dot_general(
        proj_grad, weights[:, : 3 * D], (((1,), (1,)), ((), ())), preferred_element_type=jnp.float32
    )
    block_grad = jnp.concatenate(
        [qkv_grad, out_proj_grad, jnp.zeros((D, 2 * D), jnp.float32)], axis=1
    )
    return (
        stream_grad + grad_direct,
        block_grad,
        jnp.zeros((D, 2 * D), jnp.float32),
        gain_grad,
        shift_grad,
    )


def feed_back(stream, weights, half_piece, segment, grad_next, grad_accum, row_gain, row_shift):
    inward = jnp.concatenate([half_piece, weights[:, : 2 * D]], axis=1)
    outward_t = weights[:, 2 * D :]
    branch, preact, hidden = feed_forward(stream, inward, outward_t)
    grad_direct, grad_branch, gain_grad, shift_grad = norm_back(
        stream, branch, row_gain, row_shift, grad_next, grad_accum
    )
    outward_grad = lax.dot_general(
        grad_branch, hidden, (((0,), (0,)), ((), ())), preferred_element_type=jnp.float32
    )
    hidden_grad = jnp.dot(grad_branch, outward_t, preferred_element_type=jnp.float32)
    _, gelu_pull = jax.vjp(jax.nn.gelu, preact)
    preact_grad = gelu_pull(hidden_grad)[0].astype(jnp.bfloat16)
    inward_grad = lax.dot_general(
        stream, preact_grad, (((0,), (0,)), ((), ())), preferred_element_type=jnp.float32
    )
    stream_grad = lax.dot_general(
        preact_grad, inward, (((1,), (1,)), ((), ())), preferred_element_type=jnp.float32
    )
    block_grad = jnp.concatenate([inward_grad[:, 2 * D :], outward_grad], axis=1)
    return (stream_grad + grad_direct, block_grad, inward_grad[:, : 2 * D], gain_grad, shift_grad)


def on_device(
    stream_input,
    accum_input,
    section_weights,
    section_norms,
    final_norm,
    seq_lengths,
    out_cotangent,
):
    section_id = lax.axis_index("section")
    last_section_id = lax.axis_size("section") - 1
    is_even = section_id % 2 == 0
    is_first = section_id == 0
    is_last = section_id == last_section_id
    branch_kind = jnp.where(is_even, 1, 2)
    weights = section_weights[0]
    row_gain = section_norms[0, 0].astype(jnp.float32)
    row_shift = section_norms[0, 1].astype(jnp.float32)
    micro_count = seq_lengths.shape[0]
    whole_stream, whole_accum, whole_cot, whole_final = (
        lax.all_gather(stream_input, "section", axis=1, tiled=True),
        lax.all_gather(accum_input, "section", axis=1, tiled=True),
        lax.all_gather(out_cotangent, "section", axis=1, tiled=True),
        lax.all_gather(final_norm, "section", axis=1, tiled=True),
    )
    stream_in = whole_stream.reshape(micro_count, PACK, D)
    accum_in = whole_accum.reshape(micro_count, PACK, D).astype(jnp.float32)
    segments, livings = jax.vmap(segments_of)(seq_lengths)
    half_piece = passed_along(weights[:, 4 * D :], "section", 1)
    tick_count = micro_count + last_section_id
    plane_low = jnp.zeros((PACK, D), jnp.bfloat16)
    plane_full = jnp.zeros((PACK, D), jnp.float32)
    stack_low = jnp.zeros((micro_count, PACK, D), jnp.bfloat16)
    stack_full = jnp.zeros((micro_count, PACK, D), jnp.float32)

    def forward_tick(tick_id, loop_state):
        recv_stream, recv_accum, inputs_kept, accum_kept, final_kept = loop_state
        micro_id = tick_id - section_id
        is_valid = (micro_id >= 0) & (micro_id < micro_count)
        slot_id = jnp.clip(micro_id, 0, micro_count - 1)
        stream = jnp.where(is_first, stream_in[slot_id], recv_stream)
        branch = lax.switch(
            jnp.where(is_valid, branch_kind, 0),
            [skip_step, attention_step, feed_step],
            stream,
            weights,
            half_piece,
            segments[slot_id],
        )
        new_stream = norm_rows(stream.astype(jnp.float32) + branch, row_gain, row_shift)
        new_accum = jnp.where(is_first, accum_in[slot_id], recv_accum) + branch
        recv_accum = passed_along(new_accum, "section", 1)
        inputs_kept = inputs_kept.at[slot_id].set(jnp.where(is_valid, stream, inputs_kept[slot_id]))
        accum_kept = accum_kept.at[slot_id].set(jnp.where(is_valid, new_accum, accum_kept[slot_id]))
        final_kept = final_kept.at[slot_id].set(
            jnp.where(is_valid, new_stream, final_kept[slot_id])
        )
        recv_stream = passed_along(new_stream.astype(jnp.bfloat16), "section", 1)
        return (recv_stream, recv_accum, inputs_kept, accum_kept, final_kept)

    _, _, inputs_kept, accum_kept, final_kept = lax.fori_loop(
        0, tick_count, forward_tick, (plane_low, plane_full, stack_low, stack_full, stack_full)
    )
    final_gain = whole_final[0].astype(jnp.float32)
    final_shift = whole_final[1].astype(jnp.float32)
    normed, final_pull = jax.vjp(norm_rows, accum_kept, final_gain, final_shift)
    result = (final_kept + normed).astype(jnp.bfloat16)
    cotangent = whole_cot.reshape(micro_count, PACK, D).astype(jnp.float32) * livings[:, :, None]
    accum_grad, final_gain_grad, final_shift_grad = final_pull(cotangent)

    def backward_tick(tick_id, loop_state):
        (
            recv_grad,
            recv_accum_grad,
            slab_acc,
            half_acc,
            gain_acc,
            shift_acc,
            stream_grads,
            accum_grads,
        ) = loop_state
        micro_id = tick_id - (last_section_id - section_id)
        is_valid = (micro_id >= 0) & (micro_id < micro_count)
        slot_id = jnp.clip(micro_id, 0, micro_count - 1)
        grad_next = jnp.where(is_last, cotangent[slot_id], recv_grad.astype(jnp.float32))
        grad_accum = jnp.where(is_last, accum_grad[slot_id], recv_accum_grad)
        recv_accum_grad = passed_along(grad_accum, "section", -1)
        stream_grad, block_grad, half_grad, gain_grad, shift_grad = lax.switch(
            jnp.where(is_valid, branch_kind, 0),
            [skip_back, attention_back, feed_back],
            inputs_kept[slot_id],
            weights,
            half_piece,
            segments[slot_id],
            grad_next,
            grad_accum,
            row_gain,
            row_shift,
        )
        slab_acc = slab_acc + block_grad
        half_acc = half_acc + half_grad
        gain_acc = gain_acc + gain_grad
        shift_acc = shift_acc + shift_grad
        stream_grads = stream_grads.at[slot_id].set(
            jnp.where(is_valid, stream_grad, stream_grads[slot_id])
        )
        accum_grads = accum_grads.at[slot_id].set(
            jnp.where(is_valid, grad_accum, accum_grads[slot_id])
        )
        recv_grad = passed_along(stream_grad.astype(jnp.bfloat16), "section", -1)
        return (
            recv_grad,
            recv_accum_grad,
            slab_acc,
            half_acc,
            gain_acc,
            shift_acc,
            stream_grads,
            accum_grads,
        )

    start_state = (
        plane_low,
        plane_full,
        jnp.zeros((D, 6 * D), jnp.float32),
        jnp.zeros((D, 2 * D), jnp.float32),
        jnp.zeros((D,), jnp.float32),
        jnp.zeros((D,), jnp.float32),
        stack_full,
        stack_full,
    )
    _, _, slab_acc, half_acc, gain_acc, shift_acc, stream_grads, accum_grads = lax.fori_loop(
        0, tick_count, backward_tick, start_state
    )
    half_back = passed_along(half_acc.astype(jnp.bfloat16), "section", -1).astype(half_acc.dtype)
    slab_term = slab_acc + jnp.where(is_even, jnp.pad(half_back, ((0, 0), (4 * D, 0))), 0.0)
    norm_term = jnp.stack([gain_acc, shift_acc])
    final_full = jnp.stack([final_gain_grad, final_shift_grad])
    token_rows = micro_count * PACK
    final_term = jnp.where(is_last, final_full, 0.0)
    result_term = jnp.where(is_last, result.astype(jnp.float32), 0.0).reshape(token_rows, D)
    stream_term = jnp.where(is_first, stream_grads, 0.0).reshape(token_rows, D)
    accum_term = jnp.where(is_first, accum_grads, 0.0).reshape(token_rows, D)
    result_part, stream_part, accum_part, final_part = (
        lax.psum_scatter(
            result_term.astype(jnp.bfloat16), "section", scatter_dimension=1, tiled=True
        ).astype(jnp.float32),
        lax.psum_scatter(
            stream_term.astype(jnp.bfloat16), "section", scatter_dimension=1, tiled=True
        ).astype(jnp.float32),
        lax.psum_scatter(
            accum_term.astype(jnp.bfloat16), "section", scatter_dimension=1, tiled=True
        ).astype(jnp.float32),
        lax.psum_scatter(
            final_term.astype(jnp.bfloat16), "section", scatter_dimension=1, tiled=True
        ).astype(jnp.float32),
    )
    result_part = result_part.astype(jnp.bfloat16)
    slab_part, norm_part = (
        lax.psum_scatter(slab_term, "dp", scatter_dimension=1, tiled=True),
        lax.psum_scatter(norm_term, "dp", scatter_dimension=1, tiled=True),
    )
    final_grad = lax.psum(final_part, "dp")
    return (result_part, stream_part, accum_part, slab_part[None], norm_part[None], final_grad)


def solution(mesh):
    placed = (
        P("dp", "section"),
        P("dp", "section"),
        P("section", None, None),
        P("section", None, None),
        P(None, "section"),
        P("dp", None),
        P("dp", "section"),
    )
    return jax.shard_map(
        on_device,
        mesh=mesh,
        in_specs=placed,
        out_specs=(
            P("dp", "section"),
            P("dp", "section"),
            P("dp", "section"),
            P("section", None, "dp"),
            P("section", None, "dp"),
            P(None, "section"),
        ),
        check_vma=False,
    )
```

profile of v0, /device:TPU:8, one launch (start us, length us, event | category | flops | bytes accessed | tf_op | source)
XLA Modules:
  0.0 1971.8 jit_solution(37272268925833361)
XLA Ops:
  18.1 31.4 %all_gather.14 = bf16[2,512]{1,0:T(2,128)(2,1)S(1)} all-gather(bf16[2,128]{1,0:T(2,128)(2,1)S(1)} %copy-done.49), channel_id=1, replica_groups=mesh['section'=4,'dp'=8] {'section'}, dimensions={1}, use_global_device_ids=true | all-gather | bytes 2560 | tf_op jit(solution)/shard_map/all_gather | solution.py:253
  59.1 33.0 %all-gather.4.cloned.1.call-done = bf16[2048,512]{1,0:T(8,128)(2,1)} async-done(((bf16[2048,128]{1,0:T(8,128)(2,1)}), bf16[2048,512]{1,0:T(8,128)(2,1)}) %all-gather.4.cloned.1.call-update) | async-done | bytes 2097168 | tf_op jit(solution)/shard_map/all_gather | solution.py:250
  100.2 738.2 %while.105 = (s32[]{:T(128)}, bf16[1024,512]{1,0:T(8,128)(2,1)S(1)}, f32[1024,512]{1,0:T(8,128)}, bf16[2,1024,512]{2,1,0:T(8,128)(2,1)}, f32[2,1024,512]{2,1,0:T...) while((s32[]{:T(128)}, bf16[1024,512]{1,0:T(8,128)(2,1)S(1)}, ...), condition=%wide.region_13.14_spmd, body=%wide.region_2.13_spmd.sunk | while | flops 4333765632 | bytes 248648080 | solution.py:290
  106.5 99.3 %conditional.5 = (f32[1024,512]{1,0:T(8,128)S(1)}) conditional(s32[]{:T(128)} %clamp.19, () %tuple.247, (bf16[512,3072]{1,0:T(8,128)(2,1)}, bf16[1024,512]{1,0:T(8,128)(2,1)S(1)}, s32[2,1024]{1,0:T(2,128)}, s32[]{:T(128)}) %tuple.248, (bf16[512,3072]{1,0:T(8,128)(2,1)}, bf16[512,1024]{1,0:T(8,128)(2,1)}, ...), branch_computations={%region_3.3_spmd, %region_4.8_spmd, %region_9.9_spmd} | conditional | flops 4318035968 | bytes 108067072 | solution.py:271
  121.7 79.7 %while.102 = (s32[]{:T(128)}, bf16[2,512,8,64]{1,3,2,0:T(8,128)(2,1)}, s32[2,512]{1,0:T(2,128)S(1)}, s32[1,1024]{1,0:T(1,128)S(1)}, bf16[2,512,8,64]{1,3,2,0:T(8...) while((s32[]{:T(128)}, bf16[2,512,8,64]{1,3,2,0:T(8,128)(2,1)}, ...), condition=%wide.region_8.7_spmd, body=%wide.region_5.6_spmd.sunk | while | flops 1108083712 | bytes 79734944 | solution.py:74
  121.7 8.2 fusion.195
  130.3 21.7 %fusion.196 = (f32[8,512]{1,0:T(8,128)S(1)}, f32[8,512,1024]{2,1,0:T(8,128)}) fusion(f32[8,512,1024]{2,1,0:T(8,128)} %fusion.195, pred[512,1024]{1,0:T(8,128)(4,1)S(1)} %broadcast_compare_fusion.8), kind=kOutput, calls=%fused_computation.224.clone.1 | output fusion | flops 25166848 | bytes 34095104 | tf_op jit(solution)/shard_map/while/body/eval_jaxpr/cond/branch_1_fun/while/body/eval_jaxpr/sub | solution.py:66
  152.0 9.6 fusion.197
  161.6 8.2 fusion.195
  170.1 21.7 %fusion.196 = (f32[8,512]{1,0:T(8,128)S(1)}, f32[8,512,1024]{2,1,0:T(8,128)}) fusion(f32[8,512,1024]{2,1,0:T(8,128)} %fusion.195, pred[512,1024]{1,0:T(8,128)(4,1)S(1)} %broadcast_compare_fusion.8), kind=kOutput, calls=%fused_computation.224.clone.1 | output fusion | flops 25166848 | bytes 34095104 | tf_op jit(solution)/shard_map/while/body/eval_jaxpr/cond/branch_1_fun/while/body/eval_jaxpr/sub | solution.py:66
  191.8 9.6 fusion.197
  220.8 63.3 %collective-permute-done.2 = bf16[1024,512]{1,0:T(8,128)(2,1)S(1)} collective-permute-done((bf16[1024,512]{1,0:T(8,128)(2,1)}, bf16[1024,512]{1,0:T(8,128)(2,1)S(1)}, u32[]{:S(2)}, u32[]{:S(2)}) %collective-permute-start.2) | collective-permute-done | bytes 1048608 | tf_op jit(solution)/shard_map/while/body/eval_jaxpr/ppermute | solution.py:19
  290.1 99.2 %conditional.5 = (f32[1024,512]{1,0:T(8,128)S(1)}) conditional(s32[]{:T(128)} %clamp.19, () %tuple.247, (bf16[512,3072]{1,0:T(8,128)(2,1)}, bf16[1024,512]{1,0:T(8,128)(2,1)S(1)}, s32[2,1024]{1,0:T(2,128)}, s32[]{:T(128)}) %tuple.248, (bf16[512,3072]{1,0:T(8,128)(2,1)}, bf16[512,1024]{1,0:T(8,128)(2,1)}, ...), branch_computations={%region_3.3_spmd, %region_4.8_spmd, %region_9.9_spmd} | conditional | flops 4318035968 | bytes 108067072 | solution.py:271
  305.3 79.8 %while.102 = (s32[]{:T(128)}, bf16[2,512,8,64]{1,3,2,0:T(8,128)(2,1)}, s32[2,512]{1,0:T(2,128)S(1)}, s32[1,1024]{1,0:T(1,128)S(1)}, bf16[2,512,8,64]{1,3,2,0:T(8...) while((s32[]{:T(128)}, bf16[2,512,8,64]{1,3,2,0:T(8,128)(2,1)}, ...), condition=%wide.region_8.7_spmd, body=%wide.region_5.6_spmd.sunk | while | flops 1108083712 | bytes 79734944 | solution.py:74
  305.3 8.2 fusion.195
  313.8 21.7 %fusion.196 = (f32[8,512]{1,0:T(8,128)S(1)}, f32[8,512,1024]{2,1,0:T(8,128)}) fusion(f32[8,512,1024]{2,1,0:T(8,128)} %fusion.195, pred[512,1024]{1,0:T(8,128)(4,1)S(1)} %broadcast_compare_fusion.8), kind=kOutput, calls=%fused_computation.224.clone.1 | output fusion | flops 25166848 | bytes 34095104 | tf_op jit(solution)/shard_map/while/body/eval_jaxpr/cond/branch_1_fun/while/body/eval_jaxpr/sub | solution.py:66
  335.5 9.6 fusion.197
  345.2 8.2 fusion.195
  353.7 21.7 %fusion.196 = (f32[8,512]{1,0:T(8,128)S(1)}, f32[8,512,1024]{2,1,0:T(8,128)}) fusion(f32[8,512,1024]{2,1,0:T(8,128)} %fusion.195, pred[512,1024]{1,0:T(8,128)(4,1)S(1)} %broadcast_compare_fusion.8), kind=kOutput, calls=%fused_computation.224.clone.1 | output fusion | flops 25166848 | bytes 34095104 | tf_op jit(solution)/shard_map/while/body/eval_jaxpr/cond/branch_1_fun/while/body/eval_jaxpr/sub | solution.py:66
  375.4 9.6 fusion.197
  404.4 62.8 %collective-permute-done.2 = bf16[1024,512]{1,0:T(8,128)(2,1)S(1)} collective-permute-done((bf16[1024,512]{1,0:T(8,128)(2,1)}, bf16[1024,512]{1,0:T(8,128)(2,1)S(1)}, u32[]{:S(2)}, u32[]{:S(2)}) %collective-permute-start.2) | collective-permute-done | bytes 1048608 | tf_op jit(solution)/shard_map/while/body/eval_jaxpr/ppermute | solution.py:19
  482.5 16.0 collective-permute-start.3
  505.9 57.9 %collective-permute-done.2 = bf16[1024,512]{1,0:T(8,128)(2,1)S(1)} collective-permute-done((bf16[1024,512]{1,0:T(8,128)(2,1)}, bf16[1024,512]{1,0:T(8,128)(2,1)S(1)}, u32[]{:S(2)}, u32[]{:S(2)}) %collective-permute-start.2) | collective-permute-done | bytes 1048608 | tf_op jit(solution)/shard_map/while/body/eval_jaxpr/ppermute | solution.py:19
  579.1 9.5 collective-permute-start.3
  590.1 102.9 %collective-permute-start.2 = (bf16[1024,512]{1,0:T(8,128)(2,1)}, bf16[1024,512]{1,0:T(8,128)(2,1)S(1)}, u32[]{:S(2)}, u32[]{:S(2)}) collective-permute-start(bf16[1024,512]{1,0:T(8,128)(2,1)} %fusion.174), channel_id=1, source_target_pairs={{0,8},{8,16},{16,24},{1,9},{9,17},{17,25},{2,10},{10,18},{18,26},{... | collective-permute-start | bytes 3145736 | tf_op jit(solution)/shard_map/while/body/eval_jaxpr/ppermute | solution.py:19
  693.0 20.3 %collective-permute-done.2 = bf16[1024,512]{1,0:T(8,128)(2,1)S(1)} collective-permute-done((bf16[1024,512]{1,0:T(8,128)(2,1)}, bf16[1024,512]{1,0:T(8,128)(2,1)S(1)}, u32[]{:S(2)}, u32[]{:S(2)}) %collective-permute-start.2) | collective-permute-done | bytes 1048608 | tf_op jit(solution)/shard_map/while/body/eval_jaxpr/ppermute | solution.py:19
  728.6 46.2 %collective-permute-start.3 = (f32[1024,512]{1,0:T(8,128)}, f32[1024,512]{1,0:T(8,128)}, u32[]{:S(2)}, u32[]{:S(2)}) collective-permute-start(f32[1024,512]{1,0:T(8,128)} %get-tuple-element.1955), channel_id=1, source_target_pairs={{0,8},{8,16},{16,24},{1,9},{9,17},{17,25},{2,10},{10,18},{18,26},{... | collective-permute-start | bytes 6291464 | tf_op jit(solution)/shard_map/while/body/eval_jaxpr/ppermute | solution.py:19
  780.3 57.9 %collective-permute-done.2 = bf16[1024,512]{1,0:T(8,128)(2,1)S(1)} collective-permute-done((bf16[1024,512]{1,0:T(8,128)(2,1)}, bf16[1024,512]{1,0:T(8,128)(2,1)S(1)}, u32[]{:S(2)}, u32[]{:S(2)}) %collective-permute-start.2) | collective-permute-done | bytes 1048608 | tf_op jit(solution)/shard_map/while/body/eval_jaxpr/ppermute | solution.py:19
  849.5 7.4 broadcast_add_fusion
  859.6 889.9 %while.106 = (s32[]{:T(128)}, bf16[1024,512]{0,1:T(8,128)(2,1)}, f32[1024,512]{0,1:T(8,128)}, f32[512,3072]{1,0:T(8,128)}, f32[512,1024]{0,1:T(8,128)}, /*index=...) while((s32[]{:T(128)}, bf16[1024,512]{0,1:T(8,128)(2,1)}, ...), condition=%wide.region_43.44_spmd.clone, body=%wide.region_19.43_spmd.clone.sunk | while | flops 12996583424 | bytes 632744128 | solution.py:361
  881.8 10.9 conditional.6
  915.5 27.4 %collective-permute-done = bf16[1024,512]{0,1:T(8,128)(2,1)} collective-permute-done((bf16[1024,512]{0,1:T(8,128)(2,1)}, bf16[1024,512]{0,1:T(8,128)(2,1)}, u32[]{:S(2)}, u32[]{:S(2)}) %collective-permute-start) | collective-permute-done | bytes 1048608 | tf_op jit(solution)/shard_map/while/body/eval_jaxpr/ppermute | solution.py:19
  964.8 7.3 conditional.6
  995.6 35.4 %collective-permute-done = bf16[1024,512]{0,1:T(8,128)(2,1)} collective-permute-done((bf16[1024,512]{0,1:T(8,128)(2,1)}, bf16[1024,512]{0,1:T(8,128)(2,1)}, u32[]{:S(2)}, u32[]{:S(2)}) %collective-permute-start) | collective-permute-done | bytes 1048608 | tf_op jit(solution)/shard_map/while/body/eval_jaxpr/ppermute | solution.py:19
  1052.7 7.3 conditional.6
  1083.5 199.2 %collective-permute-done = bf16[1024,512]{0,1:T(8,128)(2,1)} collective-permute-done((bf16[1024,512]{0,1:T(8,128)(2,1)}, bf16[1024,512]{0,1:T(8,128)(2,1)}, u32[]{:S(2)}, u32[]{:S(2)}) %collective-permute-start) | collective-permute-done | bytes 1048608 | tf_op jit(solution)/shard_map/while/body/eval_jaxpr/ppermute | solution.py:19
  1304.4 183.3 %conditional.6 = (bf16[1024,512]{0,1:T(8,128)(2,1)}, f32[512,3072]{1,0:T(8,128)}, f32[512,1024]{0,1:T(8,128)}, f32[512]{0:T(512)}, f32[512]{0:T(512)}) conditional(s32[]{:T(128)} %clamp.20, () %tuple.254, (bf16[512,3072]{1,0:T(8,128)(2,1)}, bf16[1024,512]{0,1:T(8,128)(2,1)S(1)}, s32[2,1024]{1,0:T(2,128)}, s32[]{:T(128)}, ...), branch_computations={%region_20.20_spmd, %region_21.34_spmd, %region_35.41_spmd} | conditional | flops 12988717056 | bytes 496374976 | solution.py:317
  1318.6 31.1 %while.103 = (s32[]{:T(128)}, bf16[2,512,8,64]{1,3,2,0:T(8,128)(2,1)S(1)}, f32[2,8,512]{2,1,0:T(8,128)S(1)}, s32[2,512]{1,0:T(2,128)S(1)}, s32[1,1024]{1,0:T(1,1...) while((s32[]{:T(128)}, ...), condition=%wide.region_25.24_spmd, body=%wide.region_22.23_spmd.sunk | while | flops 1124855808 | bytes 55715956 | solution.py:74
  1343.5 5.9 fusion.180
  1366.7 86.7 %while.104 = (s32[]{:T(128)}, f32[1024,8,64]{0,2,1:T(8,128)}, f32[1024,8,64]{0,2,1:T(8,128)}, bf16[2,512,8,64]{1,3,2,0:T(8,128)(2,1)}, bf16[2,512,8,64]{1,3,2,0:...) while((s32[]{:T(128)}, f32[1024,8,64]{0,2,1:T(8,128)}, ...), condition=%wide.region_32.31_spmd.clone, body=%wide.region_30.30_spmd.clone.sunk | while | flops 2725507072 | bytes 233924848 | solution.py:175
  1371.4 11.0 multiply_reduce_fusion.15
  1382.4 9.4 multiply_convert_fusion.2
  1391.7 6.6 bitcast_add_fusion.4
  1413.8 11.0 multiply_reduce_fusion.15
  1424.8 9.4 multiply_convert_fusion.2
  1434.2 7.2 bitcast_add_fusion.4
  1470.8 6.6 copy.119
  1536.3 183.1 %conditional.6 = (bf16[1024,512]{0,1:T(8,128)(2,1)}, f32[512,3072]{1,0:T(8,128)}, f32[512,1024]{0,1:T(8,128)}, f32[512]{0:T(512)}, f32[512]{0:T(512)}) conditional(s32[]{:T(128)} %clamp.20, () %tuple.254, (bf16[512,3072]{1,0:T(8,128)(2,1)}, bf16[1024,512]{0,1:T(8,128)(2,1)S(1)}, s32[2,1024]{1,0:T(2,128)}, s32[]{:T(128)}, ...), branch_computations={%region_20.20_spmd, %region_21.34_spmd, %region_35.41_spmd} | conditional | flops 12988717056 | bytes 496374976 | solution.py:317
  1550.5 31.1 %while.103 = (s32[]{:T(128)}, bf16[2,512,8,64]{1,3,2,0:T(8,128)(2,1)S(1)}, f32[2,8,512]{2,1,0:T(8,128)S(1)}, s32[2,512]{1,0:T(2,128)S(1)}, s32[1,1024]{1,0:T(1,1...) while((s32[]{:T(128)}, ...), condition=%wide.region_25.24_spmd, body=%wide.region_22.23_spmd.sunk | while | flops 1124855808 | bytes 55715956 | solution.py:74
  1598.5 86.5 %while.104 = (s32[]{:T(128)}, f32[1024,8,64]{0,2,1:T(8,128)}, f32[1024,8,64]{0,2,1:T(8,128)}, bf16[2,512,8,64]{1,3,2,0:T(8,128)(2,1)}, bf16[2,512,8,64]{1,3,2,0:...) while((s32[]{:T(128)}, f32[1024,8,64]{0,2,1:T(8,128)}, ...), condition=%wide.region_32.31_spmd.clone, body=%wide.region_30.30_spmd.clone.sunk | while | flops 2725507072 | bytes 233924848 | solution.py:175
  1602.9 11.0 multiply_reduce_fusion.15
  1613.9 9.4 multiply_convert_fusion.2
  1623.3 6.6 bitcast_add_fusion.4
  1645.4 11.0 multiply_reduce_fusion.15
  1656.4 9.4 multiply_convert_fusion.2
  1665.7 7.2 bitcast_add_fusion.4
  1702.7 6.6 copy.119
  1769.9 19.6 collective-permute-done.5
  1789.5 6.5 select_add_fusion.4
  1796.9 11.0 psum.7
  1809.3 9.1 reduce-scatter.19.cloned.1.call-done
  1820.4 36.4 %reduce-scatter.21.cloned.1.call-done = bf16[128,2048]{1,0:T(8,128)(2,1)} async-done(((bf16[512,2048]{1,0:T(8,128)(2,1)}), bf16[128,2048]{1,0:T(8,128)(2,1)}) %reduce-scatter.21.cloned.1.call-update) | async-done | bytes 524304
  1859.2 35.8 %reduce-scatter.23.cloned.1.call-done = bf16[128,2048]{1,0:T(8,128)(2,1)} async-done(((bf16[512,2048]{1,0:T(8,128)(2,1)}), bf16[128,2048]{1,0:T(8,128)(2,1)}) %reduce-scatter.23.cloned.1.call-update) | async-done | bytes 524304
  1897.3 67.6 %reduce-scatter.17.cloned.1.call-done = f32[512,384]{1,0:T(8,128)} async-done(((f32[512,3072]{1,0:T(8,128)}), f32[512,384]{1,0:T(8,128)}) %reduce-scatter.17.cloned.1.call-update) | async-done | bytes 786448 | tf_op jit(solution)/shard_map/reduce_scatter | solution.py:389
  (731 shorter events, 682.5 us)
Async XLA Ops:
  7.2 47.7 %all-gather.6.cloned.1.call-start = ((), (), s32[]{:S(2)}) async-start(), calls=%async_computation.7 | async-start | bytes 2621440 | tf_op jit(solution)/shard_map/all_gather | solution.py:251
  7.9 84.2 %all-gather.4.cloned.1.call-start = ((), (), s32[]{:S(2)}) async-start(), calls=%async_computation.6 | async-start | bytes 2621440 | tf_op jit(solution)/shard_map/all_gather | solution.py:250
  8.7 832.3 %all-gather.8.cloned.1.call-start = ((), (), s32[]{:S(2)}) async-start(), calls=%async_computation.8 | async-start | bytes 2621440 | tf_op jit(solution)/shard_map/all_gather | solution.py:252
  10.0 49.1 %collective-permute-start.4 = (bf16[512,1024]{1,0:T(8,128)(2,1)S(1)}, bf16[512,1024]{1,0:T(8,128)(2,1)S(1)}, u32[]{:S(2)}, u32[]{:S(2)}) collective-permute-start(bf16[512,1024]{1,0:T(8,128)(2,1)S(1)} %slice.273), channel_id=1, source_target_pairs={{0,8},{8,16},{16,24},{1,9},{9,17},{17,25},{2,10},{10,18},{18,26},{... | collective-permute-start | bytes 3145736 | tf_op jit(solution)/shard_map/ppermute | solution.py:19
  13.5 1782.6 %reduce-scatter.27.cloned.1.call-start = ((), (), s32[]{:S(2)}) async-start(), calls=%async_computation.14 | async-start | bytes 163840
  13.8 36.5 %copy-start.47 = (bf16[1,2,512]{2,1,0:T(2,128)(2,1)S(1)}, bf16[1,2,512]{2,1,0:T(2,128)(2,1)}, u32[]{:S(2)}) copy-start(bf16[1,2,512]{2,1,0:T(2,128)(2,1)} %param.36) | copy-start | bytes 6148
  59.1 38.6 %copy-start.50 = (bf16[512,1024]{1,0:T(8,128)(2,1)}, bf16[512,1024]{1,0:T(8,128)(2,1)S(1)}, u32[]{:S(2)}) copy-start(bf16[512,1024]{1,0:T(8,128)(2,1)S(1)} %collective-permute-done.4) | copy-start | bytes 3145732
  121.7 8.2 copy-start.4
  152.0 9.6 copy-start.5
  161.6 8.2 copy-start.4
  191.8 9.6 copy-start.5
  214.9 69.2 %collective-permute-start.3 = (f32[1024,512]{1,0:T(8,128)}, f32[1024,512]{1,0:T(8,128)}, u32[]{:S(2)}, u32[]{:S(2)}) collective-permute-start(f32[1024,512]{1,0:T(8,128)} %get-tuple-element.1955), channel_id=1, source_target_pairs={{0,8},{8,16},{16,24},{1,9},{9,17},{17,25},{2,10},{10,18},{18,26},{... | collective-permute-start | bytes 6291464 | tf_op jit(solution)/shard_map/while/body/eval_jaxpr/ppermute | solution.py:19
  219.5 64.7 %collective-permute-start.2 = (bf16[1024,512]{1,0:T(8,128)(2,1)}, bf16[1024,512]{1,0:T(8,128)(2,1)S(1)}, u32[]{:S(2)}, u32[]{:S(2)}) collective-permute-start(bf16[1024,512]{1,0:T(8,128)(2,1)} %fusion.174), channel_id=1, source_target_pairs={{0,8},{8,16},{16,24},{1,9},{9,17},{17,25},{2,10},{10,18},{18,26},{... | collective-permute-start | bytes 3145736 | tf_op jit(solution)/shard_map/while/body/eval_jaxpr/ppermute | solution.py:19
  305.3 8.2 copy-start.4
  335.5 9.6 copy-start.5
  345.2 8.2 copy-start.4
  375.4 9.6 copy-start.5
  398.5 68.7 %collective-permute-start.3 = (f32[1024,512]{1,0:T(8,128)}, f32[1024,512]{1,0:T(8,128)}, u32[]{:S(2)}, u32[]{:S(2)}) collective-permute-start(f32[1024,512]{1,0:T(8,128)} %get-tuple-element.1955), channel_id=1, source_target_pairs={{0,8},{8,16},{16,24},{1,9},{9,17},{17,25},{2,10},{10,18},{18,26},{... | collective-permute-start | bytes 6291464 | tf_op jit(solution)/shard_map/while/body/eval_jaxpr/ppermute | solution.py:19
  403.0 64.1 %collective-permute-start.2 = (bf16[1024,512]{1,0:T(8,128)(2,1)}, bf16[1024,512]{1,0:T(8,128)(2,1)S(1)}, u32[]{:S(2)}, u32[]{:S(2)}) collective-permute-start(bf16[1024,512]{1,0:T(8,128)(2,1)} %fusion.174), channel_id=1, source_target_pairs={{0,8},{8,16},{16,24},{1,9},{9,17},{17,25},{2,10},{10,18},{18,26},{... | collective-permute-start | bytes 3145736 | tf_op jit(solution)/shard_map/while/body/eval_jaxpr/ppermute | solution.py:19
  482.5 17.5 copy-start.7
  482.5 17.5 copy-start.22
  482.5 81.2 %collective-permute-start.3 = (f32[1024,512]{1,0:T(8,128)}, f32[1024,512]{1,0:T(8,128)}, u32[]{:S(2)}, u32[]{:S(2)}) collective-permute-start(f32[1024,512]{1,0:T(8,128)} %get-tuple-element.1955), channel_id=1, source_target_pairs={{0,8},{8,16},{16,24},{1,9},{9,17},{17,25},{2,10},{10,18},{18,26},{... | collective-permute-start | bytes 6291464 | tf_op jit(solution)/shard_map/while/body/eval_jaxpr/ppermute | solution.py:19
  500.0 63.7 %collective-permute-start.2 = (bf16[1024,512]{1,0:T(8,128)(2,1)}, bf16[1024,512]{1,0:T(8,128)(2,1)S(1)}, u32[]{:S(2)}, u32[]{:S(2)}) collective-permute-start(bf16[1024,512]{1,0:T(8,128)(2,1)} %fusion.174), channel_id=1, source_target_pairs={{0,8},{8,16},{16,24},{1,9},{9,17},{17,25},{2,10},{10,18},{18,26},{... | collective-permute-start | bytes 3145736 | tf_op jit(solution)/shard_map/while/body/eval_jaxpr/ppermute | solution.py:19
  579.1 11.0 copy-start.7
  579.1 11.0 copy-start.22
  579.1 134.2 %collective-permute-start.3 = (f32[1024,512]{1,0:T(8,128)}, f32[1024,512]{1,0:T(8,128)}, u32[]{:S(2)}, u32[]{:S(2)}) collective-permute-start(f32[1024,512]{1,0:T(8,128)} %get-tuple-element.1955), channel_id=1, source_target_pairs={{0,8},{8,16},{16,24},{1,9},{9,17},{17,25},{2,10},{10,18},{18,26},{... | collective-permute-start | bytes 6291464 | tf_op jit(solution)/shard_map/while/body/eval_jaxpr/ppermute | solution.py:19
  590.1 123.2 %collective-permute-start.2 = (bf16[1024,512]{1,0:T(8,128)(2,1)}, bf16[1024,512]{1,0:T(8,128)(2,1)S(1)}, u32[]{:S(2)}, u32[]{:S(2)}) collective-permute-start(bf16[1024,512]{1,0:T(8,128)(2,1)} %fusion.174), channel_id=1, source_target_pairs={{0,8},{8,16},{16,24},{1,9},{9,17},{17,25},{2,10},{10,18},{18,26},{... | collective-permute-start | bytes 3145736 | tf_op jit(solution)/shard_map/while/body/eval_jaxpr/ppermute | solution.py:19
  728.6 47.7 %copy-start.7 = (f32[2,1024,512]{2,1,0:T(8,128)}, f32[2,1024,512]{2,1,0:T(8,128)S(1)}, u32[]{:S(2)}) copy-start(f32[2,1024,512]{2,1,0:T(8,128)S(1)} %get-tuple-element.2172) | copy-start | bytes 12582916 | tf_op jit(solution)/shard_map/while
  728.6 47.7 %copy-start.22 = (f32[2,1024,512]{2,1,0:T(8,128)}, f32[2,1024,512]{2,1,0:T(8,128)S(1)}, u32[]{:S(2)}) copy-start(f32[2,1024,512]{2,1,0:T(8,128)S(1)} %get-tuple-element.2173) | copy-start | bytes 12582916 | tf_op jit(solution)/shard_map/while
  728.6 109.5 %collective-permute-start.3 = (f32[1024,512]{1,0:T(8,128)}, f32[1024,512]{1,0:T(8,128)}, u32[]{:S(2)}, u32[]{:S(2)}) collective-permute-start(f32[1024,512]{1,0:T(8,128)} %get-tuple-element.1955), channel_id=1, source_target_pairs={{0,8},{8,16},{16,24},{1,9},{9,17},{17,25},{2,10},{10,18},{18,26},{... | collective-permute-start | bytes 6291464 | tf_op jit(solution)/shard_map/while/body/eval_jaxpr/ppermute | solution.py:19
  776.3 61.9 %collective-permute-start.2 = (bf16[1024,512]{1,0:T(8,128)(2,1)}, bf16[1024,512]{1,0:T(8,128)(2,1)S(1)}, u32[]{:S(2)}, u32[]{:S(2)}) collective-permute-start(bf16[1024,512]{1,0:T(8,128)(2,1)} %fusion.174), channel_id=1, source_target_pairs={{0,8},{8,16},{16,24},{1,9},{9,17},{17,25},{2,10},{10,18},{18,26},{... | collective-permute-start | bytes 3145736 | tf_op jit(solution)/shard_map/while/body/eval_jaxpr/ppermute | solution.py:19
  849.5 958.4 %reduce-scatter.25.cloned.1.call-start = ((), (), s32[]{:S(2)}) async-start(), calls=%async_computation.13 | async-start | bytes 294912
  872.8 70.1 %collective-permute-start.1 = (f32[1024,512]{0,1:T(8,128)}, f32[1024,512]{0,1:T(8,128)}, u32[]{:S(2)}, u32[]{:S(2)}) collective-permute-start(f32[1024,512]{0,1:T(8,128)} %get-tuple-element.1978), channel_id=1, source_target_pairs={{8,0},{16,8},{24,16},{9,1},{17,9},{25,17},{10,2},{18,10},{26,18},{... | collective-permute-start | bytes 6291464 | tf_op jit(solution)/shard_map/while/body/eval_jaxpr/ppermute | solution.py:19
  892.7 50.2 %collective-permute-start = (bf16[1024,512]{0,1:T(8,128)(2,1)}, bf16[1024,512]{0,1:T(8,128)(2,1)}, u32[]{:S(2)}, u32[]{:S(2)}) collective-permute-start(bf16[1024,512]{0,1:T(8,128)(2,1)} %get-tuple-element.1979), channel_id=1, source_target_pairs={{8,0},{16,8},{24,16},{9,1},{17,9},{25,17},{10,2},{18,10},{26,18},{... | collective-permute-start | bytes 3145736 | tf_op jit(solution)/shard_map/while/body/eval_jaxpr/ppermute | solution.py:19
  898.2 12.4 slice-start.2
  915.5 27.4 %copy-start.9 = (f32[512,3072]{1,0:T(8,128)}, f32[512,3072]{1,0:T(8,128)S(1)}, u32[]{:S(2)}) copy-start(f32[512,3072]{1,0:T(8,128)S(1)} %select_add_fusion.8) | copy-start | bytes 18874372 | tf_op jit(solution)/shard_map/while
  955.9 75.1 %collective-permute-start.1 = (f32[1024,512]{0,1:T(8,128)}, f32[1024,512]{0,1:T(8,128)}, u32[]{:S(2)}, u32[]{:S(2)}) collective-permute-start(f32[1024,512]{0,1:T(8,128)} %get-tuple-element.1978), channel_id=1, source_target_pairs={{8,0},{16,8},{24,16},{9,1},{17,9},{25,17},{10,2},{18,10},{26,18},{... | collective-permute-start | bytes 6291464 | tf_op jit(solution)/shard_map/while/body/eval_jaxpr/ppermute | solution.py:19
  972.2 58.8 %collective-permute-start = (bf16[1024,512]{0,1:T(8,128)(2,1)}, bf16[1024,512]{0,1:T(8,128)(2,1)}, u32[]{:S(2)}, u32[]{:S(2)}) collective-permute-start(bf16[1024,512]{0,1:T(8,128)(2,1)} %get-tuple-element.1979), channel_id=1, source_target_pairs={{8,0},{16,8},{24,16},{9,1},{17,9},{25,17},{10,2},{18,10},{26,18},{... | collective-permute-start | bytes 3145736 | tf_op jit(solution)/shard_map/while/body/eval_jaxpr/ppermute | solution.py:19
  977.6 13.1 slice-start.2
  982.9 7.7 slice-start.3
  995.6 35.4 %copy-start.9 = (f32[512,3072]{1,0:T(8,128)}, f32[512,3072]{1,0:T(8,128)S(1)}, u32[]{:S(2)}) copy-start(f32[512,3072]{1,0:T(8,128)S(1)} %select_add_fusion.8) | copy-start | bytes 18874372 | tf_op jit(solution)/shard_map/while
  1043.8 238.9 %collective-permute-start.1 = (f32[1024,512]{0,1:T(8,128)}, f32[1024,512]{0,1:T(8,128)}, u32[]{:S(2)}, u32[]{:S(2)}) collective-permute-start(f32[1024,512]{0,1:T(8,128)} %get-tuple-element.1978), channel_id=1, source_target_pairs={{8,0},{16,8},{24,16},{9,1},{17,9},{25,17},{10,2},{18,10},{26,18},{... | collective-permute-start | bytes 6291464 | tf_op jit(solution)/shard_map/while/body/eval_jaxpr/ppermute | solution.py:19
  1060.1 222.6 %collective-permute-start = (bf16[1024,512]{0,1:T(8,128)(2,1)}, bf16[1024,512]{0,1:T(8,128)(2,1)}, u32[]{:S(2)}, u32[]{:S(2)}) collective-permute-start(bf16[1024,512]{0,1:T(8,128)(2,1)} %get-tuple-element.1979), channel_id=1, source_target_pairs={{8,0},{16,8},{24,16},{9,1},{17,9},{25,17},{10,2},{18,10},{26,18},{... | collective-permute-start | bytes 3145736 | tf_op jit(solution)/shard_map/while/body/eval_jaxpr/ppermute | solution.py:19
  1065.5 13.1 slice-start.2
  1083.5 199.2 %copy-start.9 = (f32[512,3072]{1,0:T(8,128)}, f32[512,3072]{1,0:T(8,128)S(1)}, u32[]{:S(2)}) copy-start(f32[512,3072]{1,0:T(8,128)S(1)} %select_add_fusion.8) | copy-start | bytes 18874372 | tf_op jit(solution)/shard_map/while
  1295.5 216.0 %collective-permute-start.1 = (f32[1024,512]{0,1:T(8,128)}, f32[1024,512]{0,1:T(8,128)}, u32[]{:S(2)}, u32[]{:S(2)}) collective-permute-start(f32[1024,512]{0,1:T(8,128)} %get-tuple-element.1978), channel_id=1, source_target_pairs={{8,0},{16,8},{24,16},{9,1},{17,9},{25,17},{10,2},{18,10},{26,18},{... | collective-permute-start | bytes 6291464 | tf_op jit(solution)/shard_map/while/body/eval_jaxpr/ppermute | solution.py:19
  1391.7 9.1 copy-start
  1391.7 13.2 slice-start
  1434.2 9.7 copy-start
  1434.2 14.5 slice-start
  1487.7 23.8 %collective-permute-start = (bf16[1024,512]{0,1:T(8,128)(2,1)}, bf16[1024,512]{0,1:T(8,128)(2,1)}, u32[]{:S(2)}, u32[]{:S(2)}) collective-permute-start(bf16[1024,512]{0,1:T(8,128)(2,1)} %get-tuple-element.1979), channel_id=1, source_target_pairs={{8,0},{16,8},{24,16},{9,1},{17,9},{25,17},{10,2},{18,10},{26,18},{... | collective-permute-start | bytes 3145736 | tf_op jit(solution)/shard_map/while/body/eval_jaxpr/ppermute | solution.py:19
  1493.1 13.4 slice-start.2
  1527.4 215.7 %collective-permute-start.1 = (f32[1024,512]{0,1:T(8,128)}, f32[1024,512]{0,1:T(8,128)}, u32[]{:S(2)}, u32[]{:S(2)}) collective-permute-start(f32[1024,512]{0,1:T(8,128)} %get-tuple-element.1978), channel_id=1, source_target_pairs={{8,0},{16,8},{24,16},{9,1},{17,9},{25,17},{10,2},{18,10},{26,18},{... | collective-permute-start | bytes 6291464 | tf_op jit(solution)/shard_map/while/body/eval_jaxpr/ppermute | solution.py:19
  1623.3 9.1 copy-start
  1623.3 13.2 slice-start
  1665.7 9.7 copy-start
  1665.7 14.5 slice-start
  1719.4 23.7 %collective-permute-start = (bf16[1024,512]{0,1:T(8,128)(2,1)}, bf16[1024,512]{0,1:T(8,128)(2,1)}, u32[]{:S(2)}, u32[]{:S(2)}) collective-permute-start(bf16[1024,512]{0,1:T(8,128)(2,1)} %get-tuple-element.1979), channel_id=1, source_target_pairs={{8,0},{16,8},{24,16},{9,1},{17,9},{25,17},{10,2},{18,10},{26,18},{... | collective-permute-start | bytes 3145736 | tf_op jit(solution)/shard_map/while/body/eval_jaxpr/ppermute | solution.py:19
  1724.9 13.3 slice-start.2
  1751.1 67.3 %reduce-scatter.19.cloned.1.call-start = ((), (), s32[]{:S(2)}) async-start(), calls=%async_computation.10 | async-start | bytes 2621440
  1755.3 101.5 %reduce-scatter.21.cloned.1.call-start = ((), (), s32[]{:S(2)}) async-start(), calls=%async_computation.11 | async-start | bytes 2621440
  1763.8 131.2 %reduce-scatter.23.cloned.1.call-start = ((), (), s32[]{:S(2)}) async-start(), calls=%async_computation.12 | async-start | bytes 2621440
  1767.9 197.0 %reduce-scatter.17.cloned.1.call-start = ((), (), s32[]{:S(2)}) async-start(), calls=%async_computation.9 | async-start | bytes 7077888 | tf_op jit(solution)/shard_map/reduce_scatter | solution.py:389
  1768.6 20.9 %collective-permute-start.5 = (bf16[512,1024]{1,0:T(8,128)(2,1)S(1)}, bf16[512,1024]{1,0:T(8,128)(2,1)S(1)}, u32[]{:S(2)}, u32[]{:S(2)}) collective-permute-start(bf16[512,1024]{1,0:T(8,128)(2,1)S(1)} %copy.129), channel_id=1, source_target_pairs={{8,0},{16,8},{24,16},{9,1},{17,9},{25,17},{10,2},{18,10},{26,18},{... | collective-permute-start | bytes 3145736 | tf_op jit(solution)/shard_map/ppermute | solution.py:19
  (116 other events, 414.8 us)
Sparse Core Ops, SparseCore 0:
  9.8 45.0 all-gather.5
  56.7 35.3 all-gather.3
  94.0 41.3 all-gather.7
  849.6 35.2 reduce-scatter.26
  1751.2 27.2 reduce-scatter.24
  1781.3 36.9 reduce-scatter.18
  1821.6 35.1 reduce-scatter.20
  1859.8 35.1 reduce-scatter.22
  1898.0 66.9 reduce-scatter.16
where the time goes:
time: 1980 us; the launch traced here: 1970 us
  waiting for transfers between devices  731 us (37%)
  other arithmetic  358 us (18%)
  local copies, waits for them, and re-layouts  308 us (16%)
  matrix products  274 us (14%)
  starting transfers between devices  211 us (11%)
  blocking collectives  42.4 us (2%)
  loops' own time  33.1 us (2%)
    ppermute x22, waiting for transfers between devices, passed_along(): return lax.ppermute(block, axis, route)  544 us
    ppermute x22, starting transfers between devices, passed_along(): return lax.ppermute(block, axis, route)  211 us
    dot_general x12, matrix products, block_scores(): jnp.einsum('qhd,khd->hqk', query_block, key_rows, preferred_element_type=...  96.2 us
    sub x4, other arithmetic, attend_one_block(): exponent = jnp.exp(scores - row_peak)  86.8 us
    unnamed x14, waiting for transfers between devices  82.8 us
    reduce_scatter x1, waiting for transfers between devices, on_device(): lax.psum_scatter(slab_term, 'dp', scatter_dimension=1, tiled=True)  67.6 us
    dot_general x8, matrix products, attend_one_block(): jnp.einsum('hqk,khd->qhd', probability, value_rows, preferred_element_typ...  62 us
    another operation x32, other arithmetic  56.3 us
  transfers between devices with their start and end apart: 31, of which 15 were waited for; matrix products, arithmetic and copies ran while one was open for 45% of the time, Pallas kernels for 0%

commit v1 on v0

v1 whole, which is shorter than its diff:
```python
import functools

import jax
import jax.numpy as jnp
from jax import lax
from jax.experimental import pallas as pl
from jax.experimental.pallas import tpu as pltpu
from jax.sharding import PartitionSpec as P

D = 512
HEADS = 8
HEAD = 64
PACK = 1024
HALF = PACK // 2
PAIRS = HEADS // 2
LANES = 2 * HEAD
SECTIONS = 4
FAR = 1e30
SCALE = HEAD ** (-0.5)
BF = jnp.bfloat16
F32 = jnp.float32
NT = (((1,), (1,)), ((), ()))
TN = (((0,), (0,)), ((), ()))


def mm(left, right):
    return jnp.dot(left, right, preferred_element_type=F32)


def mm_nt(left, right):
    return lax.dot_general(left, right, NT, preferred_element_type=F32)


def mm_tn(left, right):
    return lax.dot_general(left, right, TN, preferred_element_type=F32)


def params():
    return pltpu.CompilerParams(
        dimension_semantics=("arbitrary",), vmem_limit_bytes=48 * 1024 * 1024
    )


def shaped(rows, cols, dtype):
    return jax.ShapeDtypeStruct((rows, cols), dtype)


def whole(rows, cols):
    return pl.BlockSpec((rows, cols), lambda i: (0, 0))


def cost(flops, moved, transcendentals=0):
    return pl.CostEstimate(
        flops=int(flops), bytes_accessed=int(moved), transcendentals=int(transcendentals)
    )


def norm_parts(summed):
    average = jnp.mean(summed, axis=-1, keepdims=True)
    centered = summed - average
    spread = jnp.mean(centered * centered, axis=-1, keepdims=True)
    inverse = lax.rsqrt(spread + 1e-05)
    return centered * inverse, inverse


def norm_back(summed, gain, upstream):
    normal, inverse = norm_parts(summed)
    scaled = upstream * gain
    mean_one = jnp.mean(scaled, axis=-1, keepdims=True)
    mean_two = jnp.mean(scaled * normal, axis=-1, keepdims=True)
    grad = (scaled - mean_one - normal * mean_two) * inverse
    gain_grad = jnp.sum(upstream * normal, axis=0, keepdims=True)
    shift_grad = jnp.sum(upstream, axis=0, keepdims=True)
    return grad, gain_grad, shift_grad


def head_mask(which):
    lane = lax.broadcasted_iota(jnp.int32, (1, LANES), 1)
    return (lane // HEAD) == which


def three_way(column):
    high = column.astype(BF)
    rest = column - high.astype(F32)
    middle = rest.astype(BF)
    low = (rest - middle.astype(F32)).astype(BF)
    return high, middle, low


def project_kernel(x_ref, w_ref, out_ref):
    out_ref[...] = mm(x_ref[...], w_ref[0]).astype(BF)


def project(stream, weights, layer):
    return pl.pallas_call(
        project_kernel,
        grid=(3,),
        in_specs=[
            whole(HALF, D),
            pl.BlockSpec((1, D, D), lambda i: (layer, 0, i)),
        ],
        out_specs=pl.BlockSpec((HALF, D), lambda i: (0, i)),
        out_shape=shaped(HALF, 3 * D, BF),
        compiler_params=params(),
        cost_estimate=cost(2 * HALF * D * 3 * D, 4e6),
        name="project",
    )(stream, weights)


def attend_kernel(
    q_ref, ko_ref, vo_ref, kx_ref, vx_ref, qs_ref, kso_ref, ksx_ref, w_ref, x_ref, fsum_ref,
    norm_ref, ctx_ref, lse_ref, next_ref, sum_ref, fnew_ref, ctx_acc, lse_acc,
):
    pair = pl.program_id(0)
    q = q_ref[...] * jnp.asarray(SCALE, BF)
    keys_own = jnp.concatenate([ko_ref[...], kso_ref[...]], axis=1)
    keys_other = jnp.concatenate([kx_ref[...], ksx_ref[...]], axis=1)
    values_own, values_other = vo_ref[...], vx_ref[...]
    ones = jnp.ones((HALF, LANES), BF)
    none = jnp.zeros((), BF)
    lane = lax.broadcasted_iota(jnp.int32, (1, LANES), 1)
    context = jnp.zeros((HALF, LANES), F32)
    logs = jnp.where(pair == 0, jnp.zeros((HALF, LANES), F32), lse_acc[...])
    for which in range(2):
        mask = head_mask(which)
        query = jnp.concatenate([jnp.where(mask, q, none), qs_ref[...]], axis=1)
        score_own = mm_nt(query, keys_own)
        score_other = mm_nt(query, keys_other)
        peak = jnp.maximum(
            jnp.max(score_own, axis=1, keepdims=True), jnp.max(score_other, axis=1, keepdims=True)
        )
        own = jnp.exp(score_own - peak).astype(BF)
        other = jnp.exp(score_other - peak).astype(BF)
        total = mm(own, jnp.concatenate([jnp.where(mask, values_own, none), ones], axis=1)) + mm(
            other, jnp.concatenate([jnp.where(mask, values_other, none), ones], axis=1)
        )
        row_total = total[:, LANES:]
        context = context + total[:, :LANES] / row_total
        logs = jnp.where(lane == 2 * pair + which, peak + jnp.log(row_total), logs)
    lse_acc[...] = logs
    ctx_acc[pair] = context.astype(BF)
    ctx_ref[...] = context.astype(BF)

    @pl.when(pair == PAIRS - 1)
    def _():
        lse_ref[...] = lse_acc[...]
        full = jnp.concatenate([ctx_acc[k] for k in range(PAIRS)], axis=1)
        branch = mm(full, w_ref[0])
        summed = x_ref[...].astype(F32) + branch
        normal, _ = norm_parts(summed)
        moved = normal * norm_ref[0:1, :] + norm_ref[1:2, :]
        next_ref[...] = moved.astype(BF)
        sum_ref[...] = summed
        fnew_ref[...] = fsum_ref[...] + branch


def attend(stream, projected, other_kv, segs, weights, layer, norms, branch_sum):
    qseg, kseg_own, kseg_other = segs

    def column(offset):
        return pl.BlockSpec((HALF, LANES), lambda i: (0, offset + i))

    return pl.pallas_call(
        attend_kernel,
        grid=(PAIRS,),
        in_specs=[
            column(0), column(PAIRS), column(2 * PAIRS), column(0), column(PAIRS),
            whole(HALF, LANES), whole(HALF, LANES), whole(HALF, LANES),
            pl.BlockSpec((1, D, D), lambda i: (layer, 0, 3)),
            whole(HALF, D), whole(HALF, D), whole(2, D),
        ],
        out_specs=[
            column(0), whole(HALF, LANES), whole(HALF, D), whole(HALF, D), whole(HALF, D),
        ],
        out_shape=[
            shaped(HALF, D, BF), shaped(HALF, LANES, F32), shaped(HALF, D, BF),
            shaped(HALF, D, F32), shaped(HALF, D, F32),
        ],
        scratch_shapes=[pltpu.VMEM((PAIRS, HALF, LANES), BF), pltpu.VMEM((HALF, LANES), F32)],
        compiler_params=params(),
        cost_estimate=cost(8e9, 8e6, 4e6),
        name="attend",
    )(
        projected, projected, projected, other_kv, other_kv, qseg, kseg_own, kseg_other,
        weights, stream, branch_sum, norms,
    )


def gelu_parts(v):
    root = 0.7978845608028654
    squared = v * v
    inner = root * (v + 0.044715 * v * squared)
    t = jnp.tanh(inner)
    hidden = 0.5 * v * (1.0 + t)
    slope = 0.5 * (1.0 + t) + 0.5 * v * (1.0 - t * t) * (root * (1.0 + 3 * 0.044715 * squared))
    return hidden, slope


def feed_kernel(
    x_ref, w1_ref, w2_ref, fsum_ref, norm_ref, next_ref, sum_ref, fnew_ref, acc_ref
):
    step = pl.program_id(0)
    preact = mm(x_ref[...], w1_ref[0])
    hidden = gelu_parts(preact)[0].astype(BF)
    part = mm_nt(hidden, w2_ref[0])

    @pl.when(step == 0)
    def _():
        acc_ref[...] = part

    @pl.when(step > 0)
    def _():
        acc_ref[...] += part

    @pl.when(step == 3)
    def _():
        branch = acc_ref[...]
        summed = x_ref[...].astype(F32) + branch
        normal, _ = norm_parts(summed)
        moved = normal * norm_ref[0:1, :] + norm_ref[1:2, :]
        next_ref[...] = moved.astype(next_ref.dtype)
        sum_ref[...] = summed
        fnew_ref[...] = fsum_ref[...] + branch


def first_spec(layer):
    return pl.BlockSpec((1, D, D), lambda i: (layer - 1 + i // 2, 0, (4 + i) % 6))


def second_spec(layer):
    return pl.BlockSpec((1, D, D), lambda i: (layer, 0, 2 + i))


def feed(stream, weights, layer, norms, branch_sum, out_type):
    return pl.pallas_call(
        feed_kernel,
        grid=(4,),
        in_specs=[
            whole(HALF, D), first_spec(layer), second_spec(layer), whole(HALF, D), whole(2, D),
        ],
        out_specs=[whole(HALF, D), whole(HALF, D), whole(HALF, D)],
        out_shape=[shaped(HALF, D, out_type), shaped(HALF, D, F32), shaped(HALF, D, F32)],
        scratch_shapes=[pltpu.VMEM((HALF, D), F32)],
        compiler_params=params(),
        cost_estimate=cost(4 * HALF * D * 4 * D, 8e6, HALF * 4 * D),
        name="feed",
    )(stream, weights, weights, branch_sum, norms)


def finish_kernel(
    x_ref, fsum_ref, y_ref, cot_ref, live_ref, norm_ref, out_ref, c_ref, dy_ref, grad_ref
):
    summed = y_ref[...].astype(F32) + fsum_ref[...]
    normal, _ = norm_parts(summed)
    gain = norm_ref[0:1, :]
    out_ref[...] = (x_ref[...] + normal * gain + norm_ref[1:2, :]).astype(BF)
    cot = cot_ref[...].astype(F32) * live_ref[:, 0:1]
    c_ref[...] = cot
    grad, gain_grad, shift_grad = norm_back(summed, gain, cot)
    dy_ref[...] = grad
    grad_ref[0:1, :] = gain_grad
    grad_ref[1:2, :] = shift_grad


def finish(last, branch_sum, accum, cot, live, norms):
    return pl.pallas_call(
        finish_kernel,
        grid=(1,),
        in_specs=[
            whole(HALF, D), whole(HALF, D), whole(HALF, D), whole(HALF, D), whole(HALF, LANES),
            whole(2, D),
        ],
        out_specs=[whole(HALF, D), whole(HALF, D), whole(HALF, D), whole(2, D)],
        out_shape=[
            shaped(HALF, D, BF), shaped(HALF, D, F32), shaped(HALF, D, F32), shaped(2, D, F32),
        ],
        compiler_params=params(),
        cost_estimate=cost(1e7, 6e6),
        name="finish",
    )(last, branch_sum, accum, cot, live, norms)


def feed_back_kernel(
    x_ref, sum_ref, up_ref, dy_ref, w1_ref, w2_ref, norm_ref,
    dx_ref, dw1_ref, dw2_ref, grad_ref, acc_ref, df_ref, dft_ref, xt_ref,
):
    step = pl.program_id(0)

    @pl.when(step == 0)
    def _():
        grad, gain_grad, shift_grad = norm_back(
            sum_ref[...], norm_ref[0:1, :], up_ref[...].astype(F32)
        )
        grad_ref[0:1, :] = gain_grad
        grad_ref[1:2, :] = shift_grad
        acc_ref[...] = grad
        df = (grad + dy_ref[...]).astype(BF)
        df_ref[...] = df
        dft_ref[...] = df.T
        xt_ref[...] = x_ref[...].T

    preact = mm(x_ref[...], w1_ref[0])
    hidden, slope = gelu_parts(preact)
    dw2_ref[...] = mm(dft_ref[...], hidden.astype(BF)).astype(BF)
    hidden_grad = mm(df_ref[...], w2_ref[0])
    preact_grad = (hidden_grad * slope).astype(BF)
    dw1_ref[...] = mm(xt_ref[...], preact_grad).astype(BF)
    acc_ref[...] += mm_nt(preact_grad, w1_ref[0])

    @pl.when(step == 3)
    def _():
        dx_ref[...] = acc_ref[...].astype(BF)


def feed_back(stream, summed, upstream, dy, weights, layer, norms):
    return pl.pallas_call(
        feed_back_kernel,
        grid=(4,),
        in_specs=[
            whole(HALF, D), whole(HALF, D), whole(HALF, D), whole(HALF, D),
            first_spec(layer), second_spec(layer), whole(2, D),
        ],
        out_specs=[
            whole(HALF, D),
            pl.BlockSpec((D, D), lambda i: (0, i)),
            pl.BlockSpec((D, D), lambda i: (0, i)),
            whole(2, D),
        ],
        out_shape=[
            shaped(HALF, D, BF), shaped(D, 4 * D, BF), shaped(D, 4 * D, BF), shaped(2, D, F32),
        ],
        scratch_shapes=[
            pltpu.VMEM((HALF, D), F32), pltpu.VMEM((HALF, D), BF), pltpu.VMEM((D, HALF), BF),
            pltpu.VMEM((D, HALF), BF),
        ],
        compiler_params=params(),
        cost_estimate=cost(10 * HALF * D * 4 * D, 16e6, HALF * 4 * D),
        name="feed_back",
    )(stream, summed, upstream, dy, weights, weights, norms)


def outward_back_kernel(
    sum_ref, up_ref, dy_ref, ctx_ref, w_ref, norm_ref, dz_ref, dctx_ref, dwo_ref, delta_ref,
    grad_ref,
):
    grad, gain_grad, shift_grad = norm_back(sum_ref[...], norm_ref[0:1, :], up_ref[...].astype(F32))
    grad_ref[0:1, :] = gain_grad
    grad_ref[1:2, :] = shift_grad
    dz_ref[...] = grad
    df = (grad + dy_ref[...]).astype(BF)
    context = ctx_ref[...]
    dwo_ref[...] = mm_tn(context, df).astype(BF)
    context_grad = mm_nt(df, w_ref[0]).astype(BF)
    dctx_ref[...] = context_grad
    product = context.astype(F32) * context_grad.astype(F32)
    lane = lax.broadcasted_iota(jnp.int32, (1, LANES), 1)
    delta = jnp.zeros((HALF, LANES), F32)
    for head in range(HEADS):
        part = product[:, (head // 2) * LANES : (head // 2 + 1) * LANES]
        inner = jnp.sum(jnp.where(head_mask(head % 2), part, 0.0), axis=1, keepdims=True)
        delta = jnp.where(lane == head, inner, delta)
    delta_ref[...] = delta


def outward_back(summed, upstream, dy, context, weights, layer, norms):
    return pl.pallas_call(
        outward_back_kernel,
        grid=(1,),
        in_specs=[
            whole(HALF, D), whole(HALF, D), whole(HALF, D), whole(HALF, D),
            pl.BlockSpec((1, D, D), lambda i: (layer, 0, 3)), whole(2, D),
        ],
        out_specs=[
            whole(HALF, D), whole(HALF, D), whole(D, D), whole(HALF, LANES), whole(2, D),
        ],
        out_shape=[
            shaped(HALF, D, F32), shaped(HALF, D, BF), shaped(D, D, BF), shaped(HALF, LANES, F32),
            shaped(2, D, F32),
        ],
        compiler_params=params(),
        cost_estimate=cost(4 * HALF * D * D, 6e6),
        name="outward_back",
    )(summed, upstream, dy, context, weights, norms)


def scores_back_kernel(
    q_ref, k_ref, v_ref, dctx_ref, qs_ref, ks_ref, lse_ref, delta_ref, before_ref,
    dq_ref, dk_ref, dv_ref,
):
    pair = pl.program_id(0)
    none = jnp.zeros((), BF)
    lane = lax.broadcasted_iota(jnp.int32, (1, LANES), 1)
    q = q_ref[...] * jnp.asarray(SCALE, BF)
    k = k_ref[...]
    k_scaled = k * jnp.asarray(SCALE, BF)
    dctx = dctx_ref[...]
    extra = jnp.where((lane >= LANES - 3), jnp.ones((), BF), none)
    keys = jnp.concatenate([k, ks_ref[...] + extra], axis=1)
    values = jnp.concatenate([v_ref[...], jnp.broadcast_to(extra, (HALF, LANES))], axis=1)
    dq = before_ref[...]
    dk = jnp.zeros((HALF, LANES), F32)
    dv = jnp.zeros((HALF, LANES), F32)
    for which in range(2):
        mask = head_mask(which)
        here = lane == 2 * pair + which

        def lanes_of(table, base):
            column = -jnp.sum(jnp.where(here, table, 0.0), axis=1, keepdims=True)
            high, middle, low = three_way(column)
            base = jnp.where(lane == LANES - 3, high, base)
            base = jnp.where(lane == LANES - 2, middle, base)
            return jnp.where(lane == LANES - 1, low, base)

        query_part = jnp.where(mask, q, none)
        dctx_part = jnp.where(mask, dctx, none)
        query = jnp.concatenate([query_part, lanes_of(lse_ref[...], qs_ref[...])], axis=1)
        dcontext = jnp.concatenate(
            [dctx_part, lanes_of(delta_ref[...], jnp.zeros((HALF, LANES), BF))], axis=1
        )
        probability = jnp.exp(mm_nt(keys, query))
        score_grad = (probability * mm_nt(values, dcontext)).astype(BF)
        dv = dv + mm(probability.astype(BF), dctx_part)
        dk = dk + mm(score_grad, query_part)
        dq = dq + mm_tn(score_grad, jnp.where(mask, k_scaled, none))
    dq_ref[...] = dq
    dk_ref[...] = dk.astype(dk_ref.dtype)
    dv_ref[...] = dv.astype(dv_ref.dtype)


def scores_back(projected, keys, key_offset, dctx, qseg, kseg, lse, delta, before, out_type):
    def column(offset):
        return pl.BlockSpec((HALF, LANES), lambda i: (0, offset + i))

    return pl.pallas_call(
        scores_back_kernel,
        grid=(PAIRS,),
        in_specs=[
            column(0), column(key_offset), column(key_offset + PAIRS), column(0),
            whole(HALF, LANES), whole(HALF, LANES), whole(HALF, LANES), whole(HALF, LANES),
            column(0),
        ],
        out_specs=[column(0), column(0), column(0)],
        out_shape=[shaped(HALF, D, F32), shaped(HALF, D, out_type), shaped(HALF, D, out_type)],
        compiler_params=params(),
        cost_estimate=cost(8e9, 8e6, 2e6),
        name="scores_back",
    )(projected, keys, keys, dctx, qseg, kseg, lse, delta, before)


def project_back_kernel(
    x_ref, dq_ref, dk_ref, dv_ref, dkx_ref, dvx_ref, dz_ref, w_ref, dx_ref, dw_ref, acc_ref, xt_ref
):
    step = pl.program_id(0)

    @pl.when(step == 0)
    def _():
        xt_ref[...] = x_ref[...].T
        acc_ref[...] = dz_ref[...]

    def add(grad):
        dw_ref[...] = mm(xt_ref[...], grad).astype(BF)
        acc_ref[...] += mm_nt(grad, w_ref[0])

    @pl.when(step == 0)
    def _():
        add(dq_ref[...].astype(BF))

    @pl.when(step == 1)
    def _():
        add((dk_ref[...] + dkx_ref[...].astype(F32)).astype(BF))

    @pl.when(step == 2)
    def _():
        add((dv_ref[...] + dvx_ref[...].astype(F32)).astype(BF))
        dx_ref[...] = acc_ref[...].astype(BF)


def project_back(stream, dq, dk, dv, dk_other, dv_other, dz, weights, layer):
    return pl.pallas_call(
        project_back_kernel,
        grid=(3,),
        in_specs=[whole(HALF, D)] * 7 + [pl.BlockSpec((1, D, D), lambda i: (layer, 0, i))],
        out_specs=[whole(HALF, D), pl.BlockSpec((D, D), lambda i: (0, i))],
        out_shape=[shaped(HALF, D, BF), shaped(D, 3 * D, BF)],
        scratch_shapes=[pltpu.VMEM((HALF, D), F32), pltpu.VMEM((D, HALF), BF)],
        compiler_params=params(),
        cost_estimate=cost(4 * HALF * D * 3 * D, 10e6),
        name="project_back",
    )(stream, dq, dk, dv, dk_other, dv_other, dz, weights)


class Places:
    def __init__(self):
        self.ndp = lax.axis_size("dp")
        self.section = lax.axis_index("section")
        self.dp = lax.axis_index("dp")
        self.core = self.dp % 2

    def swap_core(self, block):
        return lax.ppermute(block, "dp", [(i, i ^ 1) for i in range(self.ndp)])

    def swap_section(self, block, step):
        return lax.ppermute(block, "section", [(i, i ^ step) for i in range(SECTIONS)])

    def send(self, block, route):
        pairs = []
        for s in range(SECTIONS):
            for d in range(self.ndp):
                to = route(s, d)
                if to is not None:
                    pairs.append((s * self.ndp + d, to[0] * self.ndp + to[1]))
        return lax.ppermute(block, ("section", "dp"), pairs)


def pick(stack, index):
    return lax.dynamic_index_in_dim(stack, index, 0, keepdims=False)


def tokens_in(places, block):
    pieces = block.reshape(4, HALF, D // SECTIONS)
    got = []
    for turn in range(4):

        def route(s, d, turn=turn):
            piece = s ^ turn
            return 2 * (d % 2) + piece // 2, d - d % 2 + piece % 2

        got.append(places.send(pick(pieces, places.section ^ turn), route))
    got = jnp.stack(got)
    mine = 2 * (places.section % 2) + places.core
    return jnp.concatenate([pick(got, mine ^ f) for f in range(SECTIONS)], axis=1)


def tokens_out(places, rows):
    features = jnp.stack(jnp.split(rows, SECTIONS, axis=1))
    mine = 2 * (places.section % 2) + places.core
    got = []
    for turn in range(4):

        def route(s, d, turn=turn):
            return (2 * (s % 2) + d % 2) ^ turn, d - d % 2 + s // 2

        got.append(places.send(pick(features, mine ^ turn), route))
    got = jnp.stack(got)
    return jnp.concatenate([pick(got, places.section ^ k) for k in range(4)], axis=0)


def weights_in(places, own):
    half = D // 2
    quarter = half // 2
    start = places.core * half
    mine = lax.dynamic_slice_in_dim(own, start, half, 0)
    from_x = places.swap_section(mine, 1)
    from_y = places.swap_section(mine, 2)
    diagonal = jnp.concatenate(
        [places.swap_section(from_x[:quarter], 2), places.swap_section(from_y[quarter:], 1)], axis=0
    )
    full = jnp.zeros((SECTIONS, D, 6 * D), BF)
    full = lax.dynamic_update_slice(full, own[None], (places.section, 0, 0))
    for step, piece in ((1, from_x), (2, from_y), (3, diagonal)):
        full = lax.dynamic_update_slice(full, piece[None], (places.section ^ step, start, 0))
        full = lax.dynamic_update_slice(
            full, places.swap_core(piece)[None], (places.section ^ step, half - start, 0)
        )
    return full


def reduce_columns(places, part, root, group):
    ndp = places.ndp
    blocks = part.reshape(D, ndp // 4, 2, 6 * D // ndp)
    keep = lax.dynamic_index_in_dim(blocks, places.core, 2, keepdims=False)
    give = lax.dynamic_index_in_dim(blocks, 1 - places.core, 2, keepdims=False)
    summed = keep + places.swap_core(give)
    half = D // 2

    def toward(block, step, second):
        if second:
            route = lambda s, d: (root, d) if s == root ^ step else None
        else:
            route = lambda s, d: (s ^ step, d) if (s ^ root) & step else None
        return block + places.send(block, route)

    upper = toward(toward(summed[:half], 1, False), 2, True)
    lower = toward(toward(summed[half:], 2, False), 1, True)
    summed = jnp.concatenate([upper, lower], axis=0)
    bit = 2
    while bit < ndp // 2:
        count = summed.shape[1]
        blocks = summed.reshape(D, count // 2, 2, summed.shape[2])
        mine = (places.dp // bit) % 2
        keep = lax.dynamic_index_in_dim(blocks, mine, 2, keepdims=False)
        give = lax.dynamic_index_in_dim(blocks, 1 - mine, 2, keepdims=False)
        route = lambda s, d, bit=bit: (s, d ^ bit) if s == root else None
        summed = keep + places.send(give, route)
        bit *= 2
    top = ndp // 2
    route = lambda s, d: (s, d ^ top) if s == root and (d // top) != group else None
    return (summed + places.send(summed, route)).reshape(D, 6 * D // ndp)


def on_device(
    stream_input,
    accum_input,
    section_weights,
    section_norms,
    final_norm,
    seq_lengths,
    out_cotangent,
):
    places = Places()
    section, core = places.section, places.core

    other_lengths = places.swap_core(seq_lengths)
    lengths = pick(jnp.where(core == section // 2, seq_lengths, other_lengths), section % 2)
    ending = jnp.cumsum(lengths, dtype=jnp.int32)

    def rows_of(which):
        spots = which * HALF + jnp.arange(HALF, dtype=jnp.int32)
        segment = jnp.sum(
            (spots[:, None] >= ending[None, :]).astype(jnp.int32), axis=1, dtype=jnp.int32
        )
        lane = jnp.arange(LANES, dtype=jnp.int32)
        hot = (segment[:, None] == lane[None, :]).astype(BF)
        alive = (spots < ending[-1]).astype(F32)
        return segment, hot, jnp.broadcast_to(alive[:, None], (HALF, LANES))

    segment_own, kseg_own, live = rows_of(core)
    _, kseg_other, _ = rows_of(1 - core)
    lane = jnp.arange(LANES, dtype=jnp.int32)
    qseg = jnp.where(
        (segment_own[:, None] != lane[None, :]) & (lane[None, :] < 32), -FAR, 0.0
    ).astype(BF)
    segs = (qseg, kseg_own, kseg_other)

    stream = tokens_in(places, stream_input)
    weights = weights_in(places, section_weights[0])
    small = jnp.concatenate([section_norms.reshape(2, D), final_norm.reshape(2, -1)], axis=1)
    small = lax.all_gather(small, "section", axis=0).astype(F32)
    norms = small[:, :, :D]
    final = jnp.concatenate([small[f, :, D:] for f in range(SECTIONS)], axis=1)
    accum = tokens_in(places, accum_input)
    cot = tokens_in(places, out_cotangent)

    branch_sum = jnp.zeros((HALF, D), F32)
    kept = []
    for layer in (0, 2):
        projected = project(stream, weights, layer)
        other_kv = places.swap_core(projected[:, D:])
        context, lse, middle, sum_a, branch_sum = attend(
            stream, projected, other_kv, segs, weights, layer, norms[layer], branch_sum
        )
        following, sum_f, branch_sum = feed(
            middle, weights, layer + 1, norms[layer + 1], branch_sum, BF if layer == 0 else F32
        )
        kept.append((stream, projected, other_kv, context, lse, sum_a, middle, sum_f))
        stream = following

    result, upstream, dy, final_grad = finish(stream, branch_sum, accum, cot, live, final)
    result_out = tokens_out(places, result)
    accum_out = tokens_out(places, dy.astype(BF))

    norm_grads = [None] * SECTIONS
    sums = {}
    for layer in (2, 0):
        entering, projected, other_kv, context, lse, sum_a, middle, sum_f = kept[layer // 2]
        upstream, dw1, dw2, norm_grads[layer + 1] = feed_back(
            middle, sum_f, upstream, dy, weights, layer + 1, norms[layer + 1]
        )
        odd = jnp.concatenate([dw1[:, 2 * D :], dw2], axis=1)
        sums[layer + 1, 0] = reduce_columns(places, odd[:, : 3 * D], layer + 1, 0)
        sums[layer + 1, 1] = reduce_columns(places, odd[:, 3 * D :], layer + 1, 1)
        dz, dctx, dwo, delta, norm_grads[layer] = outward_back(
            sum_a, upstream, dy, context, weights, layer, norms[layer]
        )
        sums[layer, 1] = reduce_columns(
            places, jnp.concatenate([dwo, dw1[:, : 2 * D]], axis=1), layer, 1
        )
        dq, dk_far, dv_far = scores_back(
            projected, other_kv, 0, dctx, qseg, kseg_other, lse, delta,
            jnp.zeros((HALF, D), F32), BF,
        )
        dk_other, dv_other = places.swap_core(dk_far), places.swap_core(dv_far)
        dq, dk, dv = scores_back(
            projected, projected, PAIRS, dctx, qseg, kseg_own, lse, delta, dq, F32
        )
        upstream, dqkv = project_back(
            entering, dq, dk, dv, dk_other, dv_other, dz, weights, layer
        )
        sums[layer, 0] = reduce_columns(places, dqkv, layer, 0)

    stream_out = tokens_out(places, upstream)
    small_grads = jnp.concatenate(norm_grads + [final_grad], axis=0)
    small_grads = lax.psum(small_grads, ("section", "dp"))
    norm_out = lax.dynamic_slice(
        small_grads, (2 * section, places.dp * (D // places.ndp)), (2, D // places.ndp)
    )
    width = D // SECTIONS
    final_out = lax.dynamic_slice(small_grads, (2 * SECTIONS, section * width), (2, width))

    group = places.dp // (places.ndp // 2)
    slab = jnp.zeros((D, 6 * D // places.ndp), BF)
    for (s, g), value in sums.items():
        slab = jnp.where((section == s) & (group == g), value, slab)

    return (
        result_out,
        stream_out.astype(F32),
        accum_out.astype(F32),
        slab.astype(F32)[None],
        norm_out[None],
        final_out,
    )


def solution(mesh):
    placed = (
        P("dp", "section"),
        P("dp", "section"),
        P("section", None, None),
        P("section", None, None),
        P(None, "section"),
        P("dp", None),
        P("dp", "section"),
    )
    return jax.shard_map(
        on_device,
        mesh=mesh,
        in_specs=placed,
        out_specs=(
            P("dp", "section"),
            P("dp", "section"),
            P("dp", "section"),
            P("section", None, "dp"),
            P("section", None, "dp"),
            P(None, "section"),
        ),
        check_vma=False,
    )
```

time: 1980 us -> 687 us (0.35)
  waiting for transfers between devices: 731 us -> 70.4 us
  other arithmetic: 358 us -> 30.5 us
  matrix products: 274 us -> 0 us
  local copies, waits for them, and re-layouts: 308 us -> 130 us
  Pallas kernels: 0 us -> 120 us
  blocking collectives: 42.4 us -> 81 us
  loops' own time: 33.1 us -> 0 us
  starting transfers between devices: 211 us -> 242 us
    ppermute x22 -> x94, waiting for transfers between devices: 544 us -> 70.4 us  [the longest x72 54.3 us: send(): return lax.ppermute(block, ('section', 'dp'), pairs)]
    dot_general x52 -> x0, matrix products: 274 us -> none  [the longest x12 96.2 us: block_scores(): jnp.einsum('qhd,khd->hqk', query_block, key_rows, preferred_element_type=...]
    pallas_call x0 -> x17, Pallas kernels: none -> 120 us  [the longest x4 39.3 us: scores_back(): pl.pallas_call(scores_back_kernel, grid=(PAIRS,), in_specs=[column(0), co...]
    sub x4 -> x0, other arithmetic: 86.8 us -> none  [attend_one_block(): exponent = jnp.exp(scores - row_peak)]
    unnamed x14 -> x0, waiting for transfers between devices: 82.8 us -> none
    reduce_scatter x1 -> x0, waiting for transfers between devices: 67.6 us -> none  [on_device(): lax.psum_scatter(slab_term, 'dp', scatter_dimension=1, tiled=True)]
    dynamic_slice x80 -> x14, local copies, waits for them, and re-layouts: 100 us -> 44.5 us  [the longest x4 33.3 us: reduce_columns(): keep = lax.dynamic_index_in_dim(blocks, places.core, 2, keepdims=False)]
    convert_element_type x18 -> x9, other arithmetic: 60.9 us -> 5.91 us  [the longest x1 1.24 us: on_device(): slab.astype(F32)[None]]
  transfers between devices with their start and end apart: 31 -> 94, of which waited for: 15 -> 20; matrix products, arithmetic and copies ran while one was open for 45% -> 19% of each run, Pallas kernels for 0% -> 10%
where the time goes in v1:
time: 687 us; the launch traced here: 676 us
  starting transfers between devices  242 us (35%)
  local copies, waits for them, and re-layouts  130 us (19%)
  Pallas kernels  120 us (17%)
  blocking collectives  81 us (12%)
  waiting for transfers between devices  70.4 us (10%)
  other arithmetic  30.5 us (4%)
    ppermute x72, starting transfers between devices, send(): return lax.ppermute(block, ('section', 'dp'), pairs)  224 us
    ppermute x72, waiting for transfers between devices, send(): return lax.ppermute(block, ('section', 'dp'), pairs)  54.3 us
    all_gather x1, blocking collectives, on_device(): small = lax.all_gather(small, 'section', axis=0).astype(F32)  41.4 us
    psum x1, blocking collectives, on_device(): small_grads = lax.psum(small_grads, ('section', 'dp'))  39.7 us
    pallas_call x4, Pallas kernels, scores_back(): pl.pallas_call(scores_back_kernel, grid=(PAIRS,), in_specs=[column(0), co...  39.3 us
    reshape x8, local copies, waits for them, and re-layouts, reduce_columns(): blocks = part.reshape(D, ndp // 4, 2, 6 * D // ndp)  35.8 us
    dynamic_slice x4, local copies, waits for them, and re-layouts, reduce_columns(): keep = lax.dynamic_index_in_dim(blocks, places.core, 2, keepdims=False)  33.3 us
    pallas_call x2, Pallas kernels, feed_back(): pl.pallas_call(feed_back_kernel, grid=(4,), in_specs=[whole(HALF, D), who...  22.4 us
  transfers between devices with their start and end apart: 94, of which 20 were waited for; matrix products, arithmetic and copies ran while one was open for 19% of the time, Pallas kernels for 10%

profile of v1, /device:TPU:8, one launch (start us, length us, event | category | flops | bytes accessed | tf_op | source)
XLA Modules:
  0.0 675.9 jit_solution(7912601484418750659)
XLA Ops:
  4.9 5.0 collective-permute-start.6
  13.8 41.4 %all-gather.1 = bf16[4,2,640]{2,1,0:T(2,128)(2,1)S(1)} all-gather(bf16[1,2,640]{2,1,0:T(2,128)(2,1)S(1)} %maximum_bitcast_fusion), channel_id=2, replica_groups=mesh['section'=4,'dp'=8] {'section'}, dimensions={0}, use_global_device_ids=true | all-gather | bytes 12800 | tf_op jit(solution)/shard_map/all_gather | solution.py:638
  55.8 6.1 broadcast_in_dim.28
  74.0 4.1 collective-permute-start.8
  82.6 14.8 %collective-permute-done.8 = bf16[128,3072]{1,0:T(8,128)(2,1)S(1)} collective-permute-done((bf16[128,3072]{1,0:T(8,128)(2,1)S(1)}, bf16[128,3072]{1,0:T(8,128)(2,1)S(1)}, u32[]{:S(2)}, u32[]{:S(2)}) %collective-permute-start.8) | collective-permute-done | bytes 786464 | tf_op jit(solution)/shard_map/ppermute | solution.py:503
  118.3 10.5 %attend.2 = (bf16[512,512]{1,0:T(8,128)(2,1)S(1)}, f32[512,128]{1,0:T(8,128)S(1)}, bf16[512,512]{1,0:T(8,128)(2,1)S(1)}, f32[512,512]{1,0:T(8,128)S(1)}, f32[512,512]{1,0:T(8,128)S(1)}) custom-call(bf16[512,1536]{1,0:T(8,128)(2,1)} %copy-done, bf16[512,1536]{1,0:T(8,128)(2,1)} %copy-done, bf16[512,1536]{1,0:T(8,128)(2,1)} %copy-done, ...), custom_call_target="tpu_custom_call" | custom-call | flops 8000000000 | bytes 8000000 | tf_op jit(solution)/shard_map/attend/pallas_call | solution.py:163
  129.9 6.4 feed.2
  137.4 3.4 project.3.q_ref.ko_ref.vo_ref.k_ref.v_ref
  149.0 3.5 collective-permute-start.21
  158.4 10.6 %attend.3 = (bf16[512,512]{1,0:T(8,128)(2,1)S(1)}, f32[512,128]{1,0:T(8,128)S(1)}, bf16[512,512]{1,0:T(8,128)(2,1)S(1)}, f32[512,512]{1,0:T(8,128)S(1)}, f32[512,512]{1,0:T(8,128)S(1)}) custom-call(bf16[512,1536]{1,0:T(8,128)(2,1)} %copy-done.1, bf16[512,1536]{1,0:T(8,128)(2,1)} %copy-done.1, bf16[512,1536]{1,0:T(8,128)(2,1)} %copy-done.1, ...), custom_call_target="tpu_custom_call" | custom-call | flops 8000000000 | bytes 8000000 | tf_op jit(solution)/shard_map/attend/pallas_call | solution.py:163
  169.1 5.9 feed.3
  177.1 11.2 %feed_back.2 = (bf16[512,512]{1,0:T(8,128)(2,1)S(1)}, bf16[512,2048]{1,0:T(8,128)(2,1)}, bf16[512,2048]{1,0:T(8,128)(2,1)}, f32[2,512]{1,0:T(2,128)S(1)}) custom-call(bf16[512,512]{1,0:T(8,128)(2,1)S(1)} %get-tuple-element.64.x_ref, f32[512,512]{1,0:T(8,128)S(1)} %get-tuple-element.72.sum_ref, f32[512,512]{1,0:T(8,128)S(1)} %get-tuple-element.73.up_ref, ...), custom_call_target="tpu_custom_call" | custom-call | flops 5368709120 | bytes 16000000 | tf_op jit(solution)/shard_map/feed_back/pallas_call | solution.py:316
  193.8 9.4 %scores_back.4 = (f32[512,512]{1,0:T(8,128)S(1)}, bf16[512,512]{1,0:T(8,128)(2,1)S(1)}, bf16[512,512]{1,0:T(8,128)(2,1)S(1)}) custom-call(bf16[512,1536]{1,0:T(8,128)(2,1)} %copy-done.1, bf16[512,1024]{1,0:T(8,128)(2,1)} %collective-permute-done.13.kx_ref.vx_ref.k_ref.v_ref, bf16[512,1024]{1,0:T(8,128)(2,1)} %collective-permute-done.13.kx_ref.vx_ref.k_ref.v_ref, ...), custom_call_target="tpu_custom_call" | custom-call | flops 8000000000 | bytes 8000000 | tf_op jit(solution)/shard_map/scores_back/pallas_call | solution.py:434
  203.2 10.2 %scores_back.5 = (f32[512,512]{1,0:T(8,128)S(1)}, f32[512,512]{1,0:T(8,128)S(1)}, f32[512,512]{1,0:T(8,128)S(1)}) custom-call(bf16[512,1536]{1,0:T(8,128)(2,1)} %copy-done.1, bf16[512,1536]{1,0:T(8,128)(2,1)} %copy-done.1, bf16[512,1536]{1,0:T(8,128)(2,1)} %copy-done.1, bf16[512,512]{1,0:T(8,128)(2,1)S(1)} %get-tuple-element.77.dctx_ref, ...), custom_call_target="tpu_custom_call" | custom-call | flops 8000000000 | bytes 8000000 | tf_op jit(solution)/shard_map/scores_back/pallas_call | solution.py:434
  218.2 4.6 reshape.240
  222.8 4.6 reshape.241
  229.3 5.9 collective-permute-start.37
  245.4 7.8 %constant_dynamic-slice_fusion.1 = (bf16[512,2,1,384]{3,2,1,0:T(2,128)(2,1)}, bf16[512,2,1,384]{3,2,1,0:T(2,128)(2,1)}, bf16[512,2,1,384]{3,2,1,0:T(2,128)(2,1)}, bf16[512,2,1,384]{3,2,1,0:T(2,128)(2,1)}) fusion(bf16[512,2,2,384]{3,2,1,0:T(2,128)(2,1)S(1)} %copy-done.43, s32[]{:T(128)S(6)} %select_n.339, s32[]{:T(128)S(6)} %select_n.340, ...), kind=kLoop, calls=%fused_computation.169 | loop fusion | bytes 6291464 | tf_op jit(solution)/shard_map/jit(dynamic_index_in_dim)/dynamic_slice | solution.py:571
  254.5 4.6 reshape.239
  275.4 5.4 project_back.2
  280.8 11.2 %feed_back.3 = (bf16[512,512]{1,0:T(8,128)(2,1)S(1)}, bf16[512,2048]{1,0:T(8,128)(2,1)S(1)}, bf16[512,2048]{1,0:T(8,128)(2,1)}, f32[2,512]{1,0:T(2,128)S(1)}) custom-call(bf16[512,512]{1,0:T(8,128)(2,1)S(1)} %copy-done.5, f32[512,512]{1,0:T(8,128)S(1)} %copy-done.19, bf16[512,512]{1,0:T(8,128)(2,1)S(1)} %get-tuple-element.87.up_ref, ...), custom_call_target="tpu_custom_call" | custom-call | flops 5368709120 | bytes 16000000 | tf_op jit(solution)/shard_map/feed_back/pallas_call | solution.py:316
  299.7 4.7 reshape.232
  306.4 9.9 %scores_back.6 = (f32[512,512]{1,0:T(8,128)S(1)}, bf16[512,512]{1,0:T(8,128)(2,1)}, bf16[512,512]{1,0:T(8,128)(2,1)}) custom-call(bf16[512,1536]{1,0:T(8,128)(2,1)} %copy-done, bf16[512,1024]{1,0:T(8,128)(2,1)S(1)} %copy-done.29, bf16[512,1024]{1,0:T(8,128)(2,1)S(1)} %copy-done.29, bf16[512,512]{1,0:T(8,128)(2,1)S(1)} %get-tuple-element.90.dctx_ref, ...), custom_call_target="tpu_custom_call" | custom-call | flops 8000000000 | bytes 8000000 | tf_op jit(solution)/shard_map/scores_back/pallas_call | solution.py:434
  316.3 9.7 %scores_back.7 = (f32[512,512]{1,0:T(8,128)S(1)}, f32[512,512]{1,0:T(8,128)S(1)}, f32[512,512]{1,0:T(8,128)S(1)}) custom-call(bf16[512,1536]{1,0:T(8,128)(2,1)} %copy-done, bf16[512,1536]{1,0:T(8,128)(2,1)} %copy-done, bf16[512,1536]{1,0:T(8,128)(2,1)} %copy-done, bf16[512,512]{1,0:T(8,128)(2,1)S(1)} %get-tuple-element.90.dctx_ref, ...), custom_call_target="tpu_custom_call" | custom-call | flops 8000000000 | bytes 8000000 | tf_op jit(solution)/shard_map/scores_back/pallas_call | solution.py:434
  327.5 4.6 reshape.238
  332.0 9.5 %constant_dynamic-slice_fusion.5 = (bf16[512,2,1,384]{3,2,1,0:T(2,128)(2,1)}, bf16[512,2,1,384]{3,2,1,0:T(2,128)(2,1)}, bf16[512,2,1,384]{3,2,1,0:T(2,128)(2,1)}, bf16[512,2,1,384]{3,2,1,0:T(2,128)(2,1)}) fusion(bf16[512,2,2,384]{3,2,1,0:T(2,128)(2,1)} %reshape.239, s32[]{:T(128)S(6)} %select_n.339, s32[]{:T(128)S(6)} %select_n.340, ...), kind=kLoop, calls=%fused_computation.173 | loop fusion | bytes 6291464 | tf_op jit(solution)/shard_map/jit(dynamic_index_in_dim)/dynamic_slice | solution.py:571
  343.5 4.6 reshape.234
  348.1 4.6 reshape.236
  352.6 9.4 %constant_dynamic-slice_fusion.9 = (bf16[512,2,1,384]{3,2,1,0:T(2,128)(2,1)}, bf16[512,2,1,384]{3,2,1,0:T(2,128)(2,1)S(1)}, bf16[512,2,1,384]{3,2,1,0:T(2,128)(2,1)S(1)}, bf16[512,2,1,384]{3,2,1,0:T(2,128)(2,1)}) fusion(bf16[512,2,2,384]{3,2,1,0:T(2,128)(2,1)} %reshape.236, s32[]{:T(128)S(6)} %select_n.339, s32[]{:T(128)S(6)} %select_n.340, ...), kind=kLoop, calls=%fused_computation.177 | loop fusion | bytes 6291464 | tf_op jit(solution)/shard_map/jit(dynamic_index_in_dim)/dynamic_slice | solution.py:571
  366.9 39.7 %psum.7 = f32[10,512]{1,0:T(8,128)S(1)} all-reduce(f32[10,512]{1,0:T(8,128)S(1)} %concatenate.87), channel_id=1, replica_groups=mesh['section'=4,'dp'=8] {'section','dp'}, use_global_device_ids=true, to_apply=%region_3.4 | all-reduce | flops 5120 | bytes 40960 | tf_op jit(solution)/shard_map/psum | solution.py:693
  410.6 4.3 collective-permute-start.81
  414.9 3.9 collective-permute-start.83
  420.3 5.4 project_back.3
  429.8 3.7 reshape.230
  433.7 4.8 collective-permute-start.33
  438.5 6.5 constant_dynamic-slice_fusion.13
  459.6 5.5 collective-permute-start.84
  465.2 6.4 collective-permute-start.82
  471.8 6.5 collective-permute-start.91
  478.5 6.5 collective-permute-start.89
  485.2 4.2 collective-permute-start.53
  494.7 4.0 collective-permute-done.53
  500.1 3.5 collective-permute-done.55
  512.6 5.7 collective-permute-start.85
  518.8 6.6 collective-permute-start.92
  528.9 4.6 collective-permute-start.54
  537.4 4.6 collective-permute-start.61
  542.0 7.0 %collective-permute-start.70 = (bf16[256,2,384]{2,0,1:T(8,128)(2,1)S(1)}, bf16[256,2,384]{2,0,1:T(8,128)(2,1)S(1)}, u32[]{:S(2)}, u32[]{:S(2)}) collective-permute-start(bf16[256,2,384]{2,0,1:T(8,128)(2,1)S(1)} %get-tuple-element.156), channel_id=1, source_target_pairs={{24,16},{25,17},{26,18},{27,19},{28,20},{29,21},{30,22},{31,23}} | collective-permute-start | bytes 1179656 | tf_op jit(solution)/shard_map/ppermute | solution.py:512
  552.4 4.6 collective-permute-start.77
  557.0 7.7 %collective-permute-start.75 = (bf16[256,2,384]{2,0,1:T(8,128)(2,1)S(1)}, bf16[256,2,384]{2,0,1:T(8,128)(2,1)S(1)}, u32[]{:S(2)}, u32[]{:S(2)}) collective-permute-start(bf16[256,2,384]{2,0,1:T(8,128)(2,1)S(1)} %get-tuple-element.161), channel_id=1, source_target_pairs={{0,16},{1,17},{2,18},{3,19},{4,20},{5,21},{6,22},{7,23}} | collective-permute-start | bytes 1179656 | tf_op jit(solution)/shard_map/ppermute | solution.py:512
  573.6 6.5 collective-permute-start.57
  580.3 6.4 collective-permute-start.64
  586.7 6.4 collective-permute-start.71
  593.2 6.4 collective-permute-start.42
  599.6 6.4 collective-permute-start.40
  606.1 6.4 collective-permute-start.49
  612.7 6.4 collective-permute-start.47
  620.0 8.2 %collective-permute-start.78 = (bf16[512,1,384]{2,0,1:T(8,128)(2,1)S(1)}, bf16[512,1,384]{2,0,1:T(8,128)(2,1)S(1)}, u32[]{:S(2)}, u32[]{:S(2)}) collective-permute-start(bf16[512,1,384]{2,0,1:T(8,128)(2,1)S(1)} %fusion.6), channel_id=1, source_target_pairs={{16,18},{17,19},{18,16},{19,17},{20,22},{21,23},{22,20},{23,21}} | collective-permute-start | bytes 1179656 | tf_op jit(solution)/shard_map/ppermute | solution.py:512
  632.3 3.8 collective-permute-start.50
  636.2 6.1 collective-permute-done.43
  643.1 6.8 %collective-permute-done.50 = bf16[512,1,384]{2,0,1:T(8,128)(2,1)S(1)} collective-permute-done((bf16[512,1,384]{2,0,1:T(8,128)(2,1)S(1)}, bf16[512,1,384]{2,0,1:T(8,128)(2,1)S(1)}, u32[]{:S(2)}, u32[]{:S(2)}) %collective-permute-start.50) | collective-permute-done | bytes 393248 | tf_op jit(solution)/shard_map/ppermute | solution.py:512
  652.7 5.5 collective-permute-start.51
  660.3 4.3 collective-permute-done.44
  664.7 9.5 %collective-permute-done.51 = bf16[512,1,384]{2,0,1:T(8,128)(2,1)S(1)} collective-permute-done((bf16[512,1,384]{2,0,1:T(8,128)(2,1)S(1)}, bf16[512,1,384]{2,0,1:T(8,128)(2,1)S(1)}, u32[]{:S(2)}, u32[]{:S(2)}) %collective-permute-start.51) | collective-permute-done | bytes 393248 | tf_op jit(solution)/shard_map/ppermute | solution.py:512
  (463 shorter events, 194.1 us)
Async XLA Ops:
  3.4 69.4 %collective-permute-start.4 = (bf16[256,3072]{1,0:T(8,128)(2,1)}, bf16[256,3072]{1,0:T(8,128)(2,1)}, u32[]{:S(2)}, u32[]{:S(2)}) collective-permute-start(bf16[256,3072]{1,0:T(8,128)(2,1)} %dynamic-slice_bitcast_fusion), channel_id=1, source_target_pairs={{0,8},{8,0},{16,24},{24,16},{1,9},{9,1},{17,25},{25,17},{2,10},{10... | collective-permute-start | bytes 4718600 | tf_op jit(solution)/shard_map/ppermute | solution.py:503
  4.9 73.5 %collective-permute-start.6 = (bf16[256,3072]{1,0:T(8,128)(2,1)}, bf16[256,3072]{1,0:T(8,128)(2,1)S(1)}, u32[]{:S(2)}, u32[]{:S(2)}) collective-permute-start(bf16[256,3072]{1,0:T(8,128)(2,1)} %dynamic-slice_bitcast_fusion), channel_id=1, source_target_pairs={{0,16},{8,24},{16,0},{24,8},{1,17},{9,25},{17,1},{25,9},{2,18},{10... | collective-permute-start | bytes 4718600 | tf_op jit(solution)/shard_map/ppermute | solution.py:503
  10.0 55.0 %collective-permute-start = (bf16[512,128]{1,0:T(8,128)(2,1)S(1)}, bf16[512,128]{1,0:T(8,128)(2,1)S(1)}, u32[]{:S(2)}, u32[]{:S(2)}) collective-permute-start(bf16[512,128]{1,0:T(8,128)(2,1)S(1)} %get-tuple-element.228), channel_id=1, source_target_pairs={{0,0},{1,16},{2,2},{3,18},{4,4},{5,20},{6,6},{7,22},{8,1},{9,17},{... | collective-permute-start | bytes 393224 | tf_op jit(solution)/shard_map/ppermute | solution.py:512
  10.6 57.6 %collective-permute-start.1 = (bf16[512,128]{1,0:T(8,128)(2,1)S(1)}, bf16[512,128]{1,0:T(8,128)(2,1)S(1)}, u32[]{:S(2)}, u32[]{:S(2)}) collective-permute-start(bf16[512,128]{1,0:T(8,128)(2,1)S(1)} %get-tuple-element.231), channel_id=1, source_target_pairs={{0,1},{1,17},{2,3},{3,19},{4,5},{5,21},{6,7},{7,23},{8,0},{9,16},{... | collective-permute-start | bytes 393224 | tf_op jit(solution)/shard_map/ppermute | solution.py:512
  13.5 54.7 %collective-permute-start.2 = (bf16[512,128]{1,0:T(8,128)(2,1)S(1)}, bf16[512,128]{1,0:T(8,128)(2,1)S(1)}, u32[]{:S(2)}, u32[]{:S(2)}) collective-permute-start(bf16[512,128]{1,0:T(8,128)(2,1)S(1)} %get-tuple-element.230), channel_id=1, source_target_pairs={{0,8},{1,24},{2,10},{3,26},{4,12},{5,28},{6,14},{7,30},{8,9},{9,25... | collective-permute-start | bytes 393224 | tf_op jit(solution)/shard_map/ppermute | solution.py:512
  68.2 46.0 %collective-permute-start.12 = (s32[2,16]{1,0:T(2,128)}, s32[2,16]{1,0:T(2,128)S(1)}, u32[]{:S(2)}, u32[]{:S(2)}) collective-permute-start(s32[2,16]{1,0:T(2,128)} %param.12), channel_id=1, source_target_pairs={{0,1},{1,0},{2,3},{3,2},{4,5},{5,4},{6,7},{7,6},{8,9},{9,8},{10,11... | collective-permute-start | bytes 392 | tf_op jit(solution)/shard_map/ppermute | solution.py:500
  68.2 76.8 %collective-permute-start.14 = (bf16[512,128]{1,0:T(8,128)(2,1)}, bf16[512,128]{1,0:T(8,128)(2,1)}, u32[]{:S(2)}, u32[]{:S(2)}) collective-permute-start(bf16[512,128]{1,0:T(8,128)(2,1)} %get-tuple-element.220), channel_id=1, source_target_pairs={{0,0},{1,16},{2,2},{3,18},{4,4},{5,20},{6,6},{7,22},{8,1},{9,17},{... | collective-permute-start | bytes 393224 | tf_op jit(solution)/shard_map/ppermute | solution.py:512
  74.0 23.5 %collective-permute-start.8 = (bf16[128,3072]{1,0:T(8,128)(2,1)S(1)}, bf16[128,3072]{1,0:T(8,128)(2,1)S(1)}, u32[]{:S(2)}, u32[]{:S(2)}) collective-permute-start(bf16[128,3072]{1,0:T(8,128)(2,1)S(1)} %slice.158), channel_id=1, source_target_pairs={{0,16},{8,24},{16,0},{24,8},{1,17},{9,25},{17,1},{25,9},{2,18},{10... | collective-permute-start | bytes 2359304 | tf_op jit(solution)/shard_map/ppermute | solution.py:503
  78.2 20.2 %collective-permute-start.5 = (bf16[256,3072]{1,0:T(8,128)(2,1)}, bf16[256,3072]{1,0:T(8,128)(2,1)S(1)}, u32[]{:S(2)}, u32[]{:S(2)}) collective-permute-start(bf16[256,3072]{1,0:T(8,128)(2,1)} %collective-permute-done.4), channel_id=1, source_target_pairs={{0,1},{1,0},{2,3},{3,2},{4,5},{5,4},{6,7},{7,6},{8,9},{9,8},{10,11... | collective-permute-start | bytes 4718600 | tf_op jit(solution)/shard_map/ppermute | solution.py:500
  78.4 19.9 %collective-permute-start.9 = (bf16[128,3072]{1,0:T(8,128)(2,1)S(1)}, bf16[128,3072]{1,0:T(8,128)(2,1)S(1)}, u32[]{:S(2)}, u32[]{:S(2)}) collective-permute-start(bf16[128,3072]{1,0:T(8,128)(2,1)S(1)} %slice.159), channel_id=1, source_target_pairs={{0,8},{8,0},{16,24},{24,16},{1,9},{9,1},{17,25},{25,17},{2,10},{10... | collective-permute-start | bytes 2359304 | tf_op jit(solution)/shard_map/ppermute | solution.py:503
  97.5 49.1 %collective-permute-start.15 = (bf16[512,128]{1,0:T(8,128)(2,1)}, bf16[512,128]{1,0:T(8,128)(2,1)}, u32[]{:S(2)}, u32[]{:S(2)}) collective-permute-start(bf16[512,128]{1,0:T(8,128)(2,1)} %get-tuple-element.223), channel_id=1, source_target_pairs={{0,1},{1,17},{2,3},{3,19},{4,5},{5,21},{6,7},{7,23},{8,0},{9,16},{... | collective-permute-start | bytes 393224 | tf_op jit(solution)/shard_map/ppermute | solution.py:512
  101.7 47.2 %collective-permute-start.16 = (bf16[512,128]{1,0:T(8,128)(2,1)}, bf16[512,128]{1,0:T(8,128)(2,1)}, u32[]{:S(2)}, u32[]{:S(2)}) collective-permute-start(bf16[512,128]{1,0:T(8,128)(2,1)} %get-tuple-element.222), channel_id=1, source_target_pairs={{0,8},{1,24},{2,10},{3,26},{4,12},{5,28},{6,14},{7,30},{8,9},{9,25... | collective-permute-start | bytes 393224 | tf_op jit(solution)/shard_map/ppermute | solution.py:512
  105.7 43.3 %collective-permute-start.17 = (bf16[512,128]{1,0:T(8,128)(2,1)}, bf16[512,128]{1,0:T(8,128)(2,1)}, u32[]{:S(2)}, u32[]{:S(2)}) collective-permute-start(bf16[512,128]{1,0:T(8,128)(2,1)} %get-tuple-element.221), channel_id=1, source_target_pairs={{0,9},{1,25},{2,11},{3,27},{4,13},{5,29},{6,15},{7,31},{8,8},{9,24... | collective-permute-start | bytes 393224 | tf_op jit(solution)/shard_map/ppermute | solution.py:512
  142.0 16.4 %collective-permute-start.13 = (bf16[512,1024]{1,0:T(8,128)(2,1)}, bf16[512,1024]{1,0:T(8,128)(2,1)}, u32[]{:S(2)}, u32[]{:S(2)}) collective-permute-start(bf16[512,1024]{1,0:T(8,128)(2,1)} %slice.163), channel_id=1, source_target_pairs={{0,1},{1,0},{2,3},{3,2},{4,5},{5,4},{6,7},{7,6},{8,9},{9,8},{10,11... | collective-permute-start | bytes 3145736 | tf_op jit(solution)/shard_map/ppermute | solution.py:500
  229.3 33.4 %collective-permute-start.37 = (bf16[512,128]{1,0:T(8,128)(2,1)}, bf16[512,128]{1,0:T(8,128)(2,1)}, u32[]{:S(2)}, u32[]{:S(2)}) collective-permute-start(bf16[512,128]{1,0:T(8,128)(2,1)} %get-tuple-element.177), channel_id=1, source_target_pairs={{0,24},{1,16},{2,26},{3,18},{4,28},{5,20},{6,30},{7,22},{8,8},{9,0... | collective-permute-start | bytes 393224 | tf_op jit(solution)/shard_map/ppermute | solution.py:512
  236.2 26.5 %collective-permute-start.22 = (bf16[512,128]{1,0:T(8,128)(2,1)}, bf16[512,128]{1,0:T(8,128)(2,1)}, u32[]{:S(2)}, u32[]{:S(2)}) collective-permute-start(bf16[512,128]{1,0:T(8,128)(2,1)} %get-tuple-element.200), channel_id=1, source_target_pairs={{0,0},{1,8},{2,2},{3,10},{4,4},{5,12},{6,6},{7,14},{8,16},{9,24},{... | collective-permute-start | bytes 393224 | tf_op jit(solution)/shard_map/ppermute | solution.py:512
  238.5 24.7 %collective-permute-start.23 = (bf16[512,128]{1,0:T(8,128)(2,1)}, bf16[512,128]{1,0:T(8,128)(2,1)}, u32[]{:S(2)}, u32[]{:S(2)}) collective-permute-start(bf16[512,128]{1,0:T(8,128)(2,1)} %get-tuple-element.203), channel_id=1, source_target_pairs={{0,8},{1,0},{2,10},{3,2},{4,12},{5,4},{6,14},{7,6},{8,24},{9,16},{... | collective-permute-start | bytes 393224 | tf_op jit(solution)/shard_map/ppermute | solution.py:512
  241.2 22.7 %collective-permute-start.24 = (bf16[512,128]{1,0:T(8,128)(2,1)}, bf16[512,128]{1,0:T(8,128)(2,1)}, u32[]{:S(2)}, u32[]{:S(2)}) collective-permute-start(bf16[512,128]{1,0:T(8,128)(2,1)} %get-tuple-element.202), channel_id=1, source_target_pairs={{0,16},{1,24},{2,18},{3,26},{4,20},{5,28},{6,22},{7,30},{8,0},{9,8... | collective-permute-start | bytes 393224 | tf_op jit(solution)/shard_map/ppermute | solution.py:512
  242.4 24.0 %collective-permute-start.25 = (bf16[512,128]{1,0:T(8,128)(2,1)}, bf16[512,128]{1,0:T(8,128)(2,1)}, u32[]{:S(2)}, u32[]{:S(2)}) collective-permute-start(bf16[512,128]{1,0:T(8,128)(2,1)} %get-tuple-element.201), channel_id=1, source_target_pairs={{0,24},{1,16},{2,26},{3,18},{4,28},{5,20},{6,30},{7,22},{8,8},{9,0... | collective-permute-start | bytes 393224 | tf_op jit(solution)/shard_map/ppermute | solution.py:512
  269.5 138.3 %collective-permute-start.80 = (bf16[512,2,384]{2,0,1:T(8,128)(2,1)}, bf16[512,2,384]{2,0,1:T(8,128)(2,1)}, u32[]{:S(2)}, u32[]{:S(2)}) collective-permute-start(bf16[512,2,384]{2,0,1:T(8,128)(2,1)} %bitcast.221), channel_id=1, source_target_pairs={{0,1},{1,0},{2,3},{3,2},{4,5},{5,4},{6,7},{7,6},{8,9},{9,8},{10,11... | collective-permute-start | bytes 2359304 | tf_op jit(solution)/shard_map/ppermute | solution.py:500
  272.6 146.2 %collective-permute-start.87 = (bf16[512,2,384]{2,0,1:T(8,128)(2,1)}, bf16[512,2,384]{2,0,1:T(8,128)(2,1)}, u32[]{:S(2)}, u32[]{:S(2)}) collective-permute-start(bf16[512,2,384]{2,0,1:T(8,128)(2,1)} %bitcast.220), channel_id=1, source_target_pairs={{0,1},{1,0},{2,3},{3,2},{4,5},{5,4},{6,7},{7,6},{8,9},{9,8},{10,11... | collective-permute-start | bytes 2359304 | tf_op jit(solution)/shard_map/ppermute | solution.py:500
  327.0 93.3 %collective-permute-start.28 = (bf16[512,512]{1,0:T(8,128)(2,1)}, bf16[512,512]{1,0:T(8,128)(2,1)S(1)}, u32[]{:S(2)}, u32[]{:S(2)}) collective-permute-start(bf16[512,512]{1,0:T(8,128)(2,1)} %get-tuple-element.97), channel_id=1, source_target_pairs={{0,1},{1,0},{2,3},{3,2},{4,5},{5,4},{6,7},{7,6},{8,9},{9,8},{10,11... | collective-permute-start | bytes 1572872 | tf_op jit(solution)/shard_map/ppermute | solution.py:500
  327.4 92.9 %collective-permute-start.29 = (bf16[512,512]{1,0:T(8,128)(2,1)}, bf16[512,512]{1,0:T(8,128)(2,1)}, u32[]{:S(2)}, u32[]{:S(2)}) collective-permute-start(bf16[512,512]{1,0:T(8,128)(2,1)} %get-tuple-element.98), channel_id=1, source_target_pairs={{0,1},{1,0},{2,3},{3,2},{4,5},{5,4},{6,7},{7,6},{8,9},{9,8},{10,11... | collective-permute-start | bytes 1572872 | tf_op jit(solution)/shard_map/ppermute | solution.py:500
  410.6 41.6 %collective-permute-start.81 = (bf16[256,2,384]{2,0,1:T(8,128)(2,1)}, bf16[256,2,384]{2,0,1:T(8,128)(2,1)S(1)}, u32[]{:S(2)}, u32[]{:S(2)}) collective-permute-start(bf16[256,2,384]{2,0,1:T(8,128)(2,1)} %get-tuple-element.167), channel_id=1, source_target_pairs={{0,8},{1,9},{2,10},{3,11},{4,12},{5,13},{6,14},{7,15},{16,24},{17,... | collective-permute-start | bytes 1179656 | tf_op jit(solution)/shard_map/ppermute | solution.py:512
  414.9 37.4 %collective-permute-start.83 = (bf16[256,2,384]{2,0,1:T(8,128)(2,1)}, bf16[256,2,384]{2,0,1:T(8,128)(2,1)}, u32[]{:S(2)}, u32[]{:S(2)}) collective-permute-start(bf16[256,2,384]{2,0,1:T(8,128)(2,1)} %get-tuple-element.166), channel_id=1, source_target_pairs={{0,16},{1,17},{2,18},{3,19},{4,20},{5,21},{6,22},{7,23},{8,24},{9,... | collective-permute-start | bytes 1179656 | tf_op jit(solution)/shard_map/ppermute | solution.py:512
  446.4 18.8 %collective-permute-start.52 = (bf16[512,2,384]{2,0,1:T(8,128)(2,1)S(1)}, bf16[512,2,384]{2,0,1:T(8,128)(2,1)S(1)}, u32[]{:S(2)}, u32[]{:S(2)}) collective-permute-start(bf16[512,2,384]{2,0,1:T(8,128)(2,1)S(1)} %bitcast.233), channel_id=1, source_target_pairs={{0,1},{1,0},{2,3},{3,2},{4,5},{5,4},{6,7},{7,6},{8,9},{9,8},{10,11... | collective-permute-start | bytes 2359304 | tf_op jit(solution)/shard_map/ppermute | solution.py:500
  452.2 19.6 %collective-permute-start.59 = (bf16[512,2,384]{2,0,1:T(8,128)(2,1)S(1)}, bf16[512,2,384]{2,0,1:T(8,128)(2,1)S(1)}, u32[]{:S(2)}, u32[]{:S(2)}) collective-permute-start(bf16[512,2,384]{2,0,1:T(8,128)(2,1)S(1)} %bitcast.232), channel_id=1, source_target_pairs={{0,1},{1,0},{2,3},{3,2},{4,5},{5,4},{6,7},{7,6},{8,9},{9,8},{10,11... | collective-permute-start | bytes 2359304 | tf_op jit(solution)/shard_map/ppermute | solution.py:500
  452.4 26.1 %collective-permute-start.66 = (bf16[512,2,384]{2,0,1:T(8,128)(2,1)S(1)}, bf16[512,2,384]{2,0,1:T(8,128)(2,1)S(1)}, u32[]{:S(2)}, u32[]{:S(2)}) collective-permute-start(bf16[512,2,384]{2,0,1:T(8,128)(2,1)S(1)} %bitcast.231), channel_id=1, source_target_pairs={{0,1},{1,0},{2,3},{3,2},{4,5},{5,4},{6,7},{7,6},{8,9},{9,8},{10,11... | collective-permute-start | bytes 2359304 | tf_op jit(solution)/shard_map/ppermute | solution.py:500
  457.0 28.2 %collective-permute-start.73 = (bf16[512,2,384]{2,0,1:T(8,128)(2,1)S(1)}, bf16[512,2,384]{2,0,1:T(8,128)(2,1)S(1)}, u32[]{:S(2)}, u32[]{:S(2)}) collective-permute-start(bf16[512,2,384]{2,0,1:T(8,128)(2,1)S(1)} %bitcast.230), channel_id=1, source_target_pairs={{0,1},{1,0},{2,3},{3,2},{4,5},{5,4},{6,7},{7,6},{8,9},{9,8},{10,11... | collective-permute-start | bytes 2359304 | tf_op jit(solution)/shard_map/ppermute | solution.py:500
  459.6 30.1 %collective-permute-start.84 = (bf16[256,2,384]{2,0,1:T(8,128)(2,1)S(1)}, bf16[256,2,384]{2,0,1:T(8,128)(2,1)S(1)}, u32[]{:S(2)}, u32[]{:S(2)}) collective-permute-start(bf16[256,2,384]{2,0,1:T(8,128)(2,1)S(1)} %get-tuple-element.164), channel_id=1, source_target_pairs={{16,24},{17,25},{18,26},{19,27},{20,28},{21,29},{22,30},{23,31}} | collective-permute-start | bytes 1179656 | tf_op jit(solution)/shard_map/ppermute | solution.py:512
  465.2 26.0 %collective-permute-start.82 = (bf16[256,2,384]{2,0,1:T(8,128)(2,1)S(1)}, bf16[256,2,384]{2,0,1:T(8,128)(2,1)S(1)}, u32[]{:S(2)}, u32[]{:S(2)}) collective-permute-start(bf16[256,2,384]{2,0,1:T(8,128)(2,1)S(1)} %get-tuple-element.165), channel_id=1, source_target_pairs={{8,24},{9,25},{10,26},{11,27},{12,28},{13,29},{14,30},{15,31}} | collective-permute-start | bytes 1179656 | tf_op jit(solution)/shard_map/ppermute | solution.py:512
  471.8 19.6 %collective-permute-start.91 = (bf16[256,2,384]{2,0,1:T(8,128)(2,1)S(1)}, bf16[256,2,384]{2,0,1:T(8,128)(2,1)S(1)}, u32[]{:S(2)}, u32[]{:S(2)}) collective-permute-start(bf16[256,2,384]{2,0,1:T(8,128)(2,1)S(1)} %get-tuple-element.168), channel_id=1, source_target_pairs={{16,24},{17,25},{18,26},{19,27},{20,28},{21,29},{22,30},{23,31}} | collective-permute-start | bytes 1179656 | tf_op jit(solution)/shard_map/ppermute | solution.py:512
  491.2 37.7 %collective-permute-start.38 = (bf16[512,2,384]{2,0,1:T(8,128)(2,1)S(1)}, bf16[512,2,384]{2,0,1:T(8,128)(2,1)S(1)}, u32[]{:S(2)}, u32[]{:S(2)}) collective-permute-start(bf16[512,2,384]{2,0,1:T(8,128)(2,1)S(1)} %bitcast.229), channel_id=1, source_target_pairs={{0,1},{1,0},{2,3},{3,2},{4,5},{5,4},{6,7},{7,6},{8,9},{9,8},{10,11... | collective-permute-start | bytes 2359304 | tf_op jit(solution)/shard_map/ppermute | solution.py:500
  491.4 15.0 %collective-permute-start.60 = (bf16[256,2,384]{2,0,1:T(8,128)(2,1)S(1)}, bf16[256,2,384]{2,0,1:T(8,128)(2,1)S(1)}, u32[]{:S(2)}, u32[]{:S(2)}) collective-permute-start(bf16[256,2,384]{2,0,1:T(8,128)(2,1)S(1)} %get-tuple-element.155), channel_id=1, source_target_pairs={{0,8},{1,9},{2,10},{3,11},{4,12},{5,13},{6,14},{7,15},{16,24},{17,... | collective-permute-start | bytes 1179656 | tf_op jit(solution)/shard_map/ppermute | solution.py:512
  493.0 17.9 %collective-permute-start.62 = (bf16[256,2,384]{2,0,1:T(8,128)(2,1)S(1)}, bf16[256,2,384]{2,0,1:T(8,128)(2,1)S(1)}, u32[]{:S(2)}, u32[]{:S(2)}) collective-permute-start(bf16[256,2,384]{2,0,1:T(8,128)(2,1)S(1)} %get-tuple-element.154), channel_id=1, source_target_pairs={{16,0},{17,1},{18,2},{19,3},{20,4},{21,5},{22,6},{23,7},{24,8},{25... | collective-permute-start | bytes 1179656 | tf_op jit(solution)/shard_map/ppermute | solution.py:512
  510.9 14.5 %collective-permute-start.76 = (bf16[256,2,384]{2,0,1:T(8,128)(2,1)S(1)}, bf16[256,2,384]{2,0,1:T(8,128)(2,1)S(1)}, u32[]{:S(2)}, u32[]{:S(2)}) collective-permute-start(bf16[256,2,384]{2,0,1:T(8,128)(2,1)S(1)} %get-tuple-element.162), channel_id=1, source_target_pairs={{0,16},{1,17},{2,18},{3,19},{4,20},{5,21},{6,22},{7,23},{8,24},{9,... | collective-permute-start | bytes 1179656 | tf_op jit(solution)/shard_map/ppermute | solution.py:512
  512.5 21.2 %collective-permute-start.45 = (bf16[512,2,384]{2,0,1:T(8,128)(2,1)S(1)}, bf16[512,2,384]{2,0,1:T(8,128)(2,1)S(1)}, u32[]{:S(2)}, u32[]{:S(2)}) collective-permute-start(bf16[512,2,384]{2,0,1:T(8,128)(2,1)S(1)} %bitcast.228), channel_id=1, source_target_pairs={{0,1},{1,0},{2,3},{3,2},{4,5},{5,4},{6,7},{7,6},{8,9},{9,8},{10,11... | collective-permute-start | bytes 2359304 | tf_op jit(solution)/shard_map/ppermute | solution.py:500
  512.6 24.8 %collective-permute-start.85 = (bf16[512,1,384]{2,0,1:T(8,128)(2,1)S(1)}, bf16[512,1,384]{2,0,1:T(8,128)(2,1)S(1)}, u32[]{:S(2)}, u32[]{:S(2)}) collective-permute-start(bf16[512,1,384]{2,0,1:T(8,128)(2,1)S(1)} %fusion.3), channel_id=1, source_target_pairs={{24,26},{25,27},{26,24},{27,25},{28,30},{29,31},{30,28},{31,29}} | collective-permute-start | bytes 1179656 | tf_op jit(solution)/shard_map/ppermute | solution.py:512
  518.8 23.2 %collective-permute-start.92 = (bf16[512,1,384]{2,0,1:T(8,128)(2,1)S(1)}, bf16[512,1,384]{2,0,1:T(8,128)(2,1)S(1)}, u32[]{:S(2)}, u32[]{:S(2)}) collective-permute-start(bf16[512,1,384]{2,0,1:T(8,128)(2,1)S(1)} %fusion), channel_id=1, source_target_pairs={{24,26},{25,27},{26,24},{27,25},{28,30},{29,31},{30,28},{31,29}} | collective-permute-start | bytes 1179656 | tf_op jit(solution)/shard_map/ppermute | solution.py:512
  525.4 23.6 %collective-permute-start.56 = (bf16[256,2,384]{2,0,1:T(8,128)(2,1)S(1)}, bf16[256,2,384]{2,0,1:T(8,128)(2,1)S(1)}, u32[]{:S(2)}, u32[]{:S(2)}) collective-permute-start(bf16[256,2,384]{2,0,1:T(8,128)(2,1)S(1)} %get-tuple-element.148), channel_id=1, source_target_pairs={{0,8},{1,9},{2,10},{3,11},{4,12},{5,13},{6,14},{7,15}} | collective-permute-start | bytes 1179656 | tf_op jit(solution)/shard_map/ppermute | solution.py:512
  528.9 23.4 %collective-permute-start.54 = (bf16[256,2,384]{2,0,1:T(8,128)(2,1)S(1)}, bf16[256,2,384]{2,0,1:T(8,128)(2,1)S(1)}, u32[]{:S(2)}, u32[]{:S(2)}) collective-permute-start(bf16[256,2,384]{2,0,1:T(8,128)(2,1)S(1)} %get-tuple-element.149), channel_id=1, source_target_pairs={{24,8},{25,9},{26,10},{27,11},{28,12},{29,13},{30,14},{31,15}} | collective-permute-start | bytes 1179656 | tf_op jit(solution)/shard_map/ppermute | solution.py:512
  533.7 23.3 %collective-permute-start.63 = (bf16[256,2,384]{2,0,1:T(8,128)(2,1)S(1)}, bf16[256,2,384]{2,0,1:T(8,128)(2,1)S(1)}, u32[]{:S(2)}, u32[]{:S(2)}) collective-permute-start(bf16[256,2,384]{2,0,1:T(8,128)(2,1)S(1)} %get-tuple-element.152), channel_id=1, source_target_pairs={{0,8},{1,9},{2,10},{3,11},{4,12},{5,13},{6,14},{7,15}} | collective-permute-start | bytes 1179656 | tf_op jit(solution)/shard_map/ppermute | solution.py:512
  537.4 27.7 %collective-permute-start.61 = (bf16[256,2,384]{2,0,1:T(8,128)(2,1)S(1)}, bf16[256,2,384]{2,0,1:T(8,128)(2,1)S(1)}, u32[]{:S(2)}, u32[]{:S(2)}) collective-permute-start(bf16[256,2,384]{2,0,1:T(8,128)(2,1)S(1)} %get-tuple-element.153), channel_id=1, source_target_pairs={{24,8},{25,9},{26,10},{27,11},{28,12},{29,13},{30,14},{31,15}} | collective-permute-start | bytes 1179656 | tf_op jit(solution)/shard_map/ppermute | solution.py:512
  542.0 24.4 %collective-permute-start.70 = (bf16[256,2,384]{2,0,1:T(8,128)(2,1)S(1)}, bf16[256,2,384]{2,0,1:T(8,128)(2,1)S(1)}, u32[]{:S(2)}, u32[]{:S(2)}) collective-permute-start(bf16[256,2,384]{2,0,1:T(8,128)(2,1)S(1)} %get-tuple-element.156), channel_id=1, source_target_pairs={{24,16},{25,17},{26,18},{27,19},{28,20},{29,21},{30,22},{31,23}} | collective-permute-start | bytes 1179656 | tf_op jit(solution)/shard_map/ppermute | solution.py:512
  549.0 19.1 %collective-permute-start.68 = (bf16[256,2,384]{2,0,1:T(8,128)(2,1)S(1)}, bf16[256,2,384]{2,0,1:T(8,128)(2,1)S(1)}, u32[]{:S(2)}, u32[]{:S(2)}) collective-permute-start(bf16[256,2,384]{2,0,1:T(8,128)(2,1)S(1)} %get-tuple-element.157), channel_id=1, source_target_pairs={{0,16},{1,17},{2,18},{3,19},{4,20},{5,21},{6,22},{7,23}} | collective-permute-start | bytes 1179656 | tf_op jit(solution)/shard_map/ppermute | solution.py:512
  552.4 17.1 %collective-permute-start.77 = (bf16[256,2,384]{2,0,1:T(8,128)(2,1)S(1)}, bf16[256,2,384]{2,0,1:T(8,128)(2,1)S(1)}, u32[]{:S(2)}, u32[]{:S(2)}) collective-permute-start(bf16[256,2,384]{2,0,1:T(8,128)(2,1)S(1)} %get-tuple-element.160), channel_id=1, source_target_pairs={{24,16},{25,17},{26,18},{27,19},{28,20},{29,21},{30,22},{31,23}} | collective-permute-start | bytes 1179656 | tf_op jit(solution)/shard_map/ppermute | solution.py:512
  557.0 16.6 %collective-permute-start.75 = (bf16[256,2,384]{2,0,1:T(8,128)(2,1)S(1)}, bf16[256,2,384]{2,0,1:T(8,128)(2,1)S(1)}, u32[]{:S(2)}, u32[]{:S(2)}) collective-permute-start(bf16[256,2,384]{2,0,1:T(8,128)(2,1)S(1)} %get-tuple-element.161), channel_id=1, source_target_pairs={{0,16},{1,17},{2,18},{3,19},{4,20},{5,21},{6,22},{7,23}} | collective-permute-start | bytes 1179656 | tf_op jit(solution)/shard_map/ppermute | solution.py:512
  565.1 15.2 %collective-permute-start.39 = (bf16[256,2,384]{2,0,1:T(8,128)(2,1)S(1)}, bf16[256,2,384]{2,0,1:T(8,128)(2,1)S(1)}, u32[]{:S(2)}, u32[]{:S(2)}) collective-permute-start(bf16[256,2,384]{2,0,1:T(8,128)(2,1)S(1)} %get-tuple-element.143), channel_id=1, source_target_pairs={{8,0},{9,1},{10,2},{11,3},{12,4},{13,5},{14,6},{15,7},{24,16},{25,... | collective-permute-start | bytes 1179656 | tf_op jit(solution)/shard_map/ppermute | solution.py:512
  566.4 20.3 %collective-permute-start.41 = (bf16[256,2,384]{2,0,1:T(8,128)(2,1)S(1)}, bf16[256,2,384]{2,0,1:T(8,128)(2,1)S(1)}, u32[]{:S(2)}, u32[]{:S(2)}) collective-permute-start(bf16[256,2,384]{2,0,1:T(8,128)(2,1)S(1)} %get-tuple-element.142), channel_id=1, source_target_pairs={{16,0},{17,1},{18,2},{19,3},{20,4},{21,5},{22,6},{23,7},{24,8},{25... | collective-permute-start | bytes 1179656 | tf_op jit(solution)/shard_map/ppermute | solution.py:512
  568.1 25.1 %collective-permute-start.46 = (bf16[256,2,384]{2,0,1:T(8,128)(2,1)S(1)}, bf16[256,2,384]{2,0,1:T(8,128)(2,1)S(1)}, u32[]{:S(2)}, u32[]{:S(2)}) collective-permute-start(bf16[256,2,384]{2,0,1:T(8,128)(2,1)S(1)} %get-tuple-element.147), channel_id=1, source_target_pairs={{8,0},{9,1},{10,2},{11,3},{12,4},{13,5},{14,6},{15,7},{24,16},{25,... | collective-permute-start | bytes 1179656 | tf_op jit(solution)/shard_map/ppermute | solution.py:512
  569.5 30.1 %collective-permute-start.48 = (bf16[256,2,384]{2,0,1:T(8,128)(2,1)S(1)}, bf16[256,2,384]{2,0,1:T(8,128)(2,1)S(1)}, u32[]{:S(2)}, u32[]{:S(2)}) collective-permute-start(bf16[256,2,384]{2,0,1:T(8,128)(2,1)S(1)} %get-tuple-element.146), channel_id=1, source_target_pairs={{16,0},{17,1},{18,2},{19,3},{20,4},{21,5},{22,6},{23,7},{24,8},{25... | collective-permute-start | bytes 1179656 | tf_op jit(solution)/shard_map/ppermute | solution.py:512
  573.6 32.6 %collective-permute-start.57 = (bf16[512,1,384]{2,0,1:T(8,128)(2,1)S(1)}, bf16[512,1,384]{2,0,1:T(8,128)(2,1)S(1)}, u32[]{:S(2)}, u32[]{:S(2)}) collective-permute-start(bf16[512,1,384]{2,0,1:T(8,128)(2,1)S(1)} %fusion.15), channel_id=1, source_target_pairs={{8,10},{9,11},{10,8},{11,9},{12,14},{13,15},{14,12},{15,13}} | collective-permute-start | bytes 1179656 | tf_op jit(solution)/shard_map/ppermute | solution.py:512
  580.3 32.3 %collective-permute-start.64 = (bf16[512,1,384]{2,0,1:T(8,128)(2,1)S(1)}, bf16[512,1,384]{2,0,1:T(8,128)(2,1)S(1)}, u32[]{:S(2)}, u32[]{:S(2)}) collective-permute-start(bf16[512,1,384]{2,0,1:T(8,128)(2,1)S(1)} %fusion.12), channel_id=1, source_target_pairs={{8,10},{9,11},{10,8},{11,9},{12,14},{13,15},{14,12},{15,13}} | collective-permute-start | bytes 1179656 | tf_op jit(solution)/shard_map/ppermute | solution.py:512
  586.7 41.7 %collective-permute-start.71 = (bf16[512,1,384]{2,0,1:T(8,128)(2,1)S(1)}, bf16[512,1,384]{2,0,1:T(8,128)(2,1)S(1)}, u32[]{:S(2)}, u32[]{:S(2)}) collective-permute-start(bf16[512,1,384]{2,0,1:T(8,128)(2,1)S(1)} %fusion.9), channel_id=1, source_target_pairs={{16,18},{17,19},{18,16},{19,17},{20,22},{21,23},{22,20},{23,21}} | collective-permute-start | bytes 1179656 | tf_op jit(solution)/shard_map/ppermute | solution.py:512
  593.2 25.9 %collective-permute-start.42 = (bf16[256,2,384]{2,0,1:T(8,128)(2,1)S(1)}, bf16[256,2,384]{2,0,1:T(8,128)(2,1)S(1)}, u32[]{:S(2)}, u32[]{:S(2)}) collective-permute-start(bf16[256,2,384]{2,0,1:T(8,128)(2,1)S(1)} %get-tuple-element.140), channel_id=1, source_target_pairs={{8,0},{9,1},{10,2},{11,3},{12,4},{13,5},{14,6},{15,7}} | collective-permute-start | bytes 1179656 | tf_op jit(solution)/shard_map/ppermute | solution.py:512
  599.6 20.4 %collective-permute-start.40 = (bf16[256,2,384]{2,0,1:T(8,128)(2,1)S(1)}, bf16[256,2,384]{2,0,1:T(8,128)(2,1)S(1)}, u32[]{:S(2)}, u32[]{:S(2)}) collective-permute-start(bf16[256,2,384]{2,0,1:T(8,128)(2,1)S(1)} %get-tuple-element.141), channel_id=1, source_target_pairs={{16,0},{17,1},{18,2},{19,3},{20,4},{21,5},{22,6},{23,7}} | collective-permute-start | bytes 1179656 | tf_op jit(solution)/shard_map/ppermute | solution.py:512
  606.1 24.5 %collective-permute-start.49 = (bf16[256,2,384]{2,0,1:T(8,128)(2,1)S(1)}, bf16[256,2,384]{2,0,1:T(8,128)(2,1)S(1)}, u32[]{:S(2)}, u32[]{:S(2)}) collective-permute-start(bf16[256,2,384]{2,0,1:T(8,128)(2,1)S(1)} %get-tuple-element.144), channel_id=1, source_target_pairs={{8,0},{9,1},{10,2},{11,3},{12,4},{13,5},{14,6},{15,7}} | collective-permute-start | bytes 1179656 | tf_op jit(solution)/shard_map/ppermute | solution.py:512
  612.7 18.7 %collective-permute-start.47 = (bf16[256,2,384]{2,0,1:T(8,128)(2,1)S(1)}, bf16[256,2,384]{2,0,1:T(8,128)(2,1)S(1)}, u32[]{:S(2)}, u32[]{:S(2)}) collective-permute-start(bf16[256,2,384]{2,0,1:T(8,128)(2,1)S(1)} %get-tuple-element.145), channel_id=1, source_target_pairs={{16,0},{17,1},{18,2},{19,3},{20,4},{21,5},{22,6},{23,7}} | collective-permute-start | bytes 1179656 | tf_op jit(solution)/shard_map/ppermute | solution.py:512
  619.2 31.5 %collective-permute-start.86 = (bf16[512,1,384]{2,0,1:T(8,128)(2,1)S(1)}, bf16[512,1,384]{2,0,1:T(8,128)(2,1)S(1)}, u32[]{:S(2)}, u32[]{:S(2)}) collective-permute-start(bf16[512,1,384]{2,0,1:T(8,128)(2,1)S(1)} %fusion.5), channel_id=1, source_target_pairs={{24,28},{25,29},{26,30},{27,31}} | collective-permute-start | bytes 1179656 | tf_op jit(solution)/shard_map/ppermute | solution.py:512
  630.6 20.8 %collective-permute-start.93 = (bf16[512,1,384]{2,0,1:T(8,128)(2,1)S(1)}, bf16[512,1,384]{2,0,1:T(8,128)(2,1)S(1)}, u32[]{:S(2)}, u32[]{:S(2)}) collective-permute-start(bf16[512,1,384]{2,0,1:T(8,128)(2,1)S(1)} %fusion.2), channel_id=1, source_target_pairs={{28,24},{29,25},{30,26},{31,27}} | collective-permute-start | bytes 1179656 | tf_op jit(solution)/shard_map/ppermute | solution.py:512
  631.4 21.3 %collective-permute-start.58 = (bf16[512,1,384]{2,0,1:T(8,128)(2,1)S(1)}, bf16[512,1,384]{2,0,1:T(8,128)(2,1)S(1)}, u32[]{:S(2)}, u32[]{:S(2)}) collective-permute-start(bf16[512,1,384]{2,0,1:T(8,128)(2,1)S(1)} %fusion.17), channel_id=1, source_target_pairs={{8,12},{9,13},{10,14},{11,15}} | collective-permute-start | bytes 1179656 | tf_op jit(solution)/shard_map/ppermute | solution.py:512
  632.3 17.6 %collective-permute-start.50 = (bf16[512,1,384]{2,0,1:T(8,128)(2,1)S(1)}, bf16[512,1,384]{2,0,1:T(8,128)(2,1)S(1)}, u32[]{:S(2)}, u32[]{:S(2)}) collective-permute-start(bf16[512,1,384]{2,0,1:T(8,128)(2,1)S(1)} %fusion.18), channel_id=1, source_target_pairs={{0,2},{1,3},{2,0},{3,1},{4,6},{5,7},{6,4},{7,5}} | collective-permute-start | bytes 1179656 | tf_op jit(solution)/shard_map/ppermute | solution.py:512
  642.3 18.0 %collective-permute-start.65 = (bf16[512,1,384]{2,0,1:T(8,128)(2,1)S(1)}, bf16[512,1,384]{2,0,1:T(8,128)(2,1)S(1)}, u32[]{:S(2)}, u32[]{:S(2)}) collective-permute-start(bf16[512,1,384]{2,0,1:T(8,128)(2,1)S(1)} %fusion.14), channel_id=1, source_target_pairs={{12,8},{13,9},{14,10},{15,11}} | collective-permute-start | bytes 1179656 | tf_op jit(solution)/shard_map/ppermute | solution.py:512
  652.7 21.5 %collective-permute-start.51 = (bf16[512,1,384]{2,0,1:T(8,128)(2,1)S(1)}, bf16[512,1,384]{2,0,1:T(8,128)(2,1)S(1)}, u32[]{:S(2)}, u32[]{:S(2)}) collective-permute-start(bf16[512,1,384]{2,0,1:T(8,128)(2,1)S(1)} %fusion.20), channel_id=1, source_target_pairs={{0,4},{1,5},{2,6},{3,7}} | collective-permute-start | bytes 1179656 | tf_op jit(solution)/shard_map/ppermute | solution.py:512
  (114 other events, 743.9 us)

commit v2 on v1

v2 whole, which is shorter than its diff:
```python
import functools

import jax
import jax.numpy as jnp
from jax import lax
from jax.experimental import pallas as pl
from jax.experimental.pallas import tpu as pltpu
from jax.sharding import PartitionSpec as P

D = 512
HEADS = 8
HEAD = 64
PACK = 1024
HALF = PACK // 2
PAIRS = HEADS // 2
LANES = 2 * HEAD
SECTIONS = 4
FAR = 1e30
SCALE = HEAD ** (-0.5)
BF = jnp.bfloat16
F32 = jnp.float32
NT = (((1,), (1,)), ((), ()))
TN = (((0,), (0,)), ((), ()))


def mm(left, right):
    return jnp.dot(left, right, preferred_element_type=F32)


def mm_nt(left, right):
    return lax.dot_general(left, right, NT, preferred_element_type=F32)


def mm_tn(left, right):
    return lax.dot_general(left, right, TN, preferred_element_type=F32)


def params():
    return pltpu.CompilerParams(
        dimension_semantics=("arbitrary",), vmem_limit_bytes=48 * 1024 * 1024
    )


def shaped(rows, cols, dtype):
    return jax.ShapeDtypeStruct((rows, cols), dtype)


def whole(rows, cols):
    return pl.BlockSpec((rows, cols), lambda i: (0, 0))


def cost(flops, moved, transcendentals=0):
    return pl.CostEstimate(
        flops=int(flops), bytes_accessed=int(moved), transcendentals=int(transcendentals)
    )


def norm_parts(summed):
    average = jnp.mean(summed, axis=-1, keepdims=True)
    centered = summed - average
    spread = jnp.mean(centered * centered, axis=-1, keepdims=True)
    inverse = lax.rsqrt(spread + 1e-05)
    return centered * inverse, inverse


def norm_back(summed, gain, upstream):
    normal, inverse = norm_parts(summed)
    scaled = upstream * gain
    mean_one = jnp.mean(scaled, axis=-1, keepdims=True)
    mean_two = jnp.mean(scaled * normal, axis=-1, keepdims=True)
    grad = (scaled - mean_one - normal * mean_two) * inverse
    gain_grad = jnp.sum(upstream * normal, axis=0, keepdims=True)
    shift_grad = jnp.sum(upstream, axis=0, keepdims=True)
    return grad, gain_grad, shift_grad


def head_mask(which):
    lane = lax.broadcasted_iota(jnp.int32, (1, LANES), 1)
    return (lane // HEAD) == which


def three_way(column):
    high = column.astype(BF)
    rest = column - high.astype(F32)
    middle = rest.astype(BF)
    low = (rest - middle.astype(F32)).astype(BF)
    return high, middle, low


def project_kernel(x_ref, w_ref, q_ref, kv_ref):
    x = x_ref[...]
    q_ref[...] = mm(x, w_ref[0, :, :D]).astype(BF)
    keys = mm(x, w_ref[0, :, D : 2 * D]).astype(BF)
    values = mm(x, w_ref[0, :, 2 * D :]).astype(BF)
    for pair in range(PAIRS):
        lanes = slice(pair * LANES, (pair + 1) * LANES)
        kv_ref[pair, :, :LANES] = keys[:, lanes]
        kv_ref[pair, :, LANES:] = values[:, lanes]


def project(stream, near, layer):
    return pl.pallas_call(
        project_kernel,
        grid=(1,),
        in_specs=[
            whole(HALF, D),
            pl.BlockSpec((1, D, 3 * D), lambda i: (layer, 0, 0)),
        ],
        out_specs=[whole(HALF, D), pl.BlockSpec((PAIRS, HALF, 2 * LANES), lambda i: (0, 0, 0))],
        out_shape=[
            shaped(HALF, D, BF), jax.ShapeDtypeStruct((PAIRS, HALF, 2 * LANES), BF),
        ],
        compiler_params=params(),
        cost_estimate=cost(2 * HALF * D * 3 * D, 4e6),
        name="project",
    )(stream, near)


def attend_kernel(
    q_ref, own_ref, far_ref, qs_ref, kso_ref, ksx_ref, w_ref, x_ref, fsum_ref,
    norm_ref, ctx_ref, lse_ref, next_ref, sum_ref, fnew_ref, ctx_acc, lse_acc,
):
    pair = pl.program_id(0)
    q = q_ref[...] * jnp.asarray(SCALE, BF)
    keys_own = jnp.concatenate([own_ref[0, :, :LANES], kso_ref[...]], axis=1)
    keys_other = jnp.concatenate([far_ref[0, :, :LANES], ksx_ref[...]], axis=1)
    values_own, values_other = own_ref[0, :, LANES:], far_ref[0, :, LANES:]
    ones = jnp.ones((HALF, LANES), BF)
    none = jnp.zeros((), BF)
    lane = lax.broadcasted_iota(jnp.int32, (1, LANES), 1)
    context = jnp.zeros((HALF, LANES), F32)
    logs = jnp.where(pair == 0, jnp.zeros((HALF, LANES), F32), lse_acc[...])
    for which in range(2):
        mask = head_mask(which)
        query = jnp.concatenate([jnp.where(mask, q, none), qs_ref[...]], axis=1)
        score_own = mm_nt(query, keys_own)
        score_other = mm_nt(query, keys_other)
        peak = jnp.maximum(
            jnp.max(score_own, axis=1, keepdims=True), jnp.max(score_other, axis=1, keepdims=True)
        )
        own = jnp.exp(score_own - peak).astype(BF)
        other = jnp.exp(score_other - peak).astype(BF)
        total = mm(own, jnp.concatenate([jnp.where(mask, values_own, none), ones], axis=1)) + mm(
            other, jnp.concatenate([jnp.where(mask, values_other, none), ones], axis=1)
        )
        row_total = total[:, LANES:]
        context = context + total[:, :LANES] / row_total
        logs = jnp.where(lane == 2 * pair + which, peak + jnp.log(row_total), logs)
    lse_acc[...] = logs
    ctx_acc[pair] = context.astype(BF)
    ctx_ref[...] = context.astype(BF)

    @pl.when(pair == PAIRS - 1)
    def _():
        lse_ref[...] = lse_acc[...]
        full = jnp.concatenate([ctx_acc[k] for k in range(PAIRS)], axis=1)
        branch = mm(full, w_ref[0])
        summed = x_ref[...].astype(F32) + branch
        normal, _ = norm_parts(summed)
        moved = normal * norm_ref[0:1, :] + norm_ref[1:2, :]
        next_ref[...] = moved.astype(BF)
        sum_ref[...] = summed
        fnew_ref[...] = fsum_ref[...] + branch


def column():
    return pl.BlockSpec((HALF, LANES), lambda i: (0, i))


def pair_block():
    return pl.BlockSpec((1, HALF, 2 * LANES), lambda i: (i, 0, 0))


def attend(stream, queries, own_kv, far_kv, segs, near, layer, norms, branch_sum):
    qseg, kseg_own, kseg_other = segs
    return pl.pallas_call(
        attend_kernel,
        grid=(PAIRS,),
        in_specs=[
            column(), pair_block(), pair_block(),
            whole(HALF, LANES), whole(HALF, LANES), whole(HALF, LANES),
            pl.BlockSpec((1, D, D), lambda i: (layer, 0, 3)),
            whole(HALF, D), whole(HALF, D), whole(2, D),
        ],
        out_specs=[
            column(), whole(HALF, LANES), whole(HALF, D), whole(HALF, D), whole(HALF, D),
        ],
        out_shape=[
            shaped(HALF, D, BF), shaped(HALF, LANES, F32), shaped(HALF, D, BF),
            shaped(HALF, D, F32), shaped(HALF, D, F32),
        ],
        scratch_shapes=[pltpu.VMEM((PAIRS, HALF, LANES), BF), pltpu.VMEM((HALF, LANES), F32)],
        compiler_params=params(),
        cost_estimate=cost(8e9, 8e6, 4e6),
        name="attend",
    )(
        queries, own_kv, far_kv, qseg, kseg_own, kseg_other, near, stream, branch_sum, norms,
    )


def gelu_parts(v):
    root = 0.7978845608028654
    squared = v * v
    inner = root * (v + 0.044715 * v * squared)
    t = jnp.tanh(inner)
    hidden = 0.5 * v * (1.0 + t)
    slope = 0.5 * (1.0 + t) + 0.5 * v * (1.0 - t * t) * (root * (1.0 + 3 * 0.044715 * squared))
    return hidden, slope


def feed_specs(layer):
    return [
        pl.BlockSpec((1, D, D), lambda i: (layer - 1, 0, i)),
        pl.BlockSpec((1, D, D), lambda i: (layer, 0, 2 + i)),
        pl.BlockSpec((1, D, D), lambda i: (layer, 0, i)),
        pl.BlockSpec((1, D, D), lambda i: (layer, 0, i)),
    ]


def feed_kernel(
    x_ref, in_a_ref, out_a_ref, in_b_ref, out_b_ref, fsum_ref, norm_ref,
    next_ref, sum_ref, fnew_ref, acc_ref,
):
    step = pl.program_id(0)
    x = x_ref[...]
    hidden_a = gelu_parts(mm(x, in_a_ref[0]))[0].astype(BF)
    hidden_b = gelu_parts(mm(x, in_b_ref[0]))[0].astype(BF)
    part = mm_nt(hidden_a, out_a_ref[0]) + mm_nt(hidden_b, out_b_ref[0])

    @pl.when(step == 0)
    def _():
        acc_ref[...] = part

    @pl.when(step == 1)
    def _():
        branch = acc_ref[...] + part
        summed = x_ref[...].astype(F32) + branch
        normal, _ = norm_parts(summed)
        moved = normal * norm_ref[0:1, :] + norm_ref[1:2, :]
        next_ref[...] = moved.astype(next_ref.dtype)
        sum_ref[...] = summed
        fnew_ref[...] = fsum_ref[...] + branch


def feed(stream, near, late, layer, norms, branch_sum, out_type):
    return pl.pallas_call(
        feed_kernel,
        grid=(2,),
        in_specs=[whole(HALF, D), *feed_specs(layer), whole(HALF, D), whole(2, D)],
        out_specs=[whole(HALF, D), whole(HALF, D), whole(HALF, D)],
        out_shape=[shaped(HALF, D, out_type), shaped(HALF, D, F32), shaped(HALF, D, F32)],
        scratch_shapes=[pltpu.VMEM((HALF, D), F32)],
        compiler_params=params(),
        cost_estimate=cost(4 * HALF * D * 4 * D, 8e6, HALF * 4 * D),
        name="feed",
    )(stream, late, near, near, late, branch_sum, norms)


def finish_kernel(
    x_ref, fsum_ref, y_ref, cot_ref, live_ref, norm_ref, out_ref, low_ref, c_ref, dy_ref, grad_ref
):
    summed = y_ref[...].astype(F32) + fsum_ref[...]
    normal, _ = norm_parts(summed)
    gain = norm_ref[0:1, :]
    out_ref[...] = (x_ref[...] + normal * gain + norm_ref[1:2, :]).astype(BF)
    cot = cot_ref[...].astype(F32) * live_ref[:, 0:1]
    c_ref[...] = cot
    grad, gain_grad, shift_grad = norm_back(summed, gain, cot)
    dy_ref[...] = grad
    low_ref[...] = grad.astype(BF)
    grad_ref[0:1, :] = gain_grad
    grad_ref[1:2, :] = shift_grad


def finish(last, branch_sum, accum, cot, live, norms):
    return pl.pallas_call(
        finish_kernel,
        grid=(1,),
        in_specs=[
            whole(HALF, D), whole(HALF, D), whole(HALF, D), whole(HALF, D), whole(HALF, LANES),
            whole(2, D),
        ],
        out_specs=[whole(HALF, D)] * 4 + [whole(2, D)],
        out_shape=[
            shaped(HALF, D, BF), shaped(HALF, D, BF), shaped(HALF, D, F32), shaped(HALF, D, F32),
            shaped(2, D, F32),
        ],
        compiler_params=params(),
        cost_estimate=cost(1e7, 6e6),
        name="finish",
    )(last, branch_sum, accum, cot, live, norms)


def feed_back_kernel(
    x_ref, sum_ref, up_ref, dy_ref, in_a_ref, out_a_ref, in_b_ref, out_b_ref, norm_ref,
    dx_ref, odd_ref, even_ref, grad_ref, acc_ref, df_ref,
):
    step = pl.program_id(0)

    @pl.when(step == 0)
    def _():
        grad, gain_grad, shift_grad = norm_back(
            sum_ref[...], norm_ref[0:1, :], up_ref[...].astype(F32)
        )
        grad_ref[0:1, :] = gain_grad
        grad_ref[1:2, :] = shift_grad
        acc_ref[...] = grad
        df_ref[...] = (grad + dy_ref[...]).astype(BF)

    x = x_ref[...]
    df = df_ref[...]

    def chunk(inner, outer):
        hidden, slope = gelu_parts(mm(x, inner))
        outer_grad = mm_tn(hidden.astype(BF), df).astype(BF)
        preact_grad = (mm(df, outer) * slope).astype(BF)
        inner_grad = mm_tn(preact_grad, x).astype(BF)
        return inner_grad, outer_grad, mm_nt(preact_grad, inner)

    inner_grad, outer_grad, back_a = chunk(in_a_ref[0], out_a_ref[0])
    even_ref[...] = inner_grad
    odd_ref[1, 0] = outer_grad
    inner_grad, outer_grad, back_b = chunk(in_b_ref[0], out_b_ref[0])
    odd_ref[0, 0] = inner_grad
    odd_ref[2, 0] = outer_grad
    total = acc_ref[...] + (back_a + back_b)
    acc_ref[...] = total

    @pl.when(step == 1)
    def _():
        dx_ref[...] = total.astype(BF)


def feed_back(stream, summed, upstream, dy, near, late, layer, norms):
    dx, odd, even, grads = pl.pallas_call(
        feed_back_kernel,
        grid=(2,),
        in_specs=[
            whole(HALF, D), whole(HALF, D), whole(HALF, D), whole(HALF, D),
            *feed_specs(layer), whole(2, D),
        ],
        out_specs=[
            whole(HALF, D),
            pl.BlockSpec((3, 1, D, D), lambda i: (0, i, 0, 0)),
            pl.BlockSpec((D, D), lambda i: (i, 0)),
            whole(2, D),
        ],
        out_shape=[
            shaped(HALF, D, BF), jax.ShapeDtypeStruct((3, 2, D, D), BF), shaped(2 * D, D, BF),
            shaped(2, D, F32),
        ],
        scratch_shapes=[pltpu.VMEM((HALF, D), F32), pltpu.VMEM((HALF, D), BF)],
        compiler_params=params(),
        cost_estimate=cost(10 * HALF * D * 4 * D, 16e6, HALF * 4 * D),
        name="feed_back",
    )(stream, summed, upstream, dy, late, near, near, late, norms)
    return dx, odd.reshape(6 * D, D), even, grads


def outward_back_kernel(
    sum_ref, up_ref, dy_ref, ctx_ref, w_ref, norm_ref, dz_ref, dctx_ref, dwo_ref, delta_ref,
    grad_ref,
):
    grad, gain_grad, shift_grad = norm_back(sum_ref[...], norm_ref[0:1, :], up_ref[...].astype(F32))
    grad_ref[0:1, :] = gain_grad
    grad_ref[1:2, :] = shift_grad
    dz_ref[...] = grad
    df = (grad + dy_ref[...]).astype(BF)
    context = ctx_ref[...]
    dwo_ref[...] = mm_tn(df, context).astype(BF)
    context_grad = mm_nt(df, w_ref[0]).astype(BF)
    dctx_ref[...] = context_grad
    product = context.astype(F32) * context_grad.astype(F32)
    lane = lax.broadcasted_iota(jnp.int32, (1, LANES), 1)
    delta = jnp.zeros((HALF, LANES), F32)
    for head in range(HEADS):
        part = product[:, (head // 2) * LANES : (head // 2 + 1) * LANES]
        inner = jnp.sum(jnp.where(head_mask(head % 2), part, 0.0), axis=1, keepdims=True)
        delta = jnp.where(lane == head, inner, delta)
    delta_ref[...] = delta


def outward_back(summed, upstream, dy, context, near, layer, norms):
    return pl.pallas_call(
        outward_back_kernel,
        grid=(1,),
        in_specs=[
            whole(HALF, D), whole(HALF, D), whole(HALF, D), whole(HALF, D),
            pl.BlockSpec((1, D, D), lambda i: (layer, 0, 3)), whole(2, D),
        ],
        out_specs=[
            whole(HALF, D), whole(HALF, D), whole(D, D), whole(HALF, LANES), whole(2, D),
        ],
        out_shape=[
            shaped(HALF, D, F32), shaped(HALF, D, BF), shaped(D, D, BF), shaped(HALF, LANES, F32),
            shaped(2, D, F32),
        ],
        compiler_params=params(),
        cost_estimate=cost(4 * HALF * D * D, 6e6),
        name="outward_back",
    )(summed, upstream, dy, context, near, norms)


def scores_back_kernel(
    q_ref, kv_ref, dctx_ref, qs_ref, ks_ref, lse_ref, delta_ref, before_ref, dq_ref, dkv_ref
):
    pair = pl.program_id(0)
    none = jnp.zeros((), BF)
    lane = lax.broadcasted_iota(jnp.int32, (1, LANES), 1)
    q = q_ref[...] * jnp.asarray(SCALE, BF)
    k = kv_ref[0, :, :LANES]
    k_scaled = k * jnp.asarray(SCALE, BF)
    dctx = dctx_ref[...]
    extra = jnp.where((lane >= LANES - 3), jnp.ones((), BF), none)
    keys = jnp.concatenate([k, ks_ref[...] + extra], axis=1)
    values = jnp.concatenate(
        [kv_ref[0, :, LANES:], jnp.broadcast_to(extra, (HALF, LANES))], axis=1
    )
    dq = before_ref[...]
    dk = jnp.zeros((HALF, LANES), F32)
    dv = jnp.zeros((HALF, LANES), F32)
    for which in range(2):
        mask = head_mask(which)
        here = lane == 2 * pair + which

        def lanes_of(table, base):
            column = -jnp.sum(jnp.where(here, table, 0.0), axis=1, keepdims=True)
            high, middle, low = three_way(column)
            base = jnp.where(lane == LANES - 3, high, base)
            base = jnp.where(lane == LANES - 2, middle, base)
            return jnp.where(lane == LANES - 1, low, base)

        query_part = jnp.where(mask, q, none)
        dctx_part = jnp.where(mask, dctx, none)
        query = jnp.concatenate([query_part, lanes_of(lse_ref[...], qs_ref[...])], axis=1)
        dcontext = jnp.concatenate(
            [dctx_part, lanes_of(delta_ref[...], jnp.zeros((HALF, LANES), BF))], axis=1
        )
        probability = jnp.exp(mm_nt(keys, query))
        score_grad = (probability * mm_nt(values, dcontext)).astype(BF)
        dv = dv + mm(probability.astype(BF), dctx_part)
        dk = dk + mm(score_grad, query_part)
        dq = dq + mm_tn(score_grad, jnp.where(mask, k_scaled, none))
    dq_ref[...] = dq
    dkv_ref[0, :, :LANES] = dk.astype(dkv_ref.dtype)
    dkv_ref[0, :, LANES:] = dv.astype(dkv_ref.dtype)


def scores_back(queries, kv, dctx, qseg, kseg, lse, delta, before, out_type):
    return pl.pallas_call(
        scores_back_kernel,
        grid=(PAIRS,),
        in_specs=[
            column(), pair_block(), column(),
            whole(HALF, LANES), whole(HALF, LANES), whole(HALF, LANES), whole(HALF, LANES),
            column(),
        ],
        out_specs=[column(), pair_block()],
        out_shape=[
            shaped(HALF, D, F32), jax.ShapeDtypeStruct((PAIRS, HALF, 2 * LANES), out_type),
        ],
        compiler_params=params(),
        cost_estimate=cost(8e9, 8e6, 2e6),
        name="scores_back",
    )(queries, kv, dctx, qseg, kseg, lse, delta, before)


def project_back_kernel(
    x_ref, dq_ref, dkv_ref, far_ref, dz_ref, w_ref, dx_ref, dw_ref
):
    x = x_ref[...]
    parts = [(dkv_ref[k] + far_ref[k].astype(F32)).astype(BF) for k in range(PAIRS)]
    dk = jnp.concatenate([part[:, :LANES] for part in parts], axis=1)
    dv = jnp.concatenate([part[:, LANES:] for part in parts], axis=1)
    total = dz_ref[...]
    for place, grad in enumerate((dq_ref[...].astype(BF), dk, dv)):
        dw_ref[place * D : (place + 1) * D] = mm_tn(grad, x).astype(BF)
        total = total + mm_nt(grad, w_ref[0, :, place * D : (place + 1) * D])
    dx_ref[...] = total.astype(BF)


def project_back(stream, dq, dkv, far, dz, near, layer):
    pairs = pl.BlockSpec((PAIRS, HALF, 2 * LANES), lambda i: (0, 0, 0))
    return pl.pallas_call(
        project_back_kernel,
        grid=(1,),
        in_specs=[
            whole(HALF, D), whole(HALF, D), pairs, pairs, whole(HALF, D),
            pl.BlockSpec((1, D, 3 * D), lambda i: (layer, 0, 0)),
        ],
        out_specs=[whole(HALF, D), whole(3 * D, D)],
        out_shape=[shaped(HALF, D, BF), shaped(3 * D, D, BF)],
        compiler_params=params(),
        cost_estimate=cost(4 * HALF * D * 3 * D, 10e6),
        name="project_back",
    )(stream, dq, dkv, far, dz, near)


class Places:
    def __init__(self):
        self.ndp = lax.axis_size("dp")
        self.section = lax.axis_index("section")
        self.dp = lax.axis_index("dp")
        self.core = self.dp % 2

    def swap_dp(self, block, step):
        return lax.ppermute(block, "dp", [(i, i ^ step) for i in range(self.ndp)])

    def swap_core(self, block):
        return self.swap_dp(block, 1)

    def swap_section(self, block, step):
        return lax.ppermute(block, "section", [(i, i ^ step) for i in range(SECTIONS)])

    def send(self, block, route):
        pairs = []
        for s in range(SECTIONS):
            for d in range(self.ndp):
                to = route(s, d)
                pairs.append((s * self.ndp + d, to[0] * self.ndp + to[1]))
        return lax.ppermute(block, ("section", "dp"), pairs)


def pick(stack, index):
    return lax.dynamic_index_in_dim(stack, index, 0, keepdims=False)


def after(value, *earlier):
    return lax.optimization_barrier((value, *earlier))[0]


def tokens_in(places, block):
    several = block.shape[0]
    width = D // SECTIONS
    pieces = jnp.swapaxes(block.reshape(several, 4, HALF, width), 0, 1)
    got = []
    for turn in range(4):

        def route(s, d, turn=turn):
            piece = s ^ turn
            return 2 * (d % 2) + piece // 2, d - d % 2 + piece % 2

        got.append(places.send(pick(pieces, places.section ^ turn), route))
    got = jnp.stack(got)
    mine = 2 * (places.section % 2) + places.core
    return jnp.concatenate([pick(got, mine ^ f) for f in range(SECTIONS)], axis=2)


def tokens_out(places, rows):
    several = rows.shape[0]
    features = jnp.stack(jnp.split(rows, SECTIONS, axis=2))
    mine = 2 * (places.section % 2) + places.core
    got = []
    for turn in range(4):

        def route(s, d, turn=turn):
            return (2 * (s % 2) + d % 2) ^ turn, d - d % 2 + s // 2

        got.append(places.send(pick(features, mine ^ turn), route))
    got = jnp.stack(got)
    return jnp.concatenate([pick(got, places.section ^ k) for k in range(4)], axis=1)


def gather_start(places, mine):
    half = D // 4
    from_x = places.swap_section(mine, 1)
    from_y = places.swap_section(mine, 2)
    upper = places.swap_section(from_x[:half], 2)
    lower = places.swap_section(from_y[half:], 1)
    return from_x, from_y, upper, lower


def place_kernel(columns, spot_ref, own_ref, out_ref, sem):
    copy = pltpu.make_async_copy(own_ref.at[:, columns], out_ref.at[spot_ref[0]], sem)
    copy.start()
    copy.wait()


def place_own(places, own, columns):
    return pl.pallas_call(
        functools.partial(place_kernel, columns),
        in_specs=[
            pl.BlockSpec(memory_space=pltpu.SMEM), pl.BlockSpec(memory_space=pl.ANY),
        ],
        out_specs=pl.BlockSpec(memory_space=pl.ANY),
        out_shape=jax.ShapeDtypeStruct((SECTIONS, D, columns.stop - columns.start), BF),
        scratch_shapes=[pltpu.SemaphoreType.DMA],
        cost_estimate=cost(0, 4e6),
        name="place_own",
    )(places.section.reshape(1).astype(jnp.int32), own)


def gather_finish(places, full, pieces):
    half = D // 2
    from_x, from_y, upper, lower = pieces
    start = places.core * half

    def put(full, piece, step, offset):
        spot = places.section ^ step
        far = places.swap_core(piece)
        full = lax.dynamic_update_slice(full, piece[None], (spot, start + offset, 0))
        return lax.dynamic_update_slice(full, far[None], (spot, half - start + offset, 0))

    full = put(full, from_x[:half], 1, 0)
    full = put(full, from_y[:half], 2, 0)
    full = put(full, upper, 3, 0)
    return put(full, lower[: half // 2], 3, half // 2)


def norm_rows(places, norm_grads, final_grad):
    ndp = places.ndp
    cut = jnp.moveaxis(norm_grads.reshape(2, ndp, D // ndp), 1, 0).reshape(ndp, 2 * D // ndp)
    shared = jnp.broadcast_to(final_grad.reshape(1, -1), (ndp, 2 * D // SECTIONS))
    row = jnp.concatenate([cut, shared], axis=1)
    return jnp.pad(row[:, None], ((0, 0), (0, 15), (0, D - row.shape[1]))).astype(BF)


def core_sums(places, rows, extra):
    ndp = places.ndp
    blocks = rows.reshape(ndp // 2, 2, -1, D)
    extra = extra.reshape(ndp // 2, 2, -1, D)

    def of(parity):
        return jnp.concatenate(
            [
                lax.dynamic_index_in_dim(blocks, parity, 1, keepdims=False),
                lax.dynamic_index_in_dim(extra, parity, 1, keepdims=False),
            ],
            axis=1,
        )

    return of(places.core) + places.swap_core(of(1 - places.core))


def reduce_sections(places, sums):
    section = places.section
    cut = max(16, sums[0].shape[1] // 32 * 16)
    stack = jnp.stack(sums)
    near, over_x, over_y, far = (pick(stack, section ^ step) for step in range(4))
    got = places.swap_section(jnp.stack([over_x[:, :cut], far[:, :cut]]), 1)
    upper, upper_y = near[:, :cut] + got[0], over_y[:, :cut] + got[1]
    got = places.swap_section(jnp.stack([over_y[:, cut:], far[:, cut:]]), 2)
    lower, lower_x = near[:, cut:] + got[0], over_x[:, cut:] + got[1]
    upper = upper + places.swap_section(upper_y, 2)
    lower = lower + places.swap_section(lower_x, 1)
    blocks = jnp.concatenate([upper, lower], axis=1)
    total = blocks.shape[0]
    place = places.dp // 2
    if total <= 4:
        got = [pick(blocks, place)]
        for step in range(1, total):
            got.append(places.swap_dp(pick(blocks, place ^ step), 2 * step))
        got = jnp.stack(got)
        out = pick(got, place).astype(F32)
        for spot in range(1, total):
            out = out + pick(got, place ^ spot).astype(F32)
        return out
    bit = total // 2
    while bit:
        blocks = blocks.reshape(2, bit, *blocks.shape[1:])
        mine = (place // bit) % 2
        blocks = pick(blocks, mine) + places.swap_dp(pick(blocks, 1 - mine), 2 * bit)
        bit //= 2
    return blocks[0].astype(F32)


def on_device(
    stream_input,
    accum_input,
    section_weights,
    section_norms,
    final_norm,
    seq_lengths,
    out_cotangent,
):
    places = Places()
    section, core = places.section, places.core
    width = D // SECTIONS
    rows = D // 2

    stream = tokens_in(places, stream_input[None])[0]
    own = section_weights[0]
    small = jnp.concatenate(
        [section_norms[0, 0], section_norms[0, 1], final_norm[0], final_norm[1]], axis=0
    )
    small = jnp.pad(small[None], ((0, 15), (0, 4 * D - small.shape[0])))
    near_own, late_own = own[:, : 4 * D], own[:, 4 * D :]
    mine = lax.dynamic_slice(near_own, (core * rows, 0), (rows, 4 * D))
    near_pieces = gather_start(places, jnp.concatenate([mine, small], axis=0))
    late_mine = after(
        lax.dynamic_slice(late_own, (core * rows, 0), (rows, 2 * D)), near_pieces[0], near_pieces[1]
    )
    late_pieces = gather_start(places, late_mine)
    near = gather_finish(places, place_own(places, own, slice(0, 4 * D)), near_pieces)
    late = gather_finish(places, place_own(places, own, slice(4 * D, 6 * D)), late_pieces)
    tail = jnp.stack(
        [small, near_pieces[0][rows:], near_pieces[1][rows:], near_pieces[3][rows // 2 :]]
    )[:, 0].astype(F32)
    tail = jnp.stack([pick(tail, section ^ j) for j in range(SECTIONS)])
    norms = tail[:, : 2 * D].reshape(SECTIONS, 2, D)
    final = jnp.moveaxis(tail[:, 2 * D : 2 * D + 2 * width].reshape(SECTIONS, 2, width), 0, 1)
    final = final.reshape(2, D)

    other_lengths = places.swap_core(seq_lengths)
    lengths = pick(jnp.where(core == section // 2, seq_lengths, other_lengths), section % 2)
    ending = jnp.cumsum(lengths, dtype=jnp.int32)

    def rows_of(which):
        spots = which * HALF + jnp.arange(HALF, dtype=jnp.int32)
        segment = jnp.sum(
            (spots[:, None] >= ending[None, :]).astype(jnp.int32), axis=1, dtype=jnp.int32
        )
        lane = jnp.arange(LANES, dtype=jnp.int32)
        hot = (segment[:, None] == lane[None, :]).astype(BF)
        alive = (spots < ending[-1]).astype(F32)
        return segment, hot, jnp.broadcast_to(alive[:, None], (HALF, LANES))

    segment_own, kseg_own, live = rows_of(core)
    _, kseg_other, _ = rows_of(1 - core)
    lane = jnp.arange(LANES, dtype=jnp.int32)
    qseg = jnp.where(
        (segment_own[:, None] != lane[None, :]) & (lane[None, :] < 32), -FAR, 0.0
    ).astype(BF)
    segs = (qseg, kseg_own, kseg_other)

    both = after(jnp.stack([accum_input, out_cotangent]), late_pieces[2], late_pieces[3])
    accum, cot = tokens_in(places, both)

    branch_sum = jnp.zeros((HALF, D), F32)
    kept = []
    for layer in (0, 2):
        queries, own_kv = project(stream, near, layer)
        far_kv = places.swap_core(own_kv)
        context, lse, middle, sum_a, branch_sum = attend(
            stream, queries, own_kv, far_kv, segs, near, layer, norms[layer], branch_sum
        )
        following, sum_f, branch_sum = feed(
            middle, near, late, layer + 1, norms[layer + 1], branch_sum, BF if layer == 0 else F32
        )
        kept.append((stream, queries, own_kv, far_kv, context, lse, sum_a, middle, sum_f))
        stream = following

    result, dy_low, upstream, dy, final_grad = finish(stream, branch_sum, accum, cot, live, final)
    result_out, accum_out = tokens_out(places, jnp.stack([result, dy_low]))

    sums = [None] * SECTIONS

    def extra(layer, grads):
        return norm_rows(places, grads, final_grad[:, layer * width : (layer + 1) * width])

    for layer in (2, 0):
        entering, queries, own_kv, far_kv, context, lse, sum_a, middle, sum_f = kept[layer // 2]
        upstream, odd, even, grads = feed_back(
            middle, sum_f, upstream, dy, near, late, layer + 1, norms[layer + 1]
        )
        sums[layer + 1] = core_sums(places, odd, extra(layer + 1, grads))
        dz, dctx, dwo, delta, grads = outward_back(
            sum_a, upstream, dy, context, near, layer, norms[layer]
        )
        dq, dkv_far = scores_back(
            queries, far_kv, dctx, qseg, segs[2], lse, delta, jnp.zeros((HALF, D), F32), BF
        )
        from_far = places.swap_core(dkv_far)
        dq, dkv = scores_back(queries, own_kv, dctx, qseg, segs[1], lse, delta, dq, F32)
        upstream, dqkv = project_back(entering, dq, dkv, from_far, dz, near, layer)
        sums[layer] = core_sums(
            places, jnp.concatenate([dqkv, dwo, even], axis=0), extra(layer, grads)
        )

    reduced = reduce_sections(places, sums)
    block = 6 * D // places.ndp
    slab = reduced[:block].T
    small_out = reduced[block]
    cut = D // places.ndp
    norm_out = small_out[: 2 * cut].reshape(2, cut)
    final_out = small_out[2 * cut : 2 * cut + 2 * width].reshape(2, width)
    stream_out = tokens_out(places, upstream[None])[0]

    return (
        result_out,
        stream_out.astype(F32),
        accum_out.astype(F32),
        slab[None],
        norm_out[None],
        final_out,
    )


def solution(mesh):
    placed = (
        P("dp", "section"),
        P("dp", "section"),
        P("section", None, None),
        P("section", None, None),
        P(None, "section"),
        P("dp", None),
        P("dp", "section"),
    )
    return jax.shard_map(
        on_device,
        mesh=mesh,
        in_specs=placed,
        out_specs=(
            P("dp", "section"),
            P("dp", "section"),
            P("dp", "section"),
            P("section", None, "dp"),
            P("section", None, "dp"),
            P(None, "section"),
        ),
        check_vma=False,
    )
```

time: 687 us -> 495 us (0.72)
  starting transfers between devices: 242 us -> 94.4 us
  Pallas kernels: 120 us -> 211 us
  blocking collectives: 81 us -> 0 us
  local copies, waits for them, and re-layouts: 130 us -> 73.3 us
    ppermute x72 -> x16, starting transfers between devices: 224 us -> 72.5 us  [send(): return lax.ppermute(block, ('section', 'dp'), pairs)]
    pallas_call x14 -> x16, Pallas kernels: 112 us -> 202 us  [the longest x2 97.5 us: place_own(): pl.pallas_call(functools.partial(place_kernel, columns), in_specs=[pl.Blo...]
    dynamic_slice x14 -> x3, local copies, waits for them, and re-layouts: 44.5 us -> 1.55 us  [the longest x1 0.84 us: on_device(): lax.dynamic_slice(late_own, (core * rows, 0), (rows, 2 * D))]
    all_gather x1 -> x0, blocking collectives: 41.4 us -> none  [on_device(): small = lax.all_gather(small, 'section', axis=0).astype(F32)]
    psum x1 -> x0, blocking collectives: 39.7 us -> none  [on_device(): small_grads = lax.psum(small_grads, ('section', 'dp'))]
    ppermute x72 -> x16, waiting for transfers between devices: 54.3 us -> 16.2 us  [send(): return lax.ppermute(block, ('section', 'dp'), pairs)]
    ppermute x18 -> x20, waiting for transfers between devices: 0.46 us -> 33.6 us  [swap_dp(): return lax.ppermute(block, 'dp', [(i, i ^ step) for i in range(self.ndp)])]
    reshape x10 -> x14, local copies, waits for them, and re-layouts: 35.9 us -> 3.83 us  [the longest x8 2.19 us: norm_rows(): norm_grads.reshape(2, ndp, D // ndp)]
  transfers between devices with their start and end apart: 94 -> 48, of which waited for: 20 -> 13; matrix products, arithmetic and copies ran while one was open for 19% -> 16% of each run, Pallas kernels for 10% -> 31%
where the time goes in v2:
time: 495 us; the launch traced here: 486 us
  Pallas kernels  211 us (43%)
  starting transfers between devices  94.4 us (19%)
  local copies, waits for them, and re-layouts  73.3 us (15%)
  waiting for transfers between devices  72 us (15%)
  other arithmetic  32.7 us (7%)
    pallas_call x2, Pallas kernels, place_own(): pl.pallas_call(functools.partial(place_kernel, columns), in_specs=[pl.Blo...  97.5 us
    ppermute x16, starting transfers between devices, send(): return lax.ppermute(block, ('section', 'dp'), pairs)  72.5 us
    pallas_call x4, Pallas kernels, scores_back(): pl.pallas_call(scores_back_kernel, grid=(PAIRS,), in_specs=[column(), pai...  37.4 us
    ppermute x20, waiting for transfers between devices, swap_dp(): return lax.ppermute(block, 'dp', [(i, i ^ step) for i in range(self.ndp)])  33.6 us
    pallas_call x2, Pallas kernels, feed_back(): pl.pallas_call(feed_back_kernel, grid=(2,), in_specs=[whole(HALF, D), who...  23 us
    ppermute x12, waiting for transfers between devices, swap_section(): lax.ppermute(block, 'section', [(i, i ^ step) for i in range(SECTIONS)])  22.3 us
    pallas_call x2, Pallas kernels, attend(): pl.pallas_call(attend_kernel, grid=(PAIRS,), in_specs=[column(), pair_blo...  20.5 us
    ppermute x16, waiting for transfers between devices, send(): return lax.ppermute(block, ('section', 'dp'), pairs)  16.2 us
  transfers between devices with their start and end apart: 48, of which 13 were waited for; matrix products, arithmetic and copies ran while one was open for 16% of the time, Pallas kernels for 31%

profile of v2, /device:TPU:8, one launch (start us, length us, event | category | flops | bytes accessed | tf_op | source)
XLA Modules:
  0.0 486.0 jit_solution(9516454837584128277)
XLA Ops:
  0.7 1.7 slice.195
  4.4 1.5 collective-permute-start.4
  5.8 1.5 collective-permute-start.6
  12.3 32.9 %place_own.3 = bf16[4,512,1024]{2,1,0:T(8,128)(2,1)} custom-call(s32[1]{0:T(128)} %bitcast.14.spot_ref, bf16[512,3072]{1,0:T(8,128)(2,1)} %bitcast.338), custom_call_target="tpu_custom_call" | custom-call | bytes 4000000 | tf_op jit(solution)/shard_map/place_own/pallas_call | solution.py:580
  45.2 64.6 %place_own.2 = bf16[4,512,2048]{2,1,0:T(8,128)(2,1)} custom-call(s32[1]{0:T(128)} %bitcast.14.spot_ref, bf16[512,3072]{1,0:T(8,128)(2,1)} %bitcast.339), custom_call_target="tpu_custom_call" | custom-call | bytes 4000000 | tf_op jit(solution)/shard_map/place_own/pallas_call | solution.py:580
  111.8 2.7 collective-permute-start.2
  115.1 1.9 collective-permute-start.3
  118.9 4.1 collective-permute-done.3
  124.9 2.3 slice.196
  128.8 1.5 collective-permute-start.10
  130.3 2.3 bitcast_dynamic-update-slice_fusion.3
  132.6 1.9 slice.198
  135.4 4.0 collective-permute-done.14
  140.2 2.0 collective-permute-start.18
  143.7 5.1 %collective-permute-done.10 = bf16[144,2048]{1,0:T(8,128)(2,1)S(1)} collective-permute-done((bf16[144,2048]{1,0:T(8,128)(2,1)S(1)}, bf16[144,2048]{1,0:T(8,128)(2,1)S(1)}, u32[]{:S(2)}, u32[]{:S(2)}) %collective-permute-start.10) | collective-permute-done | bytes 589856 | tf_op jit(solution)/shard_map/ppermute | solution.py:513
  148.8 1.7 collective-permute-start.20
  152.4 2.7 collective-permute-done.18
  156.5 2.3 bitcast_dynamic-update-slice_fusion.2
  159.9 2.3 bitcast_dynamic-update-slice_fusion
  163.5 1.9 bitcast_dynamic-update-slice_fusion.11
  168.9 2.4 project.2
  176.6 10.3 %attend.2 = (bf16[512,512]{1,0:T(8,128)(2,1)S(1)}, f32[512,128]{1,0:T(8,128)S(1)}, bf16[512,512]{1,0:T(8,128)(2,1)S(1)}, f32[512,512]{1,0:T(8,128)S(1)}, f32[512,512]{1,0:T(8,128)S(1)}) custom-call(bf16[512,512]{1,0:T(8,128)(2,1)S(1)} %get-tuple-element.63.q_ref, bf16[4,512,256]{2,1,0:T(8,128)(2,1)S(1)} %get-tuple-element.64.own_ref.kv_ref, ...), custom_call_target="tpu_custom_call" | custom-call | flops 8000000000 | bytes 8000000 | tf_op jit(solution)/shard_map/attend/pallas_call | solution.py:176
  188.7 5.1 %feed.2 = (bf16[512,512]{1,0:T(8,128)(2,1)S(1)}, f32[512,512]{1,0:T(8,128)S(1)}, f32[512,512]{1,0:T(8,128)S(1)}) custom-call(bf16[512,512]{1,0:T(8,128)(2,1)S(1)} %get-tuple-element.65.x_ref, bf16[4,512,1024]{2,1,0:T(8,128)(2,1)} %bitcast_dynamic-update-slice_fusion.12.in_a_ref.out_b_ref, ...), custom_call_target="tpu_custom_call" | custom-call | flops 2147483648 | bytes 8000000 | tf_op jit(solution)/shard_map/feed/pallas_call | solution.py:246
  194.9 2.8 project.3
  199.2 3.6 collective-permute-start.23
  202.8 2.0 collective-permute-start.25
  204.8 3.2 collective-permute-start.26
  210.7 5.2 %collective-permute-done.24 = bf16[2,512,128]{2,1,0:T(8,128)(2,1)} collective-permute-done((bf16[2,512,128]{2,1,0:T(8,128)(2,1)}, bf16[2,512,128]{2,1,0:T(8,128)(2,1)}, u32[]{:S(2)}, u32[]{:S(2)}) %collective-permute-start.24) | collective-permute-done | bytes 262176 | tf_op jit(solution)/shard_map/ppermute | solution.py:521
  215.9 3.0 collective-permute-done.26
  221.4 10.2 %attend.3 = (bf16[512,512]{1,0:T(8,128)(2,1)S(1)}, f32[512,128]{1,0:T(8,128)S(1)}, bf16[512,512]{1,0:T(8,128)(2,1)S(1)}, f32[512,512]{1,0:T(8,128)S(1)}, f32[512,512]{1,0:T(8,128)S(1)}) custom-call(bf16[512,512]{1,0:T(8,128)(2,1)S(1)} %copy-done.34, bf16[4,512,256]{2,1,0:T(8,128)(2,1)S(1)} %get-tuple-element.70.own_ref.kv_ref, ...), custom_call_target="tpu_custom_call" | custom-call | flops 8000000000 | bytes 8000000 | tf_op jit(solution)/shard_map/attend/pallas_call | solution.py:176
  231.6 5.1 %feed.3 = (f32[512,512]{1,0:T(8,128)S(1)}, f32[512,512]{1,0:T(8,128)S(1)}, f32[512,512]{1,0:T(8,128)S(1)}) custom-call(bf16[512,512]{1,0:T(8,128)(2,1)S(1)} %get-tuple-element.72.x_ref, bf16[4,512,1024]{2,1,0:T(8,128)(2,1)} %bitcast_dynamic-update-slice_fusion.12.in_a_ref.out_b_ref, ...), custom_call_target="tpu_custom_call" | custom-call | flops 2147483648 | bytes 8000000 | tf_op jit(solution)/shard_map/feed/pallas_call | solution.py:246
  237.9 2.3 finish.1
  241.0 11.5 %feed_back.2 = (bf16[512,512]{1,0:T(8,128)(2,1)S(1)}, bf16[3,2,512,512]{3,2,1,0:T(8,128)(2,1)}, bf16[1024,512]{1,0:T(8,128)(2,1)S(1)}, f32[2,512]{1,0:T(2,128)S(1)}) custom-call(bf16[512,512]{1,0:T(8,128)(2,1)S(1)} %get-tuple-element.72.x_ref, f32[512,512]{1,0:T(8,128)S(1)} %get-tuple-element.82.sum_ref, f32[512,512]{1,0:T(8,128)S(1)} %get-tuple-element.83.up_ref, ...), custom_call_target="tpu_custom_call" | custom-call | flops 5368709120 | bytes 16000000 | tf_op jit(solution)/shard_map/feed_back/pallas_call | solution.py:335
  253.5 3.1 outward_back.2
  257.5 10.1 %scores_back.4 = (f32[512,512]{1,0:T(8,128)S(1)}, bf16[4,512,256]{2,1,0:T(8,128)(2,1)}) custom-call(bf16[512,512]{1,0:T(8,128)(2,1)S(1)} %copy-done.34, bf16[4,512,256]{2,1,0:T(8,128)(2,1)} %collective-permute-done.22.far_ref.kv_ref, bf16[512,512]{1,0:T(8,128)(2,1)S(1)} %get-tuple-element.87.dctx_ref, bf16[512,128]{1,0:T(8,128)(2,1)S(1)} %select_convert_fusion.qs_ref, ...), custom_call_target="tpu_custom_call" | custom-call | flops 8000000000 | bytes 8000000 | tf_op jit(solution)/shard_map/scores_back/pallas_call | solution.py:450
  275.7 3.3 dynamic-slice_bitcast_fusion.5
  282.9 9.1 %scores_back.5 = (f32[512,512]{1,0:T(8,128)S(1)}, f32[4,512,256]{2,1,0:T(8,128)}) custom-call(bf16[512,512]{1,0:T(8,128)(2,1)S(1)} %copy-done.35, bf16[4,512,256]{2,1,0:T(8,128)(2,1)S(1)} %copy-done.28, bf16[512,512]{1,0:T(8,128)(2,1)S(1)} %copy-done.39, bf16[512,128]{1,0:T(8,128)(2,1)S(1)} %select_convert_fusion.qs_ref, ...), custom_call_target="tpu_custom_call" | custom-call | flops 8000000000 | bytes 8000000 | tf_op jit(solution)/shard_map/scores_back/pallas_call | solution.py:450
  292.0 4.3 project_back.2
  297.5 11.5 %feed_back.3 = (bf16[512,512]{1,0:T(8,128)(2,1)S(1)}, bf16[3,2,512,512]{3,2,1,0:T(8,128)(2,1)}, bf16[1024,512]{1,0:T(8,128)(2,1)S(1)}, f32[2,512]{1,0:T(2,128)S(1)}) custom-call(bf16[512,512]{1,0:T(8,128)(2,1)S(1)} %get-tuple-element.65.x_ref, f32[512,512]{1,0:T(8,128)S(1)} %copy-done.14, bf16[512,512]{1,0:T(8,128)(2,1)S(1)} %get-tuple-element.95.up_ref, ...), custom_call_target="tpu_custom_call" | custom-call | flops 5368709120 | bytes 16000000 | tf_op jit(solution)/shard_map/feed_back/pallas_call | solution.py:335
  309.1 3.4 outward_back.3
  313.4 9.0 %scores_back.6 = (f32[512,512]{1,0:T(8,128)S(1)}, bf16[4,512,256]{2,1,0:T(8,128)(2,1)}) custom-call(bf16[512,512]{1,0:T(8,128)(2,1)S(1)} %copy-done.31, bf16[4,512,256]{2,1,0:T(8,128)(2,1)S(1)} %copy-done.26, bf16[512,512]{1,0:T(8,128)(2,1)S(1)} %get-tuple-element.98.dctx_ref, bf16[512,128]{1,0:T(8,128)(2,1)S(1)} %select_convert_fusion.qs_ref, ...), custom_call_target="tpu_custom_call" | custom-call | flops 8000000000 | bytes 8000000 | tf_op jit(solution)/shard_map/scores_back/pallas_call | solution.py:450
  323.8 3.3 dynamic-slice_bitcast_fusion.9
  332.2 9.1 %scores_back.7 = (f32[512,512]{1,0:T(8,128)S(1)}, f32[4,512,256]{2,1,0:T(8,128)}) custom-call(bf16[512,512]{1,0:T(8,128)(2,1)S(1)} %copy-done.32, bf16[4,512,256]{2,1,0:T(8,128)(2,1)S(1)} %copy-done.24, bf16[512,512]{1,0:T(8,128)(2,1)S(1)} %copy-done.37, bf16[512,128]{1,0:T(8,128)(2,1)S(1)} %select_convert_fusion.qs_ref, ...), custom_call_target="tpu_custom_call" | custom-call | flops 8000000000 | bytes 8000000 | tf_op jit(solution)/shard_map/scores_back/pallas_call | solution.py:450
  343.1 4.0 project_back.3
  349.1 2.0 fusion.3
  351.2 2.0 fusion.1
  355.4 1.8 dynamic-slice_bitcast_fusion.3
  357.4 1.5 pad_maximum_fusion.9
  359.0 1.4 pad_maximum_fusion.3
  360.3 1.5 collective-permute-start.43
  363.0 3.3 collective-permute-start.28
  366.2 1.7 collective-permute-start.29
  368.0 42.2 %collective-permute-start.30 = (bf16[2,512,128]{2,1,0:T(8,128)(2,1)S(1)}, bf16[2,512,128]{2,1,0:T(8,128)(2,1)}, u32[]{:S(2)}, u32[]{:S(2)}) collective-permute-start(bf16[2,512,128]{2,1,0:T(8,128)(2,1)S(1)} %get-tuple-element.159), channel_id=1, source_target_pairs={{0,24},{1,16},{2,26},{3,18},{4,28},{5,20},{6,30},{7,22},{8,8},{9,0... | collective-permute-start | bytes 786440 | tf_op jit(solution)/shard_map/ppermute | solution.py:521
  410.3 3.8 collective-permute-done.30
  415.5 1.5 fusion.7
  417.0 1.6 collective-permute-start.42
  419.8 2.6 collective-permute-start.44
  424.7 2.8 collective-permute-start.34
  427.5 9.0 %collective-permute-done.42 = bf16[4,192,512]{2,1,0:T(8,128)(2,1)S(1)} collective-permute-done((bf16[4,192,512]{2,1,0:T(8,128)(2,1)S(1)}, bf16[4,192,512]{2,1,0:T(8,128)(2,1)S(1)}, u32[]{:S(2)}, u32[]{:S(2)}) %collective-permute-start.42) | collective-permute-done | bytes 786464 | tf_op jit(solution)/shard_map/ppermute | solution.py:513
  436.5 4.9 %collective-permute-start.36 = (bf16[1,512,128]{2,1,0:T(8,128)(2,1)S(1)}, bf16[1,512,128]{2,1,0:T(8,128)(2,1)S(1)}, u32[]{:S(2)}, u32[]{:S(2)}) collective-permute-start(bf16[1,512,128]{2,1,0:T(8,128)(2,1)S(1)} %get-tuple-element.181), channel_id=1, source_target_pairs={{0,24},{1,16},{2,26},{3,18},{4,28},{5,20},{6,30},{7,22},{8,8},{9,0... | collective-permute-start | bytes 393224 | tf_op jit(solution)/shard_map/ppermute | solution.py:521
  444.7 2.6 collective-permute-start.46
  449.0 11.6 %collective-permute-done.45 = bf16[400,512]{1,0:T(8,128)(2,1)S(1)} collective-permute-done((bf16[400,512]{1,0:T(8,128)(2,1)S(1)}, bf16[400,512]{1,0:T(8,128)(2,1)S(1)}, u32[]{:S(2)}, u32[]{:S(2)}) %collective-permute-start.45) | collective-permute-done | bytes 409632 | tf_op jit(solution)/shard_map/ppermute | solution.py:507
  460.6 14.2 %collective-permute-done.46 = bf16[400,512]{1,0:T(8,128)(2,1)S(1)} collective-permute-done((bf16[400,512]{1,0:T(8,128)(2,1)S(1)}, bf16[400,512]{1,0:T(8,128)(2,1)S(1)}, u32[]{:S(2)}, u32[]{:S(2)}) %collective-permute-start.46) | collective-permute-done | bytes 409632 | tf_op jit(solution)/shard_map/ppermute | solution.py:507
  474.8 7.7 %collective-permute-done.47 = bf16[400,512]{1,0:T(8,128)(2,1)S(1)} collective-permute-done((bf16[400,512]{1,0:T(8,128)(2,1)S(1)}, bf16[400,512]{1,0:T(8,128)(2,1)S(1)}, u32[]{:S(2)}, u32[]{:S(2)}) %collective-permute-start.47) | collective-permute-done | bytes 409632 | tf_op jit(solution)/shard_map/ppermute | solution.py:507
  (367 shorter events, 85.5 us)
Async XLA Ops:
  4.4 119.9 %collective-permute-start.4 = (bf16[272,2048]{1,0:T(8,128)(2,1)}, bf16[272,2048]{1,0:T(8,128)(2,1)}, u32[]{:S(2)}, u32[]{:S(2)}) collective-permute-start(bf16[272,2048]{1,0:T(8,128)(2,1)} %pad_maximum_fusion.10), channel_id=1, source_target_pairs={{0,8},{8,0},{16,24},{24,16},{1,9},{9,1},{17,25},{25,17},{2,10},{10... | collective-permute-start | bytes 3342344 | tf_op jit(solution)/shard_map/ppermute | solution.py:513
  5.8 118.4 %collective-permute-start.6 = (bf16[272,2048]{1,0:T(8,128)(2,1)}, bf16[272,2048]{1,0:T(8,128)(2,1)S(1)}, u32[]{:S(2)}, u32[]{:S(2)}) collective-permute-start(bf16[272,2048]{1,0:T(8,128)(2,1)} %pad_maximum_fusion.10), channel_id=1, source_target_pairs={{0,16},{8,24},{16,0},{24,8},{1,17},{9,25},{17,1},{25,9},{2,18},{10... | collective-permute-start | bytes 3342344 | tf_op jit(solution)/shard_map/ppermute | solution.py:513
  8.1 107.0 %collective-permute-start = (bf16[1,512,128]{2,1,0:T(8,128)(2,1)S(1)}, bf16[1,512,128]{2,1,0:T(8,128)(2,1)}, u32[]{:S(2)}, u32[]{:S(2)}) collective-permute-start(bf16[1,512,128]{2,1,0:T(8,128)(2,1)S(1)} %get-tuple-element.192), channel_id=1, source_target_pairs={{0,0},{1,16},{2,2},{3,18},{4,4},{5,20},{6,6},{7,22},{8,1},{9,17},{... | collective-permute-start | bytes 393224 | tf_op jit(solution)/shard_map/ppermute | solution.py:521
  9.4 109.5 %collective-permute-start.1 = (bf16[1,512,128]{2,1,0:T(8,128)(2,1)}, bf16[1,512,128]{2,1,0:T(8,128)(2,1)}, u32[]{:S(2)}, u32[]{:S(2)}) collective-permute-start(bf16[1,512,128]{2,1,0:T(8,128)(2,1)} %get-tuple-element.195), channel_id=1, source_target_pairs={{0,1},{1,17},{2,3},{3,19},{4,5},{5,21},{6,7},{7,23},{8,0},{9,16},{... | collective-permute-start | bytes 393224 | tf_op jit(solution)/shard_map/ppermute | solution.py:521
  10.7 101.1 %collective-permute-start.13 = (s32[2,16]{1,0:T(2,128)S(1)}, s32[2,16]{1,0:T(2,128)S(1)}, u32[]{:S(2)}, u32[]{:S(2)}) collective-permute-start(s32[2,16]{1,0:T(2,128)S(1)} %copy-done.78), channel_id=1, source_target_pairs={{0,1},{1,0},{2,3},{3,2},{4,5},{5,4},{6,7},{7,6},{8,9},{9,8},{10,11... | collective-permute-start | bytes 392 | tf_op jit(solution)/shard_map/ppermute | solution.py:507
  45.2 65.6 %copy-start.63 = (bf16[2048,128]{1,0:T(8,128)(2,1)S(1)}, bf16[2048,128]{1,0:T(8,128)(2,1)}, u32[]{:S(2)}) copy-start(bf16[2048,128]{1,0:T(8,128)(2,1)} %param.13) | copy-start | bytes 1572868
  45.2 65.6 %copy-start.64 = (bf16[2048,128]{1,0:T(8,128)(2,1)S(1)}, bf16[2048,128]{1,0:T(8,128)(2,1)}, u32[]{:S(2)}) copy-start(bf16[2048,128]{1,0:T(8,128)(2,1)} %param.8) | copy-start | bytes 1572868
  111.8 7.1 %collective-permute-start.2 = (bf16[1,512,128]{2,1,0:T(8,128)(2,1)}, bf16[1,512,128]{2,1,0:T(8,128)(2,1)S(1)}, u32[]{:S(2)}, u32[]{:S(2)}) collective-permute-start(bf16[1,512,128]{2,1,0:T(8,128)(2,1)} %get-tuple-element.194), channel_id=1, source_target_pairs={{0,8},{1,24},{2,10},{3,26},{4,12},{5,28},{6,14},{7,30},{8,9},{9,25... | collective-permute-start | bytes 393224 | tf_op jit(solution)/shard_map/ppermute | solution.py:521
  115.1 8.0 %collective-permute-start.3 = (bf16[1,512,128]{2,1,0:T(8,128)(2,1)}, bf16[1,512,128]{2,1,0:T(8,128)(2,1)S(1)}, u32[]{:S(2)}, u32[]{:S(2)}) collective-permute-start(bf16[1,512,128]{2,1,0:T(8,128)(2,1)} %get-tuple-element.193), channel_id=1, source_target_pairs={{0,9},{1,25},{2,11},{3,27},{4,13},{5,29},{6,15},{7,31},{8,8},{9,24... | collective-permute-start | bytes 393224 | tf_op jit(solution)/shard_map/ppermute | solution.py:521
  124.2 15.1 %collective-permute-start.14 = (bf16[256,1024]{1,0:T(8,128)(2,1)}, bf16[256,1024]{1,0:T(8,128)(2,1)S(1)}, u32[]{:S(2)}, u32[]{:S(2)}) collective-permute-start(bf16[256,1024]{1,0:T(8,128)(2,1)} %constant_dynamic-slice_fusion.3), channel_id=1, source_target_pairs={{0,8},{8,0},{16,24},{24,16},{1,9},{9,1},{17,25},{25,17},{2,10},{10... | collective-permute-start | bytes 1572872 | tf_op jit(solution)/shard_map/ppermute | solution.py:513
  124.3 15.8 %collective-permute-start.16 = (bf16[256,1024]{1,0:T(8,128)(2,1)}, bf16[256,1024]{1,0:T(8,128)(2,1)S(1)}, u32[]{:S(2)}, u32[]{:S(2)}) collective-permute-start(bf16[256,1024]{1,0:T(8,128)(2,1)} %constant_dynamic-slice_fusion.3), channel_id=1, source_target_pairs={{0,16},{8,24},{16,0},{24,8},{1,17},{9,25},{17,1},{25,9},{2,18},{10... | collective-permute-start | bytes 1572872 | tf_op jit(solution)/shard_map/ppermute | solution.py:513
  127.2 28.8 %collective-permute-start.5 = (bf16[256,2048]{1,0:T(8,128)(2,1)}, bf16[256,2048]{1,0:T(8,128)(2,1)}, u32[]{:S(2)}, u32[]{:S(2)}) collective-permute-start(bf16[256,2048]{1,0:T(8,128)(2,1)} %slice.196), channel_id=1, source_target_pairs={{0,1},{1,0},{2,3},{3,2},{4,5},{5,4},{6,7},{7,6},{8,9},{9,8},{10,11... | collective-permute-start | bytes 3145736 | tf_op jit(solution)/shard_map/ppermute | solution.py:507
  128.2 31.6 %collective-permute-start.7 = (bf16[256,2048]{1,0:T(8,128)(2,1)}, bf16[256,2048]{1,0:T(8,128)(2,1)}, u32[]{:S(2)}, u32[]{:S(2)}) collective-permute-start(bf16[256,2048]{1,0:T(8,128)(2,1)} %slice.197), channel_id=1, source_target_pairs={{0,1},{1,0},{2,3},{3,2},{4,5},{5,4},{6,7},{7,6},{8,9},{9,8},{10,11... | collective-permute-start | bytes 3145736 | tf_op jit(solution)/shard_map/ppermute | solution.py:507
  128.8 20.0 %collective-permute-start.10 = (bf16[144,2048]{1,0:T(8,128)(2,1)S(1)}, bf16[144,2048]{1,0:T(8,128)(2,1)S(1)}, u32[]{:S(2)}, u32[]{:S(2)}) collective-permute-start(bf16[144,2048]{1,0:T(8,128)(2,1)S(1)} %slice.199), channel_id=1, source_target_pairs={{0,8},{8,0},{16,24},{24,16},{1,9},{9,1},{17,25},{25,17},{2,10},{10... | collective-permute-start | bytes 1769480 | tf_op jit(solution)/shard_map/ppermute | solution.py:513
  132.6 17.9 %copy-start.68 = (bf16[1,16,2048]{2,1,0:T(8,128)(2,1)S(1)}, bf16[1,16,2048]{2,1,0:T(8,128)(2,1)}, u32[]{:S(2)}) copy-start(bf16[1,16,2048]{2,1,0:T(8,128)(2,1)} %get-tuple-element.208) | copy-start | bytes 196612
  139.4 11.8 %copy-start.61 = (bf16[256,1024]{1,0:T(8,128)(2,1)}, bf16[256,1024]{1,0:T(8,128)(2,1)S(1)}, u32[]{:S(2)}) copy-start(bf16[256,1024]{1,0:T(8,128)(2,1)S(1)} %collective-permute-done.14) | copy-start | bytes 1572868
  139.4 13.0 %collective-permute-start.8 = (bf16[128,2048]{1,0:T(8,128)(2,1)}, bf16[128,2048]{1,0:T(8,128)(2,1)}, u32[]{:S(2)}, u32[]{:S(2)}) collective-permute-start(bf16[128,2048]{1,0:T(8,128)(2,1)} %slice.198), channel_id=1, source_target_pairs={{0,16},{8,24},{16,0},{24,8},{1,17},{9,25},{17,1},{25,9},{2,18},{10... | collective-permute-start | bytes 1572872 | tf_op jit(solution)/shard_map/ppermute | solution.py:513
  140.2 11.1 %copy-start.59 = (bf16[256,1024]{1,0:T(8,128)(2,1)}, bf16[256,1024]{1,0:T(8,128)(2,1)S(1)}, u32[]{:S(2)}) copy-start(bf16[256,1024]{1,0:T(8,128)(2,1)S(1)} %collective-permute-done.16) | copy-start | bytes 1572868
  140.2 15.0 %collective-permute-start.18 = (bf16[128,1024]{1,0:T(8,128)(2,1)}, bf16[128,1024]{1,0:T(8,128)(2,1)S(1)}, u32[]{:S(2)}, u32[]{:S(2)}) collective-permute-start(bf16[128,1024]{1,0:T(8,128)(2,1)} %slice.206), channel_id=1, source_target_pairs={{0,16},{8,24},{16,0},{24,8},{1,17},{9,25},{17,1},{25,9},{2,18},{10... | collective-permute-start | bytes 786440 | tf_op jit(solution)/shard_map/ppermute | solution.py:513
  148.8 7.2 %collective-permute-start.20 = (bf16[128,1024]{1,0:T(8,128)(2,1)}, bf16[128,1024]{1,0:T(8,128)(2,1)S(1)}, u32[]{:S(2)}, u32[]{:S(2)}) collective-permute-start(bf16[128,1024]{1,0:T(8,128)(2,1)} %slice.207), channel_id=1, source_target_pairs={{0,8},{8,0},{16,24},{24,16},{1,9},{9,1},{17,25},{25,17},{2,10},{10... | collective-permute-start | bytes 786440 | tf_op jit(solution)/shard_map/ppermute | solution.py:513
  151.2 56.8 %copy-start.69 = (f32[1,2048]{1,0:T(1,128)}, f32[1,2048]{1,0:T(1,128)S(1)}, u32[]{:S(2)}) copy-start(f32[1,2048]{1,0:T(1,128)S(1)} %get-tuple-element.205) | copy-start | bytes 24580
  152.4 9.8 %collective-permute-start.15 = (bf16[256,1024]{1,0:T(8,128)(2,1)}, bf16[256,1024]{1,0:T(8,128)(2,1)S(1)}, u32[]{:S(2)}, u32[]{:S(2)}) collective-permute-start(bf16[256,1024]{1,0:T(8,128)(2,1)} %copy-done.61), channel_id=1, source_target_pairs={{0,1},{1,0},{2,3},{3,2},{4,5},{5,4},{6,7},{7,6},{8,9},{9,8},{10,11... | collective-permute-start | bytes 1572872 | tf_op jit(solution)/shard_map/ppermute | solution.py:507
  155.1 16.3 %collective-permute-start.17 = (bf16[256,1024]{1,0:T(8,128)(2,1)}, bf16[256,1024]{1,0:T(8,128)(2,1)S(1)}, u32[]{:S(2)}, u32[]{:S(2)}) collective-permute-start(bf16[256,1024]{1,0:T(8,128)(2,1)} %copy-done.59), channel_id=1, source_target_pairs={{0,1},{1,0},{2,3},{3,2},{4,5},{5,4},{6,7},{7,6},{8,9},{9,8},{10,11... | collective-permute-start | bytes 1572872 | tf_op jit(solution)/shard_map/ppermute | solution.py:507
  156.0 9.5 %collective-permute-start.9 = (bf16[128,2048]{1,0:T(8,128)(2,1)}, bf16[128,2048]{1,0:T(8,128)(2,1)S(1)}, u32[]{:S(2)}, u32[]{:S(2)}) collective-permute-start(bf16[128,2048]{1,0:T(8,128)(2,1)} %collective-permute-done.8), channel_id=1, source_target_pairs={{0,1},{1,0},{2,3},{3,2},{4,5},{5,4},{6,7},{7,6},{8,9},{9,8},{10,11... | collective-permute-start | bytes 1572872 | tf_op jit(solution)/shard_map/ppermute | solution.py:507
  156.0 12.0 %collective-permute-start.11 = (bf16[128,2048]{1,0:T(8,128)(2,1)S(1)}, bf16[128,2048]{1,0:T(8,128)(2,1)S(1)}, u32[]{:S(2)}, u32[]{:S(2)}) collective-permute-start(bf16[128,2048]{1,0:T(8,128)(2,1)S(1)} %slice.200), channel_id=1, source_target_pairs={{0,1},{1,0},{2,3},{3,2},{4,5},{5,4},{6,7},{7,6},{8,9},{9,8},{10,11... | collective-permute-start | bytes 1572872 | tf_op jit(solution)/shard_map/ppermute | solution.py:507
  159.9 13.3 %collective-permute-start.19 = (bf16[128,1024]{1,0:T(8,128)(2,1)S(1)}, bf16[128,1024]{1,0:T(8,128)(2,1)S(1)}, u32[]{:S(2)}, u32[]{:S(2)}) collective-permute-start(bf16[128,1024]{1,0:T(8,128)(2,1)S(1)} %collective-permute-done.18), channel_id=1, source_target_pairs={{0,1},{1,0},{2,3},{3,2},{4,5},{5,4},{6,7},{7,6},{8,9},{9,8},{10,11... | collective-permute-start | bytes 786440 | tf_op jit(solution)/shard_map/ppermute | solution.py:507
  162.2 12.3 %collective-permute-start.21 = (bf16[128,1024]{1,0:T(8,128)(2,1)S(1)}, bf16[128,1024]{1,0:T(8,128)(2,1)S(1)}, u32[]{:S(2)}, u32[]{:S(2)}) collective-permute-start(bf16[128,1024]{1,0:T(8,128)(2,1)S(1)} %collective-permute-done.20), channel_id=1, source_target_pairs={{0,1},{1,0},{2,3},{3,2},{4,5},{5,4},{6,7},{7,6},{8,9},{9,8},{10,11... | collective-permute-start | bytes 786440 | tf_op jit(solution)/shard_map/ppermute | solution.py:507
  171.3 4.0 collective-permute-start.12
  197.7 11.6 %copy-start.33 = (bf16[512,512]{1,0:T(8,128)(2,1)}, bf16[512,512]{1,0:T(8,128)(2,1)S(1)}, u32[]{:S(2)}) copy-start(bf16[512,512]{1,0:T(8,128)(2,1)S(1)} %get-tuple-element.69.q_ref) | copy-start | bytes 1572868
  197.7 22.9 %copy-start.27 = (bf16[4,512,256]{2,1,0:T(8,128)(2,1)}, bf16[4,512,256]{2,1,0:T(8,128)(2,1)S(1)}, u32[]{:S(2)}) copy-start(bf16[4,512,256]{2,1,0:T(8,128)(2,1)S(1)} %get-tuple-element.70.own_ref.kv_ref) | copy-start | bytes 3145732
  197.7 22.8 %collective-permute-start.22 = (bf16[4,512,256]{2,1,0:T(8,128)(2,1)S(1)}, bf16[4,512,256]{2,1,0:T(8,128)(2,1)}, u32[]{:S(2)}, u32[]{:S(2)}) collective-permute-start(bf16[4,512,256]{2,1,0:T(8,128)(2,1)S(1)} %get-tuple-element.70.own_ref.kv_ref), channel_id=1, source_target_pairs={{0,1},{1,0},{2,3},{3,2},{4,5},{5,4},{6,7},{7,6},{8,9},{9,8},{10,11... | collective-permute-start | bytes 3145736 | tf_op jit(solution)/shard_map/ppermute | solution.py:507
  199.2 11.5 %collective-permute-start.23 = (bf16[2,512,128]{2,1,0:T(8,128)(2,1)}, bf16[2,512,128]{2,1,0:T(8,128)(2,1)}, u32[]{:S(2)}, u32[]{:S(2)}) collective-permute-start(bf16[2,512,128]{2,1,0:T(8,128)(2,1)} %get-tuple-element.172), channel_id=1, source_target_pairs={{0,0},{1,16},{2,2},{3,18},{4,4},{5,20},{6,6},{7,22},{8,1},{9,17},{... | collective-permute-start | bytes 786440 | tf_op jit(solution)/shard_map/ppermute | solution.py:521
  202.8 13.2 %collective-permute-start.24 = (bf16[2,512,128]{2,1,0:T(8,128)(2,1)}, bf16[2,512,128]{2,1,0:T(8,128)(2,1)}, u32[]{:S(2)}, u32[]{:S(2)}) collective-permute-start(bf16[2,512,128]{2,1,0:T(8,128)(2,1)} %get-tuple-element.175), channel_id=1, source_target_pairs={{0,1},{1,17},{2,3},{3,19},{4,5},{5,21},{6,7},{7,23},{8,0},{9,16},{... | collective-permute-start | bytes 786440 | tf_op jit(solution)/shard_map/ppermute | solution.py:521
  202.8 13.2 %collective-permute-start.25 = (bf16[2,512,128]{2,1,0:T(8,128)(2,1)}, bf16[2,512,128]{2,1,0:T(8,128)(2,1)}, u32[]{:S(2)}, u32[]{:S(2)}) collective-permute-start(bf16[2,512,128]{2,1,0:T(8,128)(2,1)} %get-tuple-element.174), channel_id=1, source_target_pairs={{0,8},{1,24},{2,10},{3,26},{4,12},{5,28},{6,14},{7,30},{8,9},{9,25... | collective-permute-start | bytes 786440 | tf_op jit(solution)/shard_map/ppermute | solution.py:521
  204.8 14.1 %collective-permute-start.26 = (bf16[2,512,128]{2,1,0:T(8,128)(2,1)}, bf16[2,512,128]{2,1,0:T(8,128)(2,1)}, u32[]{:S(2)}, u32[]{:S(2)}) collective-permute-start(bf16[2,512,128]{2,1,0:T(8,128)(2,1)} %get-tuple-element.173), channel_id=1, source_target_pairs={{0,9},{1,25},{2,11},{3,27},{4,13},{5,29},{6,15},{7,31},{8,8},{9,24... | collective-permute-start | bytes 786440 | tf_op jit(solution)/shard_map/ppermute | solution.py:521
  231.6 25.9 %copy-start.51 = (f32[512,128]{1,0:T(8,128)}, f32[512,128]{1,0:T(8,128)S(1)}, u32[]{:S(2)}) copy-start(f32[512,128]{1,0:T(8,128)S(1)} %get-tuple-element.88.lse_ref) | copy-start | bytes 786436
  241.0 11.5 %copy-start.19 = (bf16[512,512]{1,0:T(8,128)(2,1)}, bf16[512,512]{1,0:T(8,128)(2,1)S(1)}, u32[]{:S(2)}) copy-start(bf16[512,512]{1,0:T(8,128)(2,1)S(1)} %get-tuple-element.78) | copy-start | bytes 1572868
  257.5 10.1 %copy-start.38 = (bf16[512,512]{1,0:T(8,128)(2,1)}, bf16[512,512]{1,0:T(8,128)(2,1)S(1)}, u32[]{:S(2)}) copy-start(bf16[512,512]{1,0:T(8,128)(2,1)S(1)} %get-tuple-element.87.dctx_ref) | copy-start | bytes 1572868
  257.5 10.1 %copy-start.42 = (f32[512,128]{1,0:T(8,128)}, f32[512,128]{1,0:T(8,128)S(1)}, u32[]{:S(2)}) copy-start(f32[512,128]{1,0:T(8,128)S(1)} %get-tuple-element.89.delta_ref) | copy-start | bytes 786436
  268.6 23.4 %collective-permute-start.31 = (bf16[4,512,256]{2,1,0:T(8,128)(2,1)}, bf16[4,512,256]{2,1,0:T(8,128)(2,1)}, u32[]{:S(2)}, u32[]{:S(2)}) collective-permute-start(bf16[4,512,256]{2,1,0:T(8,128)(2,1)} %get-tuple-element.93), channel_id=1, source_target_pairs={{0,1},{1,0},{2,3},{3,2},{4,5},{5,4},{6,7},{7,6},{8,9},{9,8},{10,11... | collective-permute-start | bytes 3145736 | tf_op jit(solution)/shard_map/ppermute | solution.py:507
  281.7 66.3 %collective-permute-start.40 = (bf16[4,400,512]{2,1,0:T(8,128)(2,1)}, bf16[4,400,512]{2,1,0:T(8,128)(2,1)}, u32[]{:S(2)}, u32[]{:S(2)}) collective-permute-start(bf16[4,400,512]{2,1,0:T(8,128)(2,1)} %pad_maximum_fusion.7), channel_id=1, source_target_pairs={{0,1},{1,0},{2,3},{3,2},{4,5},{5,4},{6,7},{7,6},{8,9},{9,8},{10,11... | collective-permute-start | bytes 4915208 | tf_op jit(solution)/shard_map/ppermute | solution.py:507
  297.5 11.6 %copy-start.12 = (f32[512,512]{1,0:T(8,128)S(1)}, f32[512,512]{1,0:T(8,128)}, u32[]{:S(2)}) copy-start(f32[512,512]{1,0:T(8,128)} %copy-done.11) | copy-start | bytes 3145732
  297.5 11.6 %copy-start.22 = (bf16[512,512]{1,0:T(8,128)(2,1)S(1)}, bf16[512,512]{1,0:T(8,128)(2,1)}, u32[]{:S(2)}) copy-start(bf16[512,512]{1,0:T(8,128)(2,1)} %copy-done.21) | copy-start | bytes 1572868
  313.4 10.4 %copy-start.74 = (bf16[384]{0:T(512)(128)(2,1)S(1)}, bf16[384]{0:T(512)(128)(2,1)}, u32[]{:S(2)}) copy-start(bf16[384]{0:T(512)(128)(2,1)} %pad.60.clone) | copy-start | bytes 2308
  323.4 19.7 %collective-permute-start.32 = (bf16[4,512,256]{2,1,0:T(8,128)(2,1)}, bf16[4,512,256]{2,1,0:T(8,128)(2,1)S(1)}, u32[]{:S(2)}, u32[]{:S(2)}) collective-permute-start(bf16[4,512,256]{2,1,0:T(8,128)(2,1)} %get-tuple-element.104), channel_id=1, source_target_pairs={{0,1},{1,0},{2,3},{3,2},{4,5},{5,4},{6,7},{7,6},{8,9},{9,8},{10,11... | collective-permute-start | bytes 3145736 | tf_op jit(solution)/shard_map/ppermute | solution.py:507
  328.5 22.7 %collective-permute-start.38 = (bf16[4,400,512]{2,1,0:T(8,128)(2,1)}, bf16[4,400,512]{2,1,0:T(8,128)(2,1)}, u32[]{:S(2)}, u32[]{:S(2)}) collective-permute-start(bf16[4,400,512]{2,1,0:T(8,128)(2,1)} %pad_maximum_fusion.5), channel_id=1, source_target_pairs={{0,1},{1,0},{2,3},{3,2},{4,5},{5,4},{6,7},{7,6},{8,9},{9,8},{10,11... | collective-permute-start | bytes 4915208 | tf_op jit(solution)/shard_map/ppermute | solution.py:507
  342.6 10.6 %collective-permute-start.39 = (bf16[4,400,512]{2,1,0:T(8,128)(2,1)}, bf16[4,400,512]{2,1,0:T(8,128)(2,1)S(1)}, u32[]{:S(2)}, u32[]{:S(2)}) collective-permute-start(bf16[4,400,512]{2,1,0:T(8,128)(2,1)} %pad_maximum_fusion.6), channel_id=1, source_target_pairs={{0,1},{1,0},{2,3},{3,2},{4,5},{5,4},{6,7},{7,6},{8,9},{9,8},{10,11... | collective-permute-start | bytes 4915208 | tf_op jit(solution)/shard_map/ppermute | solution.py:507
  347.9 5.8 %collective-permute-start.37 = (bf16[4,400,512]{2,1,0:T(8,128)(2,1)S(1)}, bf16[4,400,512]{2,1,0:T(8,128)(2,1)S(1)}, u32[]{:S(2)}, u32[]{:S(2)}) collective-permute-start(bf16[4,400,512]{2,1,0:T(8,128)(2,1)S(1)} %pad_maximum_fusion.4), channel_id=1, source_target_pairs={{0,1},{1,0},{2,3},{3,2},{4,5},{5,4},{6,7},{7,6},{8,9},{9,8},{10,11... | collective-permute-start | bytes 4915208 | tf_op jit(solution)/shard_map/ppermute | solution.py:507
  358.9 56.6 %collective-permute-start.41 = (bf16[2,4,192,512]{3,2,1,0:T(8,128)(2,1)}, bf16[2,4,192,512]{3,2,1,0:T(8,128)(2,1)}, u32[]{:S(2)}, u32[]{:S(2)}) collective-permute-start(bf16[2,4,192,512]{3,2,1,0:T(8,128)(2,1)} %pad_maximum_fusion.9), channel_id=1, source_target_pairs={{0,8},{8,0},{16,24},{24,16},{1,9},{9,1},{17,25},{25,17},{2,10},{10... | collective-permute-start | bytes 4718600 | tf_op jit(solution)/shard_map/ppermute | solution.py:513
  360.3 58.2 %collective-permute-start.43 = (bf16[2,4,208,512]{3,2,1,0:T(8,128)(2,1)}, bf16[2,4,208,512]{3,2,1,0:T(8,128)(2,1)}, u32[]{:S(2)}, u32[]{:S(2)}) collective-permute-start(bf16[2,4,208,512]{3,2,1,0:T(8,128)(2,1)} %pad_maximum_fusion.3), channel_id=1, source_target_pairs={{0,16},{8,24},{16,0},{24,8},{1,17},{9,25},{17,1},{25,9},{2,18},{10... | collective-permute-start | bytes 5111816 | tf_op jit(solution)/shard_map/ppermute | solution.py:513
  362.3 5.7 %collective-permute-start.27 = (bf16[2,512,128]{2,1,0:T(8,128)(2,1)S(1)}, bf16[2,512,128]{2,1,0:T(8,128)(2,1)S(1)}, u32[]{:S(2)}, u32[]{:S(2)}) collective-permute-start(bf16[2,512,128]{2,1,0:T(8,128)(2,1)S(1)} %get-tuple-element.158), channel_id=1, source_target_pairs={{0,0},{1,8},{2,2},{3,10},{4,4},{5,12},{6,6},{7,14},{8,16},{9,24},{... | collective-permute-start | bytes 786440 | tf_op jit(solution)/shard_map/ppermute | solution.py:521
  363.0 47.3 %collective-permute-start.28 = (bf16[2,512,128]{2,1,0:T(8,128)(2,1)S(1)}, bf16[2,512,128]{2,1,0:T(8,128)(2,1)}, u32[]{:S(2)}, u32[]{:S(2)}) collective-permute-start(bf16[2,512,128]{2,1,0:T(8,128)(2,1)S(1)} %get-tuple-element.161), channel_id=1, source_target_pairs={{0,8},{1,0},{2,10},{3,2},{4,12},{5,4},{6,14},{7,6},{8,24},{9,16},{... | collective-permute-start | bytes 786440 | tf_op jit(solution)/shard_map/ppermute | solution.py:521
  366.2 44.0 %collective-permute-start.29 = (bf16[2,512,128]{2,1,0:T(8,128)(2,1)S(1)}, bf16[2,512,128]{2,1,0:T(8,128)(2,1)}, u32[]{:S(2)}, u32[]{:S(2)}) collective-permute-start(bf16[2,512,128]{2,1,0:T(8,128)(2,1)S(1)} %get-tuple-element.160), channel_id=1, source_target_pairs={{0,16},{1,24},{2,18},{3,26},{4,20},{5,28},{6,22},{7,30},{8,0},{9,8... | collective-permute-start | bytes 786440 | tf_op jit(solution)/shard_map/ppermute | solution.py:521
  368.0 46.1 %collective-permute-start.30 = (bf16[2,512,128]{2,1,0:T(8,128)(2,1)S(1)}, bf16[2,512,128]{2,1,0:T(8,128)(2,1)}, u32[]{:S(2)}, u32[]{:S(2)}) collective-permute-start(bf16[2,512,128]{2,1,0:T(8,128)(2,1)S(1)} %get-tuple-element.159), channel_id=1, source_target_pairs={{0,24},{1,16},{2,26},{3,18},{4,28},{5,20},{6,30},{7,22},{8,8},{9,0... | collective-permute-start | bytes 786440 | tf_op jit(solution)/shard_map/ppermute | solution.py:521
  417.0 19.5 %collective-permute-start.42 = (bf16[4,192,512]{2,1,0:T(8,128)(2,1)S(1)}, bf16[4,192,512]{2,1,0:T(8,128)(2,1)S(1)}, u32[]{:S(2)}, u32[]{:S(2)}) collective-permute-start(bf16[4,192,512]{2,1,0:T(8,128)(2,1)S(1)} %fusion.7), channel_id=1, source_target_pairs={{0,16},{8,24},{16,0},{24,8},{1,17},{9,25},{17,1},{25,9},{2,18},{10... | collective-permute-start | bytes 2359304 | tf_op jit(solution)/shard_map/ppermute | solution.py:513
  419.8 23.0 %collective-permute-start.44 = (bf16[4,208,512]{2,1,0:T(8,128)(2,1)S(1)}, bf16[4,208,512]{2,1,0:T(8,128)(2,1)S(1)}, u32[]{:S(2)}, u32[]{:S(2)}) collective-permute-start(bf16[4,208,512]{2,1,0:T(8,128)(2,1)S(1)} %fusion.4), channel_id=1, source_target_pairs={{0,8},{8,0},{16,24},{24,16},{1,9},{9,1},{17,25},{25,17},{2,10},{10... | collective-permute-start | bytes 2555912 | tf_op jit(solution)/shard_map/ppermute | solution.py:513
  423.7 17.8 %copy-start.54 = (bf16[4,400,512]{2,1,0:T(8,128)(2,1)S(1)}, bf16[4,400,512]{2,1,0:T(8,128)(2,1)}, u32[]{:S(2)}) copy-start(bf16[4,400,512]{2,1,0:T(8,128)(2,1)} %get-tuple-element.136) | copy-start | bytes 4915204
  423.9 20.9 %collective-permute-start.33 = (bf16[1,512,128]{2,1,0:T(8,128)(2,1)S(1)}, bf16[1,512,128]{2,1,0:T(8,128)(2,1)S(1)}, u32[]{:S(2)}, u32[]{:S(2)}) collective-permute-start(bf16[1,512,128]{2,1,0:T(8,128)(2,1)S(1)} %get-tuple-element.180), channel_id=1, source_target_pairs={{0,0},{1,8},{2,2},{3,10},{4,4},{5,12},{6,6},{7,14},{8,16},{9,24},{... | collective-permute-start | bytes 393224 | tf_op jit(solution)/shard_map/ppermute | solution.py:521
  424.7 22.6 %collective-permute-start.34 = (bf16[1,512,128]{2,1,0:T(8,128)(2,1)S(1)}, bf16[1,512,128]{2,1,0:T(8,128)(2,1)S(1)}, u32[]{:S(2)}, u32[]{:S(2)}) collective-permute-start(bf16[1,512,128]{2,1,0:T(8,128)(2,1)S(1)} %get-tuple-element.183), channel_id=1, source_target_pairs={{0,8},{1,0},{2,10},{3,2},{4,12},{5,4},{6,14},{7,6},{8,24},{9,16},{... | collective-permute-start | bytes 393224 | tf_op jit(solution)/shard_map/ppermute | solution.py:521
  427.5 20.3 %collective-permute-start.35 = (bf16[1,512,128]{2,1,0:T(8,128)(2,1)S(1)}, bf16[1,512,128]{2,1,0:T(8,128)(2,1)S(1)}, u32[]{:S(2)}, u32[]{:S(2)}) collective-permute-start(bf16[1,512,128]{2,1,0:T(8,128)(2,1)S(1)} %get-tuple-element.182), channel_id=1, source_target_pairs={{0,16},{1,24},{2,18},{3,26},{4,20},{5,28},{6,22},{7,30},{8,0},{9,8... | collective-permute-start | bytes 393224 | tf_op jit(solution)/shard_map/ppermute | solution.py:521
  436.5 11.3 %collective-permute-start.36 = (bf16[1,512,128]{2,1,0:T(8,128)(2,1)S(1)}, bf16[1,512,128]{2,1,0:T(8,128)(2,1)S(1)}, u32[]{:S(2)}, u32[]{:S(2)}) collective-permute-start(bf16[1,512,128]{2,1,0:T(8,128)(2,1)S(1)} %get-tuple-element.181), channel_id=1, source_target_pairs={{0,24},{1,16},{2,26},{3,18},{4,28},{5,20},{6,30},{7,22},{8,8},{9,0... | collective-permute-start | bytes 393224 | tf_op jit(solution)/shard_map/ppermute | solution.py:521
  444.2 16.4 %collective-permute-start.45 = (bf16[400,512]{1,0:T(8,128)(2,1)S(1)}, bf16[400,512]{1,0:T(8,128)(2,1)S(1)}, u32[]{:S(2)}, u32[]{:S(2)}) collective-permute-start(bf16[400,512]{1,0:T(8,128)(2,1)S(1)} %get-tuple-element.149), channel_id=1, source_target_pairs={{0,2},{1,3},{2,0},{3,1},{4,6},{5,7},{6,4},{7,5},{8,10},{9,11},{10,... | collective-permute-start | bytes 1228808 | tf_op jit(solution)/shard_map/ppermute | solution.py:507
  444.7 30.1 %collective-permute-start.46 = (bf16[400,512]{1,0:T(8,128)(2,1)S(1)}, bf16[400,512]{1,0:T(8,128)(2,1)S(1)}, u32[]{:S(2)}, u32[]{:S(2)}) collective-permute-start(bf16[400,512]{1,0:T(8,128)(2,1)S(1)} %get-tuple-element.150), channel_id=1, source_target_pairs={{0,4},{1,5},{2,6},{3,7},{4,0},{5,1},{6,2},{7,3},{8,12},{9,13},{10,... | collective-permute-start | bytes 1228808 | tf_op jit(solution)/shard_map/ppermute | solution.py:507
  447.3 35.2 %collective-permute-start.47 = (bf16[400,512]{1,0:T(8,128)(2,1)S(1)}, bf16[400,512]{1,0:T(8,128)(2,1)S(1)}, u32[]{:S(2)}, u32[]{:S(2)}) collective-permute-start(bf16[400,512]{1,0:T(8,128)(2,1)S(1)} %get-tuple-element.151), channel_id=1, source_target_pairs={{0,6},{1,7},{2,4},{3,5},{4,2},{5,3},{6,0},{7,1},{8,14},{9,15},{10,... | collective-permute-start | bytes 1228808 | tf_op jit(solution)/shard_map/ppermute | solution.py:507
  (63 other events, 207.8 us)
